TPU v7x, 32 devices: a whole 2x2x4 slice. The times are simulated.
32 devices in a mesh: dp: 8 (over z, x), expert: 4 (over y, core).
Axes of the slice: x: 2, y: 2, z: 4, core: 2. Of those that a mesh axis runs over, the one named last changes fastest.
Arguments:
- tokens: bfloat16 [32, 256, 768], P(('dp', 'expert')), may hold values from -6 to 6
- conditioning: bfloat16 [32, 768], P(('dp', 'expert')), may hold values from -6 to 6
- routes: int32 [32, 256, 2], P(('dp', 'expert')), may hold values from 0 to 7, all different within a row
- cotangent: bfloat16 [32, 256, 768], P(('dp', 'expert')), may hold values from -6 to 6
- ada_weight: bfloat16 [768, 4608], P('dp'), may hold values from -0.21875 to 0.21875
- ada_bias: bfloat16 [4608], P('dp'), may hold values from -2.5 to 2.5
- qkv_weight: bfloat16 [768, 2304], P('dp'), may hold values from -0.21875 to 0.21875
- qv_bias: bfloat16 [2, 768], P(None, 'dp'), may hold values from -2.5 to 2.5
- out_weight: bfloat16 [768, 768], P('dp'), may hold values from -1.75 to 1.75
- out_bias: bfloat16 [768], P('dp'), may hold values from -2.5 to 2.5
- shared_in: bfloat16 [768, 3072], P('dp'), may hold values from -0.21875 to 0.21875
- shared_in_bias: bfloat16 [3072], P('dp'), may hold values from -2.5 to 2.5
- shared_out: bfloat16 [3072, 768], P('dp'), may hold values from -0.109375 to 0.109375
- shared_out_bias: bfloat16 [768], P('dp'), may hold values from -2.5 to 2.5
- router: bfloat16 [768, 8], P('dp'), may hold values from -0.15625 to 0.15625
- expert_in: bfloat16 [8, 768, 3072], P('expert'), may hold values from -0.21875 to 0.21875
- expert_in_bias: bfloat16 [8, 3072], P('expert'), may hold values from -2.5 to 2.5
- expert_out: bfloat16 [8, 3072, 768], P('expert'), may hold values from -0.109375 to 0.109375
- expert_out_bias: bfloat16 [8, 768], P('expert'), may hold values from -2.5 to 2.5
Outputs:
- output: bfloat16 [32, 256, 768], P(('dp', 'expert'))
- tokens_grad: float32 [32, 256, 768], P(('dp', 'expert'))
- conditioning_grad: float32 [32, 768], P(('dp', 'expert'))
- ada_weight_grad: float32 [768, 4608], P('dp')
- ada_bias_grad: float32 [4608], P('dp')
- qkv_weight_grad: float32 [768, 2304], P('dp')
- qv_bias_grad: float32 [2, 768], P(None, 'dp')
- out_weight_grad: float32 [768, 768], P('dp')
- out_bias_grad: float32 [768], P('dp')
- shared_in_grad: float32 [768, 3072], P('dp')
- shared_in_bias_grad: float32 [3072], P('dp')
- shared_out_grad: float32 [3072, 768], P('dp')
- shared_out_bias_grad: float32 [768], P('dp')
- router_grad: float32 [768, 8], P('dp')
- expert_in_grad: float32 [8, 768, 3072], P('expert', 'dp')
- expert_in_bias_grad: float32 [8, 3072], P('expert', 'dp')
- expert_out_grad: float32 [8, 3072, 768], P('expert', 'dp')
- expert_out_bias_grad: float32 [8, 768], P('expert', 'dp')
Inputs may be any that keep to these rules, and one draw needn't show every extreme that they name: `routes`: each patch names two different experts.
All inputs are finite; a program needn't handle non-finite values.
Results may differ from a plain program's by a relative error of at most 0.018.
The roundings to bfloat16 on the way count: a program that leaves them out, or rounds other values in their place, can miss the bound.
Values may be sent and summed in bfloat16 or wider, within the bound.
A program may use at most 256 MiB of HBM per device.

v0:
```python
import jax
import jax.numpy as jnp
from jax import lax
from jax.sharding import PartitionSpec as P

HEADS = 12
HEAD_DIM = 64
E = 8
CAP = 80


def layer_norm(rows):
    centred = rows - jnp.mean(rows, axis=-1, keepdims=True)
    return centred * lax.rsqrt(jnp.mean(centred * centred, axis=-1, keepdims=True) + 1e-06)


def modulate(rows, shift, scale):
    return layer_norm(rows) * (1.0 + scale) + shift


def gelu_tanh(values_in):
    return jax.nn.gelu(values_in, approximate=True)


def on_device(
    tokens,
    conditioning,
    routes,
    cotangent,
    ada_weight,
    ada_bias,
    qkv_weight,
    qv_bias,
    out_weight,
    out_bias,
    shared_in,
    shared_in_bias,
    shared_out,
    shared_out_bias,
    router,
    expert_in,
    expert_in_bias,
    expert_out,
    expert_out_bias,
):
    f32 = jnp.float32
    b16 = jnp.bfloat16
    gathered_dense = (
        lax.all_gather(ada_weight, "dp", axis=0, tiled=True),
        lax.all_gather(ada_bias, "dp", axis=0, tiled=True),
        lax.all_gather(qkv_weight, "dp", axis=0, tiled=True),
        lax.all_gather(qv_bias, "dp", axis=1, tiled=True),
        lax.all_gather(out_weight, "dp", axis=0, tiled=True),
        lax.all_gather(out_bias, "dp", axis=0, tiled=True),
        lax.all_gather(shared_in, "dp", axis=0, tiled=True),
        lax.all_gather(shared_in_bias, "dp", axis=0, tiled=True),
        lax.all_gather(shared_out, "dp", axis=0, tiled=True),
        lax.all_gather(shared_out_bias, "dp", axis=0, tiled=True),
        lax.all_gather(router, "dp", axis=0, tiled=True),
    )
    (
        ada_full,
        ada_bias_full,
        qkv_full,
        qv_bias_full,
        out_full,
        out_bias_full,
        shared_in_full,
        shared_in_bias_full,
        shared_out_full,
        shared_out_bias_full,
        router_full,
    ) = gathered_dense
    image_count, length, width = tokens.shape
    row_count = image_count * length
    scaling = HEAD_DIM ** (-0.5)
    head_shape = (image_count, length, HEADS, HEAD_DIM)
    cond_float = conditioning.astype(f32)
    cond_act, silu_back = jax.vjp(jax.nn.silu, cond_float)
    cond_low = cond_act.astype(b16)
    modulation = jnp.dot(cond_low, ada_full, preferred_element_type=f32) + ada_bias_full.astype(f32)
    pieces = [modulation[:, None, index * width : (index + 1) * width] for index in range(6)]
    source = tokens.astype(f32)
    first_norm, first_back = jax.vjp(modulate, source, pieces[0], pieces[1])
    normed = first_norm.astype(b16)
    projected = jnp.einsum("isd,de->ise", normed, qkv_full, preferred_element_type=f32)
    query_heads = (
        (projected[..., :width] + qv_bias_full[0].astype(f32)).astype(b16).reshape(head_shape)
    )
    key_heads = projected[..., width : 2 * width].astype(b16).reshape(head_shape)
    value_heads = (
        (projected[..., 2 * width :] + qv_bias_full[1].astype(f32)).astype(b16).reshape(head_shape)
    )
    scores = (
        jnp.einsum("iqhc,ikhc->ihqk", query_heads, key_heads, preferred_element_type=f32) * scaling
    )
    peak_score = jnp.max(scores, axis=-1, keepdims=True)
    unscaled = jnp.exp(scores - peak_score)
    exp_total = jnp.sum(unscaled, axis=-1, keepdims=True)
    log_total = peak_score + jnp.log(exp_total)
    probs_low = (unscaled / exp_total).astype(b16)
    mixed = (
        jnp.einsum("ihqk,ikhc->iqhc", probs_low, value_heads, preferred_element_type=f32)
        .reshape(image_count, length, width)
        .astype(b16)
    )
    attended = jnp.einsum(
        "isd,de->ise", mixed, out_full, preferred_element_type=f32
    ) + out_bias_full.astype(f32)
    resid = source + pieces[2] * attended
    second_float, second_back = jax.vjp(modulate, resid, pieces[3], pieces[4])
    second = second_float.astype(b16)
    shared_pre = jnp.einsum(
        "isd,df->isf", second, shared_in_full, preferred_element_type=f32
    ) + shared_in_bias_full.astype(f32)
    shared_act, shared_gelu_back = jax.vjp(gelu_tanh, shared_pre)
    shared_low = shared_act.astype(b16)
    shared = jnp.einsum(
        "isf,fd->isd", shared_low, shared_out_full, preferred_element_type=f32
    ) + shared_out_bias_full.astype(f32)
    second_rows = second.reshape(row_count, width)
    logits = jnp.dot(second_rows, router_full, preferred_element_type=f32)
    route_flat = routes.reshape(-1)
    one_hot = (route_flat[:, None] == jnp.arange(E, dtype=jnp.int32)).astype(jnp.int32)
    slot_index = jnp.sum(
        (jnp.cumsum(one_hot, axis=0, dtype=jnp.int32) - one_hot) * one_hot, axis=1, dtype=jnp.int32
    )
    position = jnp.where(slot_index < CAP, route_flat * CAP + slot_index, E * CAP)
    pair_rows = jnp.repeat(second_rows, 2, axis=0)
    buffer = (
        jnp.zeros((E * CAP, width), b16)
        .at[position]
        .set(pair_rows, mode="drop")
        .reshape(E, CAP, width)
    )
    received = lax.all_to_all(buffer, "expert", split_axis=0, concat_axis=1, tiled=True)
    expert_pre = (
        jnp.einsum("erd,edf->erf", received, expert_in, preferred_element_type=f32)
        + expert_in_bias.astype(f32)[:, None, :]
    )
    expert_low = gelu_tanh(expert_pre).astype(b16)
    expert_result = (
        jnp.einsum("erf,efd->erd", expert_low, expert_out, preferred_element_type=f32)
        + expert_out_bias.astype(f32)[:, None, :]
    ).astype(b16)
    returned = lax.all_to_all(
        expert_result, "expert", split_axis=1, concat_axis=0, tiled=True
    ).reshape(E * CAP, width)
    gathered = (
        returned.at[position]
        .get(mode="fill", fill_value=0)
        .reshape(row_count, 2, width)
        .astype(f32)
    )
    pair_mask = one_hot.reshape(row_count, 2, E).astype(f32)
    chosen = jnp.sum(logits[:, None, :] * pair_mask, axis=-1)
    gates = jax.nn.softmax(chosen, axis=-1)
    moe = (shared.reshape(row_count, width) + jnp.sum(gates[..., None] * gathered, axis=1)).reshape(
        image_count, length, width
    )
    output = (resid + pieces[5] * moe).astype(b16)
    ada_back, qkv_back, out_back, shared_in_back, shared_out_back, router_back = (
        ada_full,
        qkv_full,
        out_full,
        shared_in_full,
        shared_out_full,
        router_full,
    )
    grad_out = cotangent.astype(f32)
    gate_two_grad = jnp.sum(grad_out * moe, axis=1, keepdims=True)
    moe_grad = (pieces[5] * grad_out).astype(b16)
    moe_rows_grad = moe_grad.reshape(row_count, width)
    moe_rows_float = moe_rows_grad.astype(f32)
    pair_grad = (
        (gates[..., None] * moe_rows_float[:, None, :]).astype(b16).reshape(2 * row_count, width)
    )
    gate_grad = jnp.sum(moe_rows_float[:, None, :] * gathered, axis=-1)
    chosen_grad = gates * (gate_grad - jnp.sum(gates * gate_grad, axis=-1, keepdims=True))
    logits_grad = jnp.sum(chosen_grad[..., None] * pair_mask, axis=1).astype(b16)
    grad_buffer = (
        jnp.zeros((E * CAP, width), b16)
        .at[position]
        .set(pair_grad, mode="drop")
        .reshape(E, CAP, width)
    )
    result_grad = lax.all_to_all(grad_buffer, "expert", split_axis=0, concat_axis=1, tiled=True)
    pre_again = (
        jnp.einsum("erd,edf->erf", received, expert_in, preferred_element_type=f32)
        + expert_in_bias.astype(f32)[:, None, :]
    )
    act_again, expert_gelu_back = jax.vjp(gelu_tanh, pre_again)
    low_again = act_again.astype(b16)
    expert_out_grad = jnp.einsum("erf,erd->efd", low_again, result_grad, preferred_element_type=f32)
    expert_out_bias_grad = jnp.sum(result_grad.astype(f32), axis=1)
    expert_act_grad = jnp.einsum(
        "erd,efd->erf", result_grad, expert_out, preferred_element_type=f32
    )
    pre_grad = expert_gelu_back(expert_act_grad)[0].astype(b16)
    expert_in_grad = jnp.einsum("erd,erf->edf", received, pre_grad, preferred_element_type=f32)
    expert_in_bias_grad = jnp.sum(pre_grad.astype(f32), axis=1)
    received_grad = jnp.einsum(
        "erf,edf->erd", pre_grad, expert_in, preferred_element_type=f32
    ).astype(b16)
    sent_grad = lax.all_to_all(
        received_grad, "expert", split_axis=1, concat_axis=0, tiled=True
    ).reshape(E * CAP, width)
    dispatch_rows_grad = jnp.sum(
        sent_grad.at[position]
        .get(mode="fill", fill_value=0)
        .reshape(row_count, 2, width)
        .astype(f32),
        axis=1,
    )
    shared_out_grad = jnp.einsum("isf,isd->fd", shared_low, moe_grad, preferred_element_type=f32)
    shared_out_bias_grad = jnp.sum(moe_rows_float, axis=0)
    shared_act_grad = jnp.einsum(
        "isd,fd->isf", moe_grad, shared_out_back, preferred_element_type=f32
    )
    shared_pre_grad = shared_gelu_back(shared_act_grad)[0].astype(b16)
    shared_in_grad = jnp.einsum("isd,isf->df", second, shared_pre_grad, preferred_element_type=f32)
    shared_in_bias_grad = jnp.sum(shared_pre_grad.astype(f32), axis=(0, 1))
    router_grad = jnp.einsum("rd,re->de", second_rows, logits_grad, preferred_element_type=f32)
    second_grad = jnp.einsum(
        "isf,df->isd", shared_pre_grad, shared_in_back, preferred_element_type=f32
    )
    side_grad = dispatch_rows_grad + jnp.einsum(
        "re,de->rd", logits_grad, router_back, preferred_element_type=f32
    )
    second_grad = second_grad + side_grad.reshape(image_count, length, width)
    resid_extra, shift_two_grad, scale_two_grad = second_back(second_grad)
    resid_grad = grad_out + resid_extra
    attended_grad = (pieces[2] * resid_grad).astype(b16)
    gate_one_grad = jnp.sum(resid_grad * attended, axis=1, keepdims=True)
    out_weight_grad = jnp.einsum("isd,ise->de", mixed, attended_grad, preferred_element_type=f32)
    out_bias_grad = jnp.sum(attended_grad.astype(f32), axis=(0, 1))
    mixed_grad = (
        jnp.einsum("ise,de->isd", attended_grad, out_back, preferred_element_type=f32)
        .astype(b16)
        .reshape(head_shape)
    )
    again_scores = (
        jnp.einsum("iqhc,ikhc->ihqk", query_heads, key_heads, preferred_element_type=f32) * scaling
    )
    probs_float = jnp.exp(again_scores - log_total)
    again_low = probs_float.astype(b16)
    probs_grad = jnp.einsum("iqhc,ikhc->ihqk", mixed_grad, value_heads, preferred_element_type=f32)
    values_grad = jnp.einsum(
        "ihqk,iqhc->ikhc", again_low, mixed_grad, preferred_element_type=f32
    ).astype(b16)
    scores_grad = (
        probs_float * (probs_grad - jnp.sum(probs_float * probs_grad, axis=-1, keepdims=True))
    ).astype(b16)
    query_grad = (
        jnp.einsum("ihqk,ikhc->iqhc", scores_grad, key_heads, preferred_element_type=f32) * scaling
    ).astype(b16)
    keys_grad = (
        jnp.einsum("ihqk,iqhc->ikhc", scores_grad, query_heads, preferred_element_type=f32)
        * scaling
    ).astype(b16)
    flat_shape = (image_count, length, width)
    projected_grad = jnp.concatenate(
        [
            query_grad.reshape(flat_shape),
            keys_grad.reshape(flat_shape),
            values_grad.reshape(flat_shape),
        ],
        axis=-1,
    )
    qkv_weight_grad = jnp.einsum("isd,ise->de", normed, projected_grad, preferred_element_type=f32)
    qv_bias_grad = jnp.stack(
        [
            jnp.sum(query_grad.astype(f32), axis=(0, 1)).reshape(width),
            jnp.sum(values_grad.astype(f32), axis=(0, 1)).reshape(width),
        ]
    )
    normed_grad = jnp.einsum("ise,de->isd", projected_grad, qkv_back, preferred_element_type=f32)
    token_extra, shift_one_grad, scale_one_grad = first_back(normed_grad)
    tokens_grad = resid_grad + token_extra
    modulation_grad = jnp.concatenate(
        [
            shift_one_grad,
            scale_one_grad,
            gate_one_grad,
            shift_two_grad,
            scale_two_grad,
            gate_two_grad,
        ],
        axis=-1,
    )[:, 0, :].astype(b16)
    ada_weight_grad = jnp.einsum("id,ie->de", cond_low, modulation_grad, preferred_element_type=f32)
    ada_bias_grad = jnp.sum(modulation_grad.astype(f32), axis=0)
    cond_act_grad = jnp.einsum("ie,de->id", modulation_grad, ada_back, preferred_element_type=f32)
    conditioning_grad = silu_back(cond_act_grad)[0]
    expert_sums = (
        lax.psum_scatter(
            expert_in_grad.astype(jnp.bfloat16), "dp", scatter_dimension=1, tiled=True
        ).astype(jnp.float32),
        lax.psum_scatter(
            expert_in_bias_grad.astype(jnp.bfloat16), "dp", scatter_dimension=1, tiled=True
        ).astype(jnp.float32),
        lax.psum_scatter(
            expert_out_grad.astype(jnp.bfloat16), "dp", scatter_dimension=1, tiled=True
        ).astype(jnp.float32),
        lax.psum_scatter(
            expert_out_bias_grad.astype(jnp.bfloat16), "dp", scatter_dimension=1, tiled=True
        ).astype(jnp.float32),
    )
    dense_parts = (
        lax.psum_scatter(
            ada_weight_grad.astype(jnp.bfloat16), "dp", scatter_dimension=0, tiled=True
        ).astype(jnp.float32),
        lax.psum_scatter(
            ada_bias_grad.astype(jnp.bfloat16), "dp", scatter_dimension=0, tiled=True
        ).astype(jnp.float32),
        lax.psum_scatter(
            qkv_weight_grad.astype(jnp.bfloat16), "dp", scatter_dimension=0, tiled=True
        ).astype(jnp.float32),
        lax.psum_scatter(
            qv_bias_grad.astype(jnp.bfloat16), "dp", scatter_dimension=1, tiled=True
        ).astype(jnp.float32),
        lax.psum_scatter(
            out_weight_grad.astype(jnp.bfloat16), "dp", scatter_dimension=0, tiled=True
        ).astype(jnp.float32),
        lax.psum_scatter(
            out_bias_grad.astype(jnp.bfloat16), "dp", scatter_dimension=0, tiled=True
        ).astype(jnp.float32),
        lax.psum_scatter(
            shared_in_grad.astype(jnp.bfloat16), "dp", scatter_dimension=0, tiled=True
        ).astype(jnp.float32),
        lax.psum_scatter(
            shared_in_bias_grad.astype(jnp.bfloat16), "dp", scatter_dimension=0, tiled=True
        ).astype(jnp.float32),
        lax.psum_scatter(
            shared_out_grad.astype(jnp.bfloat16), "dp", scatter_dimension=0, tiled=True
        ).astype(jnp.float32),
        lax.psum_scatter(
            shared_out_bias_grad.astype(jnp.bfloat16), "dp", scatter_dimension=0, tiled=True
        ).astype(jnp.float32),
        lax.psum_scatter(
            router_grad.astype(jnp.bfloat16), "dp", scatter_dimension=0, tiled=True
        ).astype(jnp.float32),
    )
    dense_sums = lax.psum(
        (
            dense_parts[0],
            dense_parts[1],
            dense_parts[2],
            dense_parts[3],
            dense_parts[4],
            dense_parts[5],
            dense_parts[6],
            dense_parts[7],
            dense_parts[8],
            dense_parts[9],
            dense_parts[10],
        ),
        "expert",
    )
    return (
        output,
        tokens_grad,
        conditioning_grad,
        dense_sums[0],
        dense_sums[1],
        dense_sums[2],
        dense_sums[3],
        dense_sums[4],
        dense_sums[5],
        dense_sums[6],
        dense_sums[7],
        dense_sums[8],
        dense_sums[9],
        dense_sums[10],
        expert_sums[0],
        expert_sums[1],
        expert_sums[2],
        expert_sums[3],
    )


def solution(mesh):
    in_specs = (
        P(("dp", "expert"), None, None),
        P(("dp", "expert"), None),
        P(("dp", "expert"), None, None),
        P(("dp", "expert"), None, None),
        P("dp", None),
        P("dp"),
        P("dp", None),
        P(None, "dp"),
        P("dp", None),
        P("dp"),
        P("dp", None),
        P("dp"),
        P("dp", None),
        P("dp"),
        P("dp", None),
        P("expert", None, None),
        P("expert", None),
        P("expert", None, None),
        P("expert", None),
    )
    out_specs = (
        P(("dp", "expert"), None, None),
        P(("dp", "expert"), None, None),
        P(("dp", "expert"), None),
        P("dp", None),
        P("dp"),
        P("dp", None),
        P(None, "dp"),
        P("dp", None),
        P("dp"),
        P("dp", None),
        P("dp"),
        P("dp", None),
        P("dp"),
        P("dp", None),
        P("expert", "dp", None),
        P("expert", "dp"),
        P("expert", "dp", None),
        P("expert", "dp"),
    )
    return jax.shard_map(
        on_device, mesh=mesh, in_specs=in_specs, out_specs=out_specs, check_vma=False
    )
```

profile of v0, /device:TPU:0, one launch (start us, length us, event | category | flops | bytes accessed | tf_op | source)
XLA Modules:
  0.0 1505.7 jit_solution(14408032452444399799)
XLA Ops:
  12.9 22.5 %all-gather = bf16[8,96,2]{1,2,0:T(2,128)(2,1)S(1)} all-gather(bf16[1,96,2]{1,2,0:T(2,128)(2,1)S(1)} %bitcast.227), channel_id=1, replica_groups=mesh['dp'=8,'expert'=4] {'dp'}, dimensions={0}, use_global_device_ids=true | all-gather | bytes 3456 | tf_op jit(solution)/shard_map/all_gather | solution.py:52
  39.6 34.5 %all-reduce.9 = (bf16[4608]{0:T(1024)(128)(2,1)S(1)}, bf16[768]{0:T(1024)(128)(2,1)S(1)}, bf16[768]{0:T(1024)(128)(2,1)}) all-reduce(bf16[4608]{0:T(1024)(128)(2,1)S(1)} %dynamic-update-slice, bf16[768]{0:T(1024)(128)(2,1)S(1)} %dynamic-update-slice.1, bf16[768]{0:T(1024)(128)(2,1)S(1)} %dynamic-update-slice.2), channel_id=1, replica_groups=mesh['dp'=8,'expert'=4] {'dp'}, use_global_device_ids=true, to_apply=%add | all-reduce | flops 6144 | bytes 24576
  75.6 46.7 %all-gather.9.cloned.1.call-done = bf16[768,4608]{1,0:T(8,128)(2,1)} async-done(((bf16[96,4608]{1,0:T(8,128)(2,1)}), bf16[768,4608]{1,0:T(8,128)(2,1)}) %all-gather.9.cloned.1.call-update) | async-done | bytes 7077904 | tf_op jit(solution)/shard_map/all_gather | solution.py:49
  122.3 4.0 convolution_reduce_fusion
  127.1 60.9 %all-gather.11.cloned.1.call-done = bf16[768,2304]{1,0:T(8,128)(2,1)} async-done(((bf16[96,2304]{1,0:T(8,128)(2,1)}), bf16[768,2304]{1,0:T(8,128)(2,1)}) %all-gather.11.cloned.1.call-update) | async-done | bytes 3538960 | tf_op jit(solution)/shard_map/all_gather | solution.py:51
  188.0 3.2 convolution_bitcast_fusion
  198.6 31.1 %all-gather.13.cloned.1.call-done = bf16[768,768]{1,0:T(8,128)(2,1)} async-done(((bf16[96,768]{1,0:T(8,128)(2,1)}), bf16[768,768]{1,0:T(8,128)(2,1)}) %all-gather.13.cloned.1.call-update) | async-done | bytes 1179664 | tf_op jit(solution)/shard_map/all_gather | solution.py:53
  237.8 4.5 scatter_custom_fusion
  242.3 4.3 all-to-all-start
  248.0 26.3 %all-gather.1 = bf16[8,1,384]{2,1,0:T(2,128)(2,1)S(1)} all-gather(bf16[1,1,384]{2,1,0:T(2,128)(2,1)S(1)} %reshape.765), channel_id=1, replica_groups=mesh['dp'=8,'expert'=4] {'dp'}, dimensions={0}, use_global_device_ids=true | all-gather | bytes 6912 | tf_op jit(solution)/shard_map/all_gather | solution.py:56
  282.1 26.4 %all-gather.2 = bf16[8,96,8]{1,2,0:T(8,128)(2,1)S(1)} all-gather(bf16[1,96,8]{1,2,0:T(8,128)(2,1)} %bitcast.226), channel_id=1, replica_groups=mesh['dp'=8,'expert'=4] {'dp'}, dimensions={0}, use_global_device_ids=true | all-gather | bytes 13824 | tf_op jit(solution)/shard_map/all_gather | solution.py:59
  314.4 6.2 fusion.103
  320.6 10.6 add_convert_fusion
  333.2 4.5 all-to-all-start.1
  341.4 3.1 mul.461
  345.9 6.0 convolution_add_fusion
  354.1 4.4 gather_fusion
  365.4 4.6 scatter_custom_fusion.1
  370.0 4.6 all-to-all-start.2
  374.6 16.3 %all-gather.17.cloned.1.call-done = bf16[3072,768]{1,0:T(8,128)(2,1)} async-done(((bf16[384,768]{1,0:T(8,128)(2,1)}), bf16[3072,768]{1,0:T(8,128)(2,1)}) %all-gather.17.cloned.1.call-update) | async-done | bytes 4718608 | tf_op jit(solution)/shard_map/all_gather | solution.py:57
  390.9 8.0 fusion.101
  400.2 12.2 fusion.94
  412.4 8.7 convolution_convert_fusion.6
  423.1 4.2 all-to-all-start.3
  428.5 5.1 fusion.104
  443.9 4.6 gather_fusion.1
  451.4 6.8 convert_reduce_fusion
  476.8 3.5 convolution_convert_fusion.3
  481.3 6.3 convolution_convert_fusion.2
  490.4 3.8 convolution_convert_fusion.4
  495.6 4.1 fusion.39
  504.6 6.9 fusion.41
  512.4 4.3 multiply_convert_fusion
  517.9 9.6 convolution_convert_fusion.1
  528.7 10.5 convolution_convert_fusion
  542.0 12.3 reduce-scatter.40.cloned.1.call-done
  555.7 63.5 %reduce-scatter.38.cloned.1.call-done = bf16[384,2]{1,0:T(8,128)(2,1)} async-done(((bf16[3072,2]{1,0:T(8,128)(2,1)}), bf16[384,2]{1,0:T(8,128)(2,1)}) %reduce-scatter.38.cloned.1.call-update) | async-done | bytes 1552
  620.9 35.1 %all-reduce.8 = (bf16[4608]{0:T(1024)(128)(2,1)S(1)}, bf16[768]{0:T(1024)(128)(2,1)S(1)}, bf16[3072]{0:T(1024)(128)(2,1)S(1)}, bf16[768]{0:T(1024)(128)(2,1)S(1)}) all-reduce(bf16[4608]{0:T(1024)(128)(2,1)S(1)} %reduce.46, bf16[768]{0:T(1024)(128)(2,1)S(1)} %copy-done.68, ...), channel_id=3, replica_groups=mesh['dp'=8,'expert'=4] {'dp'}, use_global_device_ids=true, to_apply=%region_32.33.clone | all-reduce | flops 9216 | bytes 36864
  656.2 5.6 fusion.72
  661.8 21.7 %reduce-scatter.34.cloned.1.call-done = bf16[96,2]{1,0:T(8,128)(2,1)} async-done(((bf16[768,2]{1,0:T(8,128)(2,1)}), bf16[96,2]{1,0:T(8,128)(2,1)}) %reduce-scatter.34.cloned.1.call-update) | async-done | bytes 400
  684.2 66.5 %reduce-scatter.24.cloned.1.call-done = bf16[96,768]{1,0:T(8,128)(2,1)} async-done(((bf16[768,768]{1,0:T(8,128)(2,1)}), bf16[96,768]{1,0:T(8,128)(2,1)}) %reduce-scatter.24.cloned.1.call-update) | async-done | bytes 147472 | tf_op jit(solution)/shard_map/reduce_scatter | solution.py:322
  750.8 98.5 %reduce-scatter.26.cloned.1.call-done = bf16[96,3072]{1,0:T(8,128)(2,1)} async-done(((bf16[768,3072]{1,0:T(8,128)(2,1)}), bf16[96,3072]{1,0:T(8,128)(2,1)}) %reduce-scatter.26.cloned.1.call-update) | async-done | bytes 589840 | tf_op jit(solution)/shard_map/reduce_scatter | solution.py:328
  849.3 99.0 %reduce-scatter.28.cloned.1.call-done = bf16[384,768]{1,0:T(8,128)(2,1)} async-done(((bf16[3072,768]{1,0:T(8,128)(2,1)}), bf16[384,768]{1,0:T(8,128)(2,1)}) %reduce-scatter.28.cloned.1.call-update) | async-done | bytes 589840 | tf_op jit(solution)/shard_map/reduce_scatter | solution.py:334
  948.3 83.0 %reduce-scatter.22.cloned.1.call-done = bf16[96,2304]{1,0:T(8,128)(2,1)} async-done(((bf16[768,2304]{1,0:T(8,128)(2,1)}), bf16[96,2304]{1,0:T(8,128)(2,1)}) %reduce-scatter.22.cloned.1.call-update) | async-done | bytes 442384 | tf_op jit(solution)/shard_map/reduce_scatter | solution.py:316
  1031.3 132.6 %reduce-scatter.20.cloned.1.call-done = bf16[96,4608]{1,0:T(8,128)(2,1)} async-done(((bf16[768,4608]{1,0:T(8,128)(2,1)}), bf16[96,4608]{1,0:T(8,128)(2,1)}) %reduce-scatter.20.cloned.1.call-update) | async-done | bytes 884752 | tf_op jit(solution)/shard_map/reduce_scatter | solution.py:310
  1163.9 95.3 %all-reduce.11 = (f32[96,4608]{1,0:T(8,128)}, f32[576]{0:T(1024)}, f32[96,2304]{1,0:T(8,128)}, f32[2,96]{1,0:T(2,128)}, f32[96,768]{1,0:T(8,128)}, /*index=5*/f3...) all-reduce(bf16[96,4608]{1,0:T(8,128)(2,1)} %reduce-scatter.20.clon, ...), channel_id=1, replica_groups=mesh['dp'=8,'expert'=4] {'expert'}, use_global_device_ids=true, to_apply=%region_31.32 | all-reduce | flops 1329216 | bytes 7977600 | tf_op jit(solution)/shard_map/psum | solution.py:344
  1259.1 70.7 %reduce-scatter.30.cloned.1.call-done = bf16[2,96,3072]{2,1,0:T(8,128)(2,1)} async-done(((bf16[2,768,3072]{2,1,0:T(8,128)(2,1)}), bf16[2,96,3072]{2,1,0:T(8,128)(2,1)}) %reduce-scatter.30.cloned.1.call-update) | async-done | bytes 1179664 | tf_op jit(solution)/shard_map/reduce_scatter | solution.py:296
  1332.8 163.1 %reduce-scatter.32.cloned.1.call-done = bf16[2,384,768]{2,1,0:T(8,128)(2,1)} async-done(((bf16[2,3072,768]{2,1,0:T(8,128)(2,1)}), bf16[2,384,768]{2,1,0:T(8,128)(2,1)}) %reduce-scatter.32.cloned.1.call-update) | async-done | bytes 1179664 | tf_op jit(solution)/shard_map/reduce_scatter | solution.py:302
  (340 shorter events, 117.2 us)
Async XLA Ops:
  7.2 29.8 %copy-start.77 = (u32[32]{0:T(128)S(1)}, u32[32]{0:T(128)}, u32[]{:S(2)}) copy-start(u32[32]{0:T(128)} %constant.79) | copy-start | bytes 388
  7.2 31.7 %copy-start.80 = (bf16[96]{0:T(256)(128)(2,1)S(1)}, bf16[96]{0:T(256)(128)(2,1)}, u32[]{:S(2)}) copy-start(bf16[96]{0:T(256)(128)(2,1)} %param.28) | copy-start | bytes 580
  7.2 31.9 %copy-start.81 = (bf16[96]{0:T(256)(128)(2,1)S(1)}, bf16[96]{0:T(256)(128)(2,1)}, u32[]{:S(2)}) copy-start(bf16[96]{0:T(256)(128)(2,1)} %param.32) | copy-start | bytes 580
  7.2 32.1 %copy-start.78 = (bf16[576]{0:T(1024)(128)(2,1)S(1)}, bf16[576]{0:T(1024)(128)(2,1)}, u32[]{:S(2)}) copy-start(bf16[576]{0:T(1024)(128)(2,1)} %param.24) | copy-start | bytes 3460
  7.3 115.1 %copy-start.45 = (bf16[1,768]{1,0:T(2,128)(2,1)S(1)}, bf16[1,768]{1,0:T(2,128)(2,1)}, u32[]{:S(2)}) copy-start(bf16[1,768]{1,0:T(2,128)(2,1)} %param.20) | copy-start | bytes 4612
  7.3 115.1 %all-gather.9.cloned.1.call-start = ((), (), s32[]{:S(2)}) async-start(), calls=%async_computation.15 | async-start | bytes 7962624 | tf_op jit(solution)/shard_map/all_gather | solution.py:49
  8.0 180.0 %all-gather.11.cloned.1.call-start = ((), (), s32[]{:S(2)}) async-start(), calls=%async_computation.16 | async-start | bytes 3981312 | tf_op jit(solution)/shard_map/all_gather | solution.py:51
  8.8 220.9 %all-gather.13.cloned.1.call-start = ((), (), s32[]{:S(2)}) async-start(), calls=%async_computation.17 | async-start | bytes 1327104 | tf_op jit(solution)/shard_map/all_gather | solution.py:53
  9.5 336.4 %all-gather.15.cloned.1.call-start = ((), (), s32[]{:S(2)}) async-start(), calls=%async_computation.18 | async-start | bytes 5308416 | tf_op jit(solution)/shard_map/all_gather | solution.py:55
  10.1 380.9 %all-gather.17.cloned.1.call-start = ((), (), s32[]{:S(2)}) async-start(), calls=%async_computation.19 | async-start | bytes 5308416 | tf_op jit(solution)/shard_map/all_gather | solution.py:57
  11.5 114.9 %copy-start.17 = (s32[1,256,2]{2,1,0:T(8,128)}, s32[1,256,2]{2,1,0:T(8,128)S(1)}, u32[]{:S(2)}) copy-start(s32[1,256,2]{2,1,0:T(8,128)S(1)} %copy.100) | copy-start | bytes 6148
  12.6 175.4 %copy-start.66 = (f32[256]{0:T(256)}, f32[256]{0:T(256)S(1)}, u32[]{:S(2)}) copy-start(f32[256]{0:T(256)S(1)} %broadcast_multiply_fusion.2) | copy-start | bytes 3076
  12.8 26.5 %copy-start.62 = (f32[256]{0:T(256)}, f32[256]{0:T(256)S(1)}, u32[]{:S(2)}) copy-start(f32[256]{0:T(256)S(1)} %fusion.38) | copy-start | bytes 3076
  12.9 175.1 %copy-start.60 = (f32[256]{0:T(256)}, f32[256]{0:T(256)S(1)}, u32[]{:S(2)}) copy-start(f32[256]{0:T(256)S(1)} %fusion.85) | copy-start | bytes 3076
  127.1 60.9 %copy-start.55 = (f32[768]{0:T(1024)}, f32[768]{0:T(1024)S(1)}, u32[]{:S(2)}) copy-start(f32[768]{0:T(1024)S(1)} %get-tuple-element.30) | copy-start | bytes 9220
  127.1 60.9 %copy-start.73 = (f32[768]{0:T(1024)}, f32[768]{0:T(1024)S(1)}, u32[]{:S(2)}) copy-start(f32[768]{0:T(1024)S(1)} %get-tuple-element.29) | copy-start | bytes 9220
  127.1 102.6 %copy-start.42 = (f32[768]{0:T(1024)}, f32[768]{0:T(1024)S(1)}, u32[]{:S(2)}) copy-start(f32[768]{0:T(1024)S(1)} %get-tuple-element.31) | copy-start | bytes 9220
  127.1 106.3 %copy-start.34 = (f32[768]{0:T(1024)}, f32[768]{0:T(1024)S(1)}, u32[]{:S(2)}) copy-start(f32[768]{0:T(1024)S(1)} %get-tuple-element.28) | copy-start | bytes 9220
  127.1 263.9 %copy-start.39 = (f32[768]{0:T(1024)}, f32[768]{0:T(1024)S(1)}, u32[]{:S(2)}) copy-start(f32[768]{0:T(1024)S(1)} %get-tuple-element.26) | copy-start | bytes 9220
  232.5 9.8 copy-start.47
  242.3 70.9 %all-to-all-start = ((bf16[8,80,768]{2,1,0:T(8,128)(2,1)}), bf16[8,80,768]{2,1,0:T(8,128)(2,1)}, u32[]{:S(2)}, u32[]{:S(2)}) async-start(bf16[8,80,768]{2,1,0:T(8,128)(2,1)} %bitcast.193), calls=%async_computation | async-start | bytes 1966080 | tf_op jit(solution)/shard_map/all_to_all | solution.py:136
  309.9 27.8 %copy-start.32 = (bf16[768,8]{0,1:T(8,128)(2,1)}, bf16[768,8]{0,1:T(8,128)(2,1)S(1)}, u32[]{:S(2)}) copy-start(bf16[768,8]{0,1:T(8,128)(2,1)S(1)} %reshape.768) | copy-start | bytes 36868
  320.6 10.6 copy-start
  333.2 18.6 %all-to-all-start.1 = ((bf16[2,320,768]{2,0,1:T(2,128)(2,1)}), bf16[2,320,768]{2,0,1:T(2,128)(2,1)}, u32[]{:S(2)}, u32[]{:S(2)}) async-start(bf16[2,320,768]{2,0,1:T(2,128)(2,1)} %copy.107), calls=%async_computation.1 | async-start | bytes 1966080 | tf_op jit(solution)/shard_map/all_to_all | solution.py:146
  345.9 8.2 copy-start.58
  370.0 28.9 %all-to-all-start.2 = ((bf16[8,80,768]{2,1,0:T(8,128)(2,1)}), bf16[8,80,768]{2,1,0:T(8,128)(2,1)}, u32[]{:S(2)}, u32[]{:S(2)}) async-start(bf16[8,80,768]{2,1,0:T(8,128)(2,1)} %bitcast.194), calls=%async_computation.2 | async-start | bytes 1966080 | tf_op jit(solution)/shard_map/all_to_all | solution.py:187
  374.6 24.3 %copy-start.51 = (s32[256,2]{0,1:T(2,128)S(1)}, s32[256,2]{0,1:T(2,128)}, u32[]{:S(2)}) copy-start(s32[256,2]{0,1:T(2,128)} %copy.101) | copy-start | bytes 6148
  398.9 28.5 %copy-start.37 = (bf16[256,8]{0,1:T(8,128)(2,1)}, bf16[256,8]{0,1:T(8,128)(2,1)S(1)}, u32[]{:S(2)}) copy-start(bf16[256,8]{0,1:T(8,128)(2,1)S(1)} %multiply_reduce_fusion.5) | copy-start | bytes 12292
  400.2 12.2 copy-start.25
  412.4 8.7 copy-start.82
  423.1 18.5 %all-to-all-start.3 = ((bf16[2,320,768]{2,0,1:T(2,128)(2,1)}), bf16[2,320,768]{2,0,1:T(2,128)(2,1)}, u32[]{:S(2)}, u32[]{:S(2)}) async-start(bf16[2,320,768]{2,0,1:T(2,128)(2,1)} %copy.111), calls=%async_computation.3 | async-start | bytes 1966080 | tf_op jit(solution)/shard_map/all_to_all | solution.py:205
  427.3 113.9 %reduce-scatter.36.cloned.1.call-start = ((), (), s32[]{:S(2)}) async-start(), calls=%async_computation.28 | async-start | bytes 221184
  428.4 125.9 %reduce-scatter.40.cloned.1.call-start = ((), (), s32[]{:S(2)}) async-start(), calls=%async_computation.30 | async-start | bytes 221184
  435.8 183.3 %reduce-scatter.38.cloned.1.call-start = ((), (), s32[]{:S(2)}) async-start(), calls=%async_computation.29 | async-start | bytes 884736
  441.4 242.0 %reduce-scatter.34.cloned.1.call-start = ((), (), s32[]{:S(2)}) async-start(), calls=%async_computation.27 | async-start | bytes 221184
  472.3 17.4 %copy-start.29 = (bf16[12,64,256]{2,1,0:T(8,128)(2,1)}, bf16[12,64,256]{2,1,0:T(8,128)(2,1)S(1)}, u32[]{:S(2)}) copy-start(bf16[12,64,256]{2,1,0:T(8,128)(2,1)S(1)} %get-tuple-element.82) | copy-start | bytes 1179652
  474.1 276.7 %reduce-scatter.24.cloned.1.call-start = ((), (), s32[]{:S(2)}) async-start(), calls=%async_computation.22 | async-start | bytes 1327104 | tf_op jit(solution)/shard_map/reduce_scatter | solution.py:322
  476.7 372.6 %reduce-scatter.26.cloned.1.call-start = ((), (), s32[]{:S(2)}) async-start(), calls=%async_computation.23 | async-start | bytes 5308416 | tf_op jit(solution)/shard_map/reduce_scatter | solution.py:328
  480.4 467.9 %reduce-scatter.28.cloned.1.call-start = ((), (), s32[]{:S(2)}) async-start(), calls=%async_computation.24 | async-start | bytes 5308416 | tf_op jit(solution)/shard_map/reduce_scatter | solution.py:334
  487.7 543.6 %reduce-scatter.22.cloned.1.call-start = ((), (), s32[]{:S(2)}) async-start(), calls=%async_computation.21 | async-start | bytes 3981312 | tf_op jit(solution)/shard_map/reduce_scatter | solution.py:316
  494.2 669.6 %reduce-scatter.20.cloned.1.call-start = ((), (), s32[]{:S(2)}) async-start(), calls=%async_computation.20 | async-start | bytes 7962624 | tf_op jit(solution)/shard_map/reduce_scatter | solution.py:310
  495.6 9.0 copy-start.3
  495.6 9.0 copy-start.19
  516.7 813.1 %reduce-scatter.30.cloned.1.call-start = ((), (), s32[]{:S(2)}) async-start(), calls=%async_computation.25 | async-start | bytes 10616832 | tf_op jit(solution)/shard_map/reduce_scatter | solution.py:296
  527.6 968.3 %reduce-scatter.32.cloned.1.call-start = ((), (), s32[]{:S(2)}) async-start(), calls=%async_computation.26 | async-start | bytes 10616832 | tf_op jit(solution)/shard_map/reduce_scatter | solution.py:302
  539.2 81.6 %copy-start.68 = (bf16[768]{0:T(1024)(128)(2,1)S(1)}, bf16[768]{0:T(1024)(128)(2,1)}, u32[]{:S(2)}) copy-start(bf16[768]{0:T(1024)(128)(2,1)} %get-tuple-element.54) | copy-start | bytes 4612
  539.2 81.7 %copy-start.69 = (bf16[768]{0:T(1024)(128)(2,1)S(1)}, bf16[768]{0:T(1024)(128)(2,1)}, u32[]{:S(2)}) copy-start(bf16[768]{0:T(1024)(128)(2,1)} %get-tuple-element.66) | copy-start | bytes 4612
  539.2 81.7 %copy-start.71 = (bf16[3072]{0:T(1024)(128)(2,1)S(1)}, bf16[3072]{0:T(1024)(128)(2,1)}, u32[]{:S(2)}) copy-start(bf16[3072]{0:T(1024)(128)(2,1)} %get-tuple-element.77) | copy-start | bytes 18436
  (55 other events, 187.1 us)
Sparse Core Ops, SparseCore 0:
  10.3 112.0 all-gather.8
  124.5 63.4 all-gather.10
  190.2 39.4 all-gather.12
  231.7 79.0 all-gather.14
  312.8 78.0 all-gather.16
  431.1 59.7 reduce-scatter.35
  494.2 60.0 reduce-scatter.39
  557.6 61.4 reduce-scatter.37
  623.3 60.0 reduce-scatter.33
  687.6 63.0 reduce-scatter.23
  754.9 94.3 reduce-scatter.25
  853.2 95.0 reduce-scatter.27
  952.3 78.8 reduce-scatter.21
  1035.3 128.5 reduce-scatter.19
  1167.3 162.4 reduce-scatter.29
  1333.3 162.5 reduce-scatter.31
where the time goes:
time: 1520 us; the launch traced here: 1510 us
  waiting for transfers between devices  969 us (64%)
  blocking collectives  240 us (16%)
  matrix products  131 us (9%)
  local copies, waits for them, and re-layouts  80.1 us (5%)
  other arithmetic  47.6 us (3%)
  starting transfers between devices  18.9 us (1%)
  between operations  18.6 us (1%)
    reduce_scatter x1, waiting for transfers between devices, on_device(): lax.psum_scatter(expert_out_grad.astype(jnp.bfloat16), 'dp', scatter_dime...  163 us
    reduce_scatter x1, waiting for transfers between devices, on_device(): lax.psum_scatter(ada_weight_grad.astype(jnp.bfloat16), 'dp', scatter_dime...  133 us
    unnamed x20, waiting for transfers between devices  101 us
    reduce_scatter x1, waiting for transfers between devices, on_device(): lax.psum_scatter(shared_out_grad.astype(jnp.bfloat16), 'dp', scatter_dime...  99 us
    reduce_scatter x1, waiting for transfers between devices, on_device(): lax.psum_scatter(shared_in_grad.astype(jnp.bfloat16), 'dp', scatter_dimen...  98.5 us
    psum x1, blocking collectives, on_device(): lax.psum((dense_parts[0], dense_parts[1], dense_parts[2], dense_parts[3],...  95.3 us
    reduce_scatter x1, waiting for transfers between devices, on_device(): lax.psum_scatter(qkv_weight_grad.astype(jnp.bfloat16), 'dp', scatter_dime...  83 us
    reduce_scatter x1, waiting for transfers between devices, on_device(): lax.psum_scatter(expert_in_grad.astype(jnp.bfloat16), 'dp', scatter_dimen...  70.7 us
  transfers between devices with their start and end apart: 20, of which 14 were waited for; matrix products, arithmetic and copies ran while one was open for 15% of the time, Pallas kernels for 0%

commit v1 on v0

--- a/solution.py
+++ b/solution.py
@@ -1,12 +1,1356 @@
+import functools
+
 import jax
 import jax.numpy as jnp
 from jax import lax
+from jax.experimental import pallas as pl
+from jax.experimental.pallas import tpu as pltpu
 from jax.sharding import PartitionSpec as P
 
 HEADS = 12
 HEAD_DIM = 64
 E = 8
 CAP = 80
+MESH = pl.DeviceIdType.MESH
+F32 = jnp.float32
+B16 = jnp.bfloat16
+VMEM_LIMIT = 60 * 1024 * 1024
+SCALE = HEAD_DIM ** (-0.5)
+GELU_C = 0.7978845608028654
+NZ, NX = 4, 2
+
+
+def coords():
+    dp = lax.axis_index("dp")
+    ex = lax.axis_index("expert")
+    return lax.div(dp, NX), lax.rem(dp, NX), lax.div(ex, 2), lax.rem(ex, 2)
+
+
+def dev(z, x, y, c):
+    return (NX * z + x, 2 * y + c)
+
+
+def dot(a, b):
+    return jnp.dot(a, b, preferred_element_type=F32)
+
+
+def dot_nt(a, b):
+    return lax.dot_general(a, b, (((1,), (1,)), ((), ())), preferred_element_type=F32)
+
+
+def dot_tn(a, b):
+    return lax.dot_general(a, b, (((0,), (0,)), ((), ())), preferred_element_type=F32)
+
+
+def gelu_parts(v):
+    v2 = v * v
+    t = jnp.tanh(GELU_C * v * (1.0 + 0.044715 * v2))
+    h = 0.5 * (1.0 + t)
+    return v * h, h + 0.5 * v * (1.0 - t * t) * (GELU_C * (1.0 + 0.134145 * v2))
+
+
+def norm_parts(v):
+    centred = v - jnp.mean(v, axis=-1, keepdims=True)
+    r = lax.rsqrt(jnp.mean(centred * centred, axis=-1, keepdims=True) + 1e-06)
+    return centred * r, r
+
+
+def norm_back(u, n, r):
+    return r * (
+        u - jnp.mean(u, axis=-1, keepdims=True) - n * jnp.mean(u * n, axis=-1, keepdims=True)
+    )
+
+
+def remote(src, dst, send, recv, to):
+    return pltpu.make_async_remote_copy(
+        src_ref=src,
+        dst_ref=dst,
+        send_sem=send,
+        recv_sem=recv,
+        device_id=to,
+        device_id_type=MESH,
+    )
+
+
+def greet(barrier, to):
+    pl.semaphore_signal(barrier, inc=1, device_id=to, device_id_type=MESH)
+
+
+def params(collective_id=None):
+    if collective_id is None:
+        return pltpu.CompilerParams(vmem_limit_bytes=VMEM_LIMIT)
+    return pltpu.CompilerParams(
+        vmem_limit_bytes=VMEM_LIMIT, collective_id=collective_id, has_side_effects=True
+    )
+
+
+VM = pl.BlockSpec(memory_space=pltpu.VMEM)
+HB = pl.BlockSpec(memory_space=pl.ANY)
+
+
+def sds(shape, dtype):
+    return jax.ShapeDtypeStruct(shape, dtype)
+
+
+class Gather:
+    def __init__(self, shards, fulls, splits, sems):
+        self.z, self.x, self.y, self.c = coords()
+        self.mats = list(zip(shards, fulls, splits))
+        (self.zs, self.zr, self.xs, self.xr, self.ys, self.yr, self.cs, self.cr, self.loc) = sems
+
+    @staticmethod
+    def semaphores(count):
+        dma = pltpu.SemaphoreType.DMA
+        return [
+            dma((count, 2, NZ)),
+            dma((count, NZ)),
+            dma((count, NZ)),
+            dma((count, NZ)),
+            dma((count, NZ, NX)),
+            dma((count, NZ, NX)),
+            dma((count, NZ, NX, 2)),
+            dma((count, NZ, NX, 2)),
+            dma((count,)),
+        ]
+
+    def region(self, m, zb, xb, yh, ch):
+        shard, full, split = self.mats[m]
+        rows, width = shard.shape[0], shard.shape[1] // 2
+        start = (NX * zb + xb) * rows
+        if split:
+            rows = rows // 2
+            start = start + yh * rows
+        return full.at[
+            pl.ds(pl.multiple_of(start, 16), rows), pl.ds(pl.multiple_of(ch * width, 128), width)
+        ]
+
+    def own(self, m):
+        shard, full, split = self.mats[m]
+        rows, width = shard.shape[0], shard.shape[1] // 2
+        start = 0
+        if split:
+            rows = rows // 2
+            start = self.y * rows
+        return shard.at[
+            pl.ds(pl.multiple_of(start, 16), rows),
+            pl.ds(pl.multiple_of(self.c * width, 128), width),
+        ]
+
+    def zcopy(self, m, zb, side, mine=False):
+        here = self.region(m, zb, self.x, self.y, self.c)
+        step = 1 if side else -1
+        return remote(
+            self.own(m) if mine else here,
+            here,
+            self.zs.at[m, side, zb],
+            self.zr.at[m, zb],
+            dev(lax.rem(self.z + step + NZ, NZ), self.x, self.y, self.c),
+        )
+
+    def xcopy(self, m, zb, mine=False, xb=None):
+        here = self.region(m, zb, self.x if xb is None else xb, self.y, self.c)
+        return remote(
+            self.own(m) if mine else here,
+            here,
+            self.xs.at[m, zb],
+            self.xr.at[m, zb],
+            dev(self.z, 1 - self.x, self.y, self.c),
+        )
+
+    def ycopy(self, m, zb, xb, yh=None):
+        here = self.region(m, zb, xb, self.y if yh is None else yh, self.c)
+        return remote(
+            here,
+            here,
+            self.ys.at[m, zb, xb],
+            self.yr.at[m, zb, xb],
+            dev(self.z, self.x, 1 - self.y, self.c),
+        )
+
+    def ccopy(self, m, zb, xb, yh, ch=None):
+        here = self.region(m, zb, xb, yh, self.c if ch is None else ch)
+        slot = yh if self.mats[m][2] else 0
+        return remote(
+            here,
+            here,
+            self.cs.at[m, zb, xb, slot],
+            self.cr.at[m, zb, xb, slot],
+            dev(self.z, self.x, self.y, 1 - self.c),
+        )
+
+    def local(self, m):
+        shard, full, _ = self.mats[m]
+        rows = shard.shape[0]
+        start = (NX * self.z + self.x) * rows
+        return pltpu.make_async_copy(
+            shard, full.at[pl.ds(pl.multiple_of(start, 16), rows), :], self.loc.at[m]
+        )
+
+    def blocks(self, step):
+        if step == 0:
+            return [(self.z, None, None)]
+        return [
+            (self.z - step, self.z - step >= 0, 1),
+            (self.z + step, self.z + step < NZ, 0),
+        ]
+
+    def more(self, side):
+        return self.z + 1 < NZ if side else self.z - 1 >= 0
+
+    def begin(self, m):
+        for side in (1, 0):
+
+            @pl.when(self.more(side))
+            def _():
+                self.zcopy(m, self.z, side, True).start()
+
+        self.xcopy(m, self.z, True).start()
+        self.local(m).start()
+
+    def spread(self, m, zb, xb):
+        if self.mats[m][2]:
+            self.ycopy(m, zb, xb).start()
+        self.ccopy(m, zb, xb, self.y).start()
+
+    def take_z(self, m, step):
+        for zb, exists, side in self.blocks(step):
+
+            @pl.when(exists)
+            def _():
+                self.zcopy(m, zb, side).wait_recv()
+                if step < NZ - 1:
+
+                    @pl.when(self.more(side))
+                    def _():
+                        self.zcopy(m, zb, side).start()
+
+                self.xcopy(m, zb).start()
+                self.spread(m, zb, self.x)
+
+    def take_x(self, m, step):
+        for zb, exists, _ in self.blocks(step):
+
+            def body():
+                self.xcopy(m, zb, False, 1 - self.x).wait_recv()
+                self.spread(m, zb, 1 - self.x)
+
+            body() if exists is None else pl.when(exists)(body)
+
+    def others(self, m, step, action):
+        for zb, exists, _ in self.blocks(step):
+            for xb in (self.x, 1 - self.x) if step else (1 - self.x,):
+                body = functools.partial(action, m, zb, xb)
+                body() if exists is None else pl.when(exists)(body)
+
+    def take_y(self, m, step):
+        if not self.mats[m][2]:
+            return
+
+        def action(m, zb, xb):
+            self.ycopy(m, zb, xb, 1 - self.y).wait_recv()
+            self.ccopy(m, zb, xb, 1 - self.y).start()
+
+        self.others(m, step, action)
+
+    def finish(self, m):
+        def action(m, zb, xb):
+            for yh in (self.y, 1 - self.y) if self.mats[m][2] else (self.y,):
+                self.ccopy(m, zb, xb, yh, 1 - self.c).wait_recv()
+                self.ccopy(m, zb, xb, yh).wait_send()
+            if self.mats[m][2]:
+                self.ycopy(m, zb, xb).wait_send()
+
+        for step in range(NZ):
+            self.others(m, step, action)
+        for side in (1, 0):
+
+            @pl.when(self.more(side))
+            def _():
+                self.zcopy(m, self.z, side, True).wait_send()
+
+        for step in range(1, NZ):
+            for zb, exists, side in self.blocks(step):
+
+                @pl.when(exists)
+                def _():
+                    self.xcopy(m, zb).wait_send()
+                    if step < NZ - 1:
+
+                        @pl.when(self.more(side))
+                        def _():
+                            self.zcopy(m, zb, side).wait_send()
+
+        self.xcopy(m, self.z, True).wait_send()
+        self.local(m).wait()
+
+    def run(self, mats):
+        for step in range(NZ):
+            for m in mats:
+                if step:
+                    self.take_z(m, step)
+                self.take_x(m, step)
+            if step:
+                for m in mats:
+                    self.take_y(m, step - 1)
+        for m in mats:
+            self.take_y(m, NZ - 1)
+        for m in mats:
+            self.finish(m)
+
+
+def gather_kernel(splits, *refs):
+    count = len(splits)
+    ada, pack = refs[:2]
+    shards = refs[2 : 2 + count]
+    rest = refs[2 + count :]
+    mod_ref, packs = rest[:2]
+    fulls = rest[2 : 2 + count]
+    sent, got, s1, r1, s2, r2 = rest[2 + count : 8 + count]
+    plan = Gather(shards, fulls, splits, rest[8 + count :])
+    dp, ex = lax.axis_index("dp"), lax.axis_index("expert")
+    n = NZ * NX
+    barrier = pltpu.get_barrier_semaphore()
+    for p in range(n):
+
+        @pl.when(p != dp)
+        def _():
+            greet(barrier, (p, ex))
+
+    greet(barrier, dev(plan.z, plan.x, 1 - plan.y, plan.c))
+    greet(barrier, dev(plan.z, plan.x, plan.y, 1 - plan.c))
+    pl.semaphore_wait(barrier, n + 1)
+
+    def first(p):
+        return remote(pack, packs.at[dp], s1.at[p], r1.at[dp], (p, ex))
+
+    def first_from(p):
+        return remote(pack, packs.at[p], s1.at[p], r1.at[p], (p, ex))
+
+    def second(p):
+        return remote(sent.at[p], got.at[dp], s2.at[p], r2.at[dp], (p, ex))
+
+    def second_from(p):
+        return remote(sent.at[p], got.at[p], s2.at[p], r2.at[p], (p, ex))
+
+    def peers(action):
+        for p in range(n):
+
+            @pl.when(p != dp)
+            def _():
+                action(p)
+
+    peers(lambda p: first(p).start())
+    for m in range(count):
+        plan.begin(m)
+    packs[dp] = pack[...]
+    peers(lambda p: first_from(p).wait_recv())
+    rows = jnp.concatenate([packs[p, pl.ds(24 + dp, 1), :] for p in range(n)], axis=0)
+    width = ada.shape[0]
+    partial = dot(rows[:, :width].astype(B16), ada[...])
+    for j in range(partial.shape[1] // 128):
+        sent[:, j, :] = partial[:, 128 * j : 128 * (j + 1)]
+    peers(lambda p: second(p).start())
+    got[dp] = sent[dp]
+
+    plan.run(range(count))
+
+    peers(lambda p: second_from(p).wait_recv())
+    total = got[0]
+    for p in range(1, n):
+        total = total + got[p]
+    per = mod_ref.shape[1] // 128
+    mod_ref[...] = jnp.zeros_like(mod_ref)
+    for i in range(6):
+        for b in range(per):
+            mod_ref[i : i + 1, 128 * b : 128 * (b + 1)] = total[per * i + b : per * i + b + 1, :]
+    peers(lambda p: first(p).wait_send())
+    peers(lambda p: second(p).wait_send())
+
+
+def gather_dense(ada, pack, shards, splits):
+    n = NZ * NX
+    dma = pltpu.SemaphoreType.DMA
+    tiles = ada.shape[1] // 128
+    tiles = (tiles + 7) // 8 * 8
+    fulls = [sds((n * s.shape[0], s.shape[1]), s.dtype) for s in shards]
+    out = pl.pallas_call(
+        functools.partial(gather_kernel, splits),
+        out_shape=[sds((8, ada.shape[1] // 6), F32), sds((n,) + pack.shape, F32)] + fulls,
+        in_specs=[VM, VM] + [HB] * len(shards),
+        out_specs=[VM, VM] + [HB] * len(shards),
+        scratch_shapes=[
+            pltpu.VMEM((n, tiles, 128), F32),
+            pltpu.VMEM((n, tiles, 128), F32),
+            dma((n,)),
+            dma((n,)),
+            dma((n,)),
+            dma((n,)),
+        ]
+        + Gather.semaphores(len(shards)),
+        compiler_params=params(1),
+        name="gather_dense",
+    )(ada, pack, *shards)
+    return out[0], out[1], out[2:]
+
+
+def choose_rows(place, slots):
+    return place == lax.broadcasted_iota(jnp.int32, (place.shape[0], slots), 1)
+
+
+def front_kernel(
+    tok, cot, routes, mod_in, abias, qkv, outw, bias, router,
+    normed_o, proj_o, lsum_o, mixed_o, att_o, resid_o, second_o, gates_o, place_o, sbuf_o, gbuf_o, mod_o,
+):
+    length, width = tok.shape
+    mod = mod_in[...] + abias[...]
+    mod_o[...] = mod
+    source = tok[...].astype(F32)
+    n1, _ = norm_parts(source)
+    normed = (n1 * (1.0 + mod[1:2]) + mod[0:1]).astype(B16)
+    normed_o[...] = normed
+    for k in range(3):
+        part = dot(normed, qkv[:, k * width : (k + 1) * width])
+        if k != 1:
+            part = part + bias[k // 2 : k // 2 + 1, :]
+        proj_o[:, k * width : (k + 1) * width] = part.astype(B16)
+    low_lane = lax.broadcasted_iota(jnp.int32, (length, 128), 1) < HEAD_DIM
+    lane = lax.broadcasted_iota(jnp.int32, (length, 128), 1)
+    lsum = jnp.zeros((length, 128), F32)
+    for p in range(HEADS // 2):
+        q2 = proj_o[:, 128 * p : 128 * (p + 1)]
+        k2 = proj_o[:, width + 128 * p : width + 128 * (p + 1)]
+        v2 = proj_o[:, 2 * width + 128 * p : 2 * width + 128 * (p + 1)]
+        outs = []
+        for h in range(2):
+            mine = low_lane if h == 0 else jnp.logical_not(low_lane)
+            s = dot_nt(jnp.where(mine, q2, jnp.zeros_like(q2)), k2) * SCALE
+            peak = jnp.max(s, axis=-1, keepdims=True)
+            e = jnp.exp(s - peak)
+            total = jnp.sum(e, axis=-1, keepdims=True)
+            lsum = jnp.where(lane == 2 * p + h, peak + jnp.log(total), lsum)
+            outs.append(dot((e / total).astype(B16), v2))
+        mixed_o[:, 128 * p : 128 * (p + 1)] = jnp.where(low_lane, outs[0], outs[1]).astype(B16)
+    lsum_o[...] = lsum
+    att = dot(mixed_o[...], outw[...]) + bias[2:3, :]
+    att_o[...] = att
+    resid = source + mod[2:3] * att
+    resid_o[...] = resid
+    n2, _ = norm_parts(resid)
+    second = (n2 * (1.0 + mod[4:5]) + mod[3:4]).astype(B16)
+    second_o[...] = second
+    logits = dot(second, router[...])
+    picks = [(routes[:, k : k + 1] == lane) for k in range(2)]
+    chosen = [jnp.sum(jnp.where(pick, logits, 0.0), axis=-1, keepdims=True) for pick in picks]
+    top = jnp.maximum(chosen[0], chosen[1])
+    ex = [jnp.exp(v - top) for v in chosen]
+    gates = [v / (ex[0] + ex[1]) for v in ex]
+    gates_o[...] = jnp.where(lane == 0, gates[0], jnp.where(lane == 1, gates[1], 0.0))
+    both = jnp.where(picks[0], 1.0, 0.0) + jnp.where(picks[1], 1.0, 0.0)
+    earlier = (
+        lax.broadcasted_iota(jnp.int32, (length, length), 1)
+        < lax.broadcasted_iota(jnp.int32, (length, length), 0)
+    )
+    rank = dot(jnp.where(earlier, 1.0, 0.0).astype(B16), both.astype(B16))
+    places = []
+    for k in range(2):
+        slot = jnp.sum(jnp.where(picks[k], rank, 0.0), axis=-1, keepdims=True).astype(jnp.int32)
+        places.append(jnp.where(slot < CAP, routes[:, k : k + 1] * CAP + slot, -1))
+    place_o[...] = jnp.where(lane == 0, places[0], jnp.where(lane == 1, places[1], -1))
+    maps = [jnp.where(choose_rows(v, E * CAP), 1.0, 0.0) for v in places]
+    sbuf_o[...] = dot_tn((maps[0] + maps[1]).astype(B16), second).astype(B16)
+    moe_grad = (mod[5:6] * cot[...].astype(F32)).astype(B16).astype(F32)
+    pair = [(g * moe_grad).astype(B16) for g in gates]
+    gbuf_o[...] = (
+        dot_tn(maps[0].astype(B16), pair[0]) + dot_tn(maps[1].astype(B16), pair[1])
+    ).astype(B16)
+
+
+def front(tok, cot, routes, mod_in, abias, qkv, outw, bias, router):
+    length, width = tok.shape
+    rows = E * CAP
+    return pl.pallas_call(
+        front_kernel,
+        out_shape=[
+            sds((length, width), B16),
+            sds((length, 3 * width), B16),
+            sds((length, 128), F32),
+            sds((length, width), B16),
+            sds((length, width), F32),
+            sds((length, width), F32),
+            sds((length, width), B16),
+            sds((length, 128), F32),
+            sds((length, 128), jnp.int32),
+            sds((rows, width), B16),
+            sds((rows, width), B16),
+            sds((8, width), F32),
+        ],
+        in_specs=[VM] * 9,
+        out_specs=[VM] * 12,
+        compiler_params=params(),
+        name="attention_front",
+    )(tok, cot, routes, mod_in, abias, qkv, outw, bias, router)
+
+
+def plane_peer(k):
+    z, x, y, c = coords()
+    xt = 1 - x if k & 1 else x
+    ct = 1 - c if k & 2 else c
+    yt = 1 - y if k & 4 else y
+    return dev(z, xt, yt, ct), 4 * yt + 2 * ct + xt
+
+
+def plane_rank():
+    _, x, y, c = coords()
+    return 4 * y + 2 * c + x
+
+
+def greet_plane():
+    barrier = pltpu.get_barrier_semaphore()
+    for k in range(1, E):
+        greet(barrier, plane_peer(k)[0])
+    pl.semaphore_wait(barrier, E - 1)
+
+
+def slot_rows(ref, rank):
+    return ref.at[pl.ds(pl.multiple_of(rank * CAP, 16), CAP), :]
+
+
+def plane_exchange(sources, targets, send, recv):
+    rank = plane_rank()
+
+    def copy(k, i, to=None):
+        peer, other = plane_peer(k)
+        return remote(
+            slot_rows(sources[i], other), slot_rows(targets[i], rank), send.at[i, k], recv.at[i, k], peer
+        )
+
+    pairs = [(k, i) for k in (7, 5, 6, 4, 3, 1, 2) for i in range(len(sources))]
+    for k, i in pairs:
+        copy(k, i).start()
+    for source, target in zip(sources, targets):
+        start = pl.multiple_of(rank * CAP, 16)
+        target[pl.ds(start, CAP), :] = source[pl.ds(start, CAP), :]
+
+    def take(k, i):
+        _, other = plane_peer(k)
+        return remote(
+            slot_rows(sources[i], other), slot_rows(targets[i], other), send.at[i, k], recv.at[i, k],
+            plane_peer(k)[0],
+        )
+
+    def wait_in():
+        for k, i in pairs:
+            take(k, i).wait_recv()
+
+    def wait_out():
+        for k, i in pairs:
+            take(k, i).wait_send()
+
+    return wait_in, wait_out
+
+
+EXPERT_CHUNK = 512
+
+
+def expert_kernel(
+    sbuf, gbuf, win_h, wout_h, bin_r, bout_r,
+    dwin, dwout, res, bgr, ebias,
+    rows, grads, win, wout, acc, back, send, recv, wsem,
+):
+    x = coords()[1]
+    loads = [
+        pltpu.make_async_copy(win_h.at[x], win, wsem.at[0]),
+        pltpu.make_async_copy(wout_h.at[x], wout, wsem.at[1]),
+    ]
+    for load in loads:
+        load.start()
+    greet_plane()
+    wait_in, wait_out = plane_exchange((sbuf, gbuf), (rows, grads), send, recv)
+    for load in loads:
+        load.wait()
+    first_x = x == 0
+    bout = jnp.where(first_x, bout_r[0:1, :], bout_r[1:2, :])
+    acc[...] = jnp.zeros_like(acc) + bout
+    back[...] = jnp.zeros_like(back)
+    ebias[...] = jnp.zeros_like(ebias)
+    wait_in()
+    width = rows.shape[1]
+    hidden = win.shape[1]
+    chunk = EXPERT_CHUNK
+    tiles = chunk // 128
+    column = jnp.sum(grads[...].astype(F32), axis=0, keepdims=True)
+    for j in range(width // 128):
+        at = hidden // 128 + j
+        ebias[at : at + 1, :] = column[:, 128 * j : 128 * (j + 1)]
+
+    def body(f, carry):
+        cols = pl.ds(pl.multiple_of(f * chunk, 128), chunk)
+        bias = jnp.where(first_x, bin_r[0:1, cols], bin_r[1:2, cols])
+        w1 = win[:, cols]
+        w2 = wout[cols, :]
+        data = rows[...]
+        grad = grads[...]
+        act, slope = gelu_parts(dot(data, w1) + bias)
+        low = act.astype(B16)
+        acc[...] += dot(low, w2)
+        pre = (dot_nt(grad, w2) * slope).astype(B16)
+        dwout[cols, :] = dot_tn(low, grad).astype(B16)
+        dwin[:, cols] = dot_tn(data, pre).astype(B16)
+        back[...] += dot_nt(pre, w1)
+        col = jnp.sum(pre.astype(F32), axis=0, keepdims=True)
+        for j in range(tiles):
+            ebias[pl.ds(f * tiles + j, 1), :] = col[:, 128 * j : 128 * (j + 1)]
+        return carry
+
+    lax.fori_loop(0, hidden // chunk, body, 0)
+    res[...] = acc[...].astype(B16)
+    bgr[...] = back[...].astype(B16)
+    wait_out()
+
+
+def expert(sbuf, gbuf, win, wout, bin_r, bout_r):
+    rows, width = sbuf.shape
+    hidden = win.shape[2]
+    dma = pltpu.SemaphoreType.DMA
+    return pl.pallas_call(
+        expert_kernel,
+        out_shape=[
+            sds((width, hidden), B16),
+            sds((hidden, width), B16),
+            sds((rows, width), B16),
+            sds((rows, width), B16),
+            sds((32, 128), F32),
+        ],
+        in_specs=[VM, VM, HB, HB, VM, VM],
+        out_specs=[VM] * 5,
+        scratch_shapes=[
+            pltpu.VMEM((rows, width), B16),
+            pltpu.VMEM((rows, width), B16),
+            pltpu.VMEM((width, hidden), B16),
+            pltpu.VMEM((hidden, width), B16),
+            pltpu.VMEM((rows, width), F32),
+            pltpu.VMEM((rows, width), F32),
+            dma((2, E)),
+            dma((2, E)),
+            dma((2,)),
+        ],
+        compiler_params=params(2),
+        name="routed_expert",
+    )(sbuf, gbuf, win, wout, bin_r, bout_r)
+
+
+SHARED_CHUNK = 768
+
+
+def middle_kernel(
+    res, bgr, second_r, resid_r, att_r, cot, routes, mod, sin, sout, sinb, bias, router, gates_r, place_r,
+    mixed, outw,
+    out_o, rgrad_o, mgrad_o, dsin, dsout, dout, drouter, vecs, mg2,
+    ret, retg, shared, sgrad, send, recv,
+):
+    greet_plane()
+    wait_in, wait_out = plane_exchange((res, bgr), (ret, retg), send, recv)
+    length, width = second_r.shape
+    hidden = sin.shape[1]
+    chunk = SHARED_CHUNK
+    second = second_r[...]
+    grad_out = cot[...].astype(F32)
+    moe_low = (mod[5:6] * grad_out).astype(B16)
+    moe_grad = moe_low.astype(F32)
+    shared[...] = jnp.zeros_like(shared) + bias[3:4, :]
+    sgrad[...] = jnp.zeros_like(sgrad)
+    vecs[...] = jnp.zeros_like(vecs)
+
+    def body(f, carry):
+        cols = pl.ds(pl.multiple_of(f * chunk, 128), chunk)
+        w1 = sin[:, cols]
+        w2 = sout[cols, :]
+        act, slope = gelu_parts(dot(second, w1) + sinb[:, cols])
+        low = act.astype(B16)
+        shared[...] += dot(low, w2)
+        pre = (dot_nt(moe_low, w2) * slope).astype(B16)
+        dsout[cols, :] = dot_tn(low, moe_low).astype(B16)
+        dsin[:, cols] = dot_tn(second, pre).astype(B16)
+        sgrad[...] += dot_nt(pre, w1)
+        col = jnp.sum(pre.astype(F32), axis=0, keepdims=True)
+        for j in range(chunk // 128):
+            vecs[pl.ds(f * (chunk // 128) + j, 1), :] = col[:, 128 * j : 128 * (j + 1)]
+        return carry
+
+    lax.fori_loop(0, hidden // chunk, body, 0)
+    lane = lax.broadcasted_iota(jnp.int32, (length, 128), 1)
+    gates = [gates_r[:, k : k + 1] for k in range(2)]
+    maps = [
+        jnp.where(choose_rows(place_r[:, k : k + 1], E * CAP), 1.0, 0.0) for k in range(2)
+    ]
+    wait_in()
+    back = ret[...]
+    rows = [dot(m.astype(B16), back) for m in maps]
+    moe = shared[...] + (gates[0] * rows[0] + gates[1] * rows[1])
+    resid = resid_r[...]
+    out_o[...] = (resid + mod[5:6] * moe).astype(B16)
+    mg2[...] = jnp.zeros_like(mg2)
+    mg2[5:6, :] = jnp.sum(grad_out * moe, axis=0, keepdims=True)
+    ggrad = [jnp.sum(moe_grad * r, axis=-1, keepdims=True) for r in rows]
+    inner = gates[0] * ggrad[0] + gates[1] * ggrad[1]
+    lgrad = jnp.zeros((length, 128), F32)
+    for k in range(2):
+        pick = routes[:, k : k + 1] == lane
+        lgrad = lgrad + jnp.where(pick, gates[k] * (ggrad[k] - inner), 0.0)
+    lgrad = lgrad.astype(B16)
+    drouter[...] = dot_tn(lgrad, second)[0:E, :]
+    grad = (
+        sgrad[...]
+        + dot((maps[0] + maps[1]).astype(B16), retg[...])
+        + dot_nt(lgrad, router[...])
+    )
+    n2, r2 = norm_parts(resid)
+    mg2[3:4, :] = jnp.sum(grad, axis=0, keepdims=True)
+    mg2[4:5, :] = jnp.sum(grad * n2, axis=0, keepdims=True)
+    rgrad = grad_out + norm_back(grad * (1.0 + mod[4:5]), n2, r2)
+    rgrad_o[...] = rgrad
+    agrad = (mod[2:3] * rgrad).astype(B16)
+    mg2[2:3, :] = jnp.sum(rgrad * att_r[...], axis=0, keepdims=True)
+    dout[...] = dot_tn(mixed[...], agrad).astype(B16)
+    mgrad_o[...] = dot_nt(agrad, outw[...]).astype(B16)
+    sums = [
+        jnp.sum(moe_grad, axis=0, keepdims=True),
+        jnp.sum(agrad.astype(F32), axis=0, keepdims=True),
+    ]
+    base = hidden // 128
+    for i, row in enumerate(sums):
+        for j in range(width // 128):
+            at = base + i * (width // 128) + j
+            vecs[at : at + 1, :] = row[:, 128 * j : 128 * (j + 1)]
+    wait_out()
+
+
+def middle(*args):
+    res, second, sin = args[0], args[2], args[8]
+    length, width = second.shape
+    rows, hidden = res.shape[0], sin.shape[1]
+    dma = pltpu.SemaphoreType.DMA
+    return pl.pallas_call(
+        middle_kernel,
+        out_shape=[
+            sds((length, width), B16),
+            sds((length, width), F32),
+            sds((length, width), B16),
+            sds((width, hidden), B16),
+            sds((hidden, width), B16),
+            sds((width, width), B16),
+            sds((E, width), F32),
+            sds((40, 128), F32),
+            sds((8, width), F32),
+        ],
+        in_specs=[VM] * 17,
+        out_specs=[VM] * 9,
+        scratch_shapes=[
+            pltpu.VMEM((rows, width), B16),
+            pltpu.VMEM((rows, width), B16),
+            pltpu.VMEM((length, width), F32),
+            pltpu.VMEM((length, width), F32),
+            dma((2, E)),
+            dma((2, E)),
+        ],
+        compiler_params=params(3),
+        name="shared_expert_combine",
+    )(*args)
+
+
+def back_kernel(
+    tok, mod, normed, proj, lsum, mgrad, rgrad, qkv, mg2,
+    tgrad_o, dqkv, qvec, mgt,
+    pgrad,
+):
+    length, width = tok.shape
+    low_lane = lax.broadcasted_iota(jnp.int32, (length, 128), 1) < HEAD_DIM
+    for p in range(HEADS // 2):
+        q2 = proj[:, 128 * p : 128 * (p + 1)]
+        k2 = proj[:, width + 128 * p : width + 128 * (p + 1)]
+        v2 = proj[:, 2 * width + 128 * p : 2 * width + 128 * (p + 1)]
+        m2 = mgrad[:, 128 * p : 128 * (p + 1)]
+        parts = []
+        for h in range(2):
+            mine = low_lane if h == 0 else jnp.logical_not(low_lane)
+            zero = jnp.zeros_like(q2)
+            s = dot_nt(jnp.where(mine, q2, zero), k2) * SCALE
+            prob = jnp.exp(s - lsum[:, 2 * p + h : 2 * p + h + 1])
+            pg = dot_nt(jnp.where(mine, m2, zero), v2)
+            inner = jnp.sum(prob * pg, axis=-1, keepdims=True)
+            sg = (prob * (pg - inner)).astype(B16)
+            parts.append(
+                (dot(sg, k2) * SCALE, dot_tn(sg, q2) * SCALE, dot_tn(prob.astype(B16), m2))
+            )
+        for i in range(3):
+            pgrad[:, i * width + 128 * p : i * width + 128 * (p + 1)] = jnp.where(
+                low_lane, parts[0][i], parts[1][i]
+            ).astype(B16)
+    ngrad = dot_nt(pgrad[...], qkv[...])
+    for i in range(3):
+        dqkv[:, i * width : (i + 1) * width] = dot_tn(
+            normed[...], pgrad[:, i * width : (i + 1) * width]
+        ).astype(B16)
+    per = width // 128
+    for i, k in enumerate((0, 2)):
+        row = jnp.sum(pgrad[:, k * width : (k + 1) * width].astype(F32), axis=0, keepdims=True)
+        for j in range(per):
+            qvec[i * per + j : i * per + j + 1, :] = row[:, 128 * j : 128 * (j + 1)]
+    for j in range(2 * per, qvec.shape[0]):
+        qvec[j : j + 1, :] = jnp.zeros((1, 128), F32)
+    n1, r1 = norm_parts(tok[...].astype(F32))
+    tgrad_o[...] = rgrad[...] + norm_back(ngrad * (1.0 + mod[1:2]), n1, r1)
+    rows = [
+        jnp.sum(ngrad, axis=0, keepdims=True),
+        jnp.sum(ngrad * n1, axis=0, keepdims=True),
+    ] + [mg2[i : i + 1, :] for i in range(2, 6)]
+    mgt[...] = jnp.zeros_like(mgt)
+    for i, row in enumerate(rows):
+        row = row.astype(B16).astype(F32)
+        for j in range(per):
+            mgt[i * per + j : i * per + j + 1, :] = row[:, 128 * j : 128 * (j + 1)]
+
+
+def back(*args):
+    tok, qkv = args[0], args[7]
+    length, width = tok.shape
+    return pl.pallas_call(
+        back_kernel,
+        out_shape=[
+            sds((length, width), F32),
+            sds(qkv.shape, B16),
+            sds((16, 128), F32),
+            sds((48, 128), F32),
+        ],
+        in_specs=[VM] * 9,
+        out_specs=[VM] * 4,
+        scratch_shapes=[pltpu.VMEM((length, 3 * width), B16)],
+        compiler_params=params(),
+        name="attention_back",
+    )(*args)
+
+
+PIECES = ((2, 0, 2, True), (3, 0, 1, False), (0, 0, 1, True), (2, 1, 2, False), (1, 0, 1, True))
+
+
+def add_into(target, source, lead):
+    count = 1
+    for n in lead:
+        count *= n
+
+    def body(i, carry):
+        at = []
+        rest = i
+        for n in reversed(lead):
+            at.append(lax.rem(rest, n))
+            rest = lax.div(rest, n)
+        at = tuple(reversed(at))
+        target[at] = (target[at].astype(F32) + source(at).astype(F32)).astype(B16)
+        return carry
+
+    lax.fori_loop(0, count, body, 0)
+
+
+class Reduce:
+    def __init__(self, grad, out, col, width, y_first, bufs, sems):
+        self.z, self.x, self.y, self.c = coords()
+        self.grad, self.out, self.width, self.y_first = grad, out, width, y_first
+        self.half = grad.shape[-1] // 2
+        self.col = col
+        self.cbuf, self.lbuf, self.ebuf, self.fbuf, self.zl, self.zr = bufs
+        self.one, self.zsem = sems
+
+    @staticmethod
+    def scratch(rows, width):
+        vm = lambda *lead: pltpu.VMEM(lead + (rows, width), B16)
+        return [
+            vm(NZ, NX, 2),
+            vm(NZ, NX, 2),
+            vm(NZ, 2),
+            vm(NZ),
+            vm(NZ),
+            vm(NZ),
+            pltpu.SemaphoreType.DMA((14,)),
+            pltpu.SemaphoreType.DMA((4, NZ)),
+        ]
+
+    def cols(self, c):
+        return pl.ds(pl.multiple_of(c * self.half + self.col, 128), self.width)
+
+    def core_copy(self):
+        return remote(
+            self.grad.at[:, :, :, :, self.cols(1 - self.c)],
+            self.cbuf,
+            self.one.at[0],
+            self.one.at[1],
+            dev(self.z, self.x, self.y, 1 - self.c),
+        )
+
+    def load(self):
+        return pltpu.make_async_copy(
+            self.grad.at[:, :, :, :, self.cols(self.c)], self.lbuf, self.one.at[2]
+        )
+
+    def copy1(self):
+        if self.y_first:
+            source, to = self.cbuf.at[:, :, 1 - self.y], dev(self.z, self.x, 1 - self.y, self.c)
+        else:
+            source, to = self.cbuf.at[:, 1 - self.x], dev(self.z, 1 - self.x, self.y, self.c)
+        return remote(source, self.ebuf, self.one.at[3], self.one.at[4], to)
+
+    def copy2(self):
+        if self.y_first:
+            source, to = self.ebuf.at[:, 1 - self.x], dev(self.z, 1 - self.x, self.y, self.c)
+        else:
+            source, to = self.ebuf.at[:, 1 - self.y], dev(self.z, self.x, 1 - self.y, self.c)
+        return remote(source, self.fbuf, self.one.at[5], self.one.at[6], to)
+
+    def zcopy(self, zb, side):
+        into = self.zl if side else self.zr
+        to = lax.rem(self.z + (1 if side else NZ - 1), NZ)
+        return remote(
+            self.fbuf.at[zb],
+            into.at[zb],
+            self.zsem.at[side, zb],
+            self.zsem.at[2 + side, zb],
+            dev(to, self.x, self.y, self.c),
+        )
+
+    def own(self):
+        return self.fbuf.at[self.z]
+
+    def place(self, y, c):
+        return self.out.at[y, :, self.cols(c)]
+
+    def keep(self):
+        return pltpu.make_async_copy(self.own(), self.place(self.y, self.c), self.one.at[7])
+
+    def give_y(self):
+        return remote(
+            self.own(), self.place(self.y, self.c), self.one.at[8], self.one.at[9],
+            dev(self.z, self.x, 1 - self.y, self.c),
+        )
+
+    def give_c(self):
+        return remote(
+            self.own(), self.place(self.y, self.c), self.one.at[10], self.one.at[11],
+            dev(self.z, self.x, self.y, 1 - self.c),
+        )
+
+    def pass_c(self):
+        here = self.place(1 - self.y, self.c)
+        return remote(
+            here, here, self.one.at[12], self.one.at[13], dev(self.z, self.x, self.y, 1 - self.c)
+        )
+
+    def absorb(self, zb, side):
+        into = self.zl if side else self.zr
+        has = self.z > 0 if side else self.z < NZ - 1
+
+        @pl.when(has)
+        def _():
+            self.zcopy(zb, side).wait_recv()
+            self.fbuf[zb] = (self.fbuf[zb].astype(F32) + into[zb].astype(F32)).astype(B16)
+
+    def stage(self, s):
+        if s == 0:
+            self.core_copy().wait_recv()
+            self.load().wait()
+            add_into(self.cbuf, lambda i: self.lbuf[i], (NZ, NX, 2))
+            self.copy1().start()
+        elif s == 1:
+            self.copy1().wait_recv()
+            if self.y_first:
+                add_into(self.ebuf, lambda i: self.cbuf[i[0], i[1], self.y], (NZ, NX))
+            else:
+                add_into(self.ebuf, lambda i: self.cbuf[i[0], self.x, i[1]], (NZ, 2))
+            self.copy2().start()
+        elif s == 2:
+            self.copy2().wait_recv()
+            side = self.x if self.y_first else self.y
+            add_into(self.fbuf, lambda i: self.ebuf[i[0], side], (NZ,))
+        if 2 <= s < 2 + NZ - 1:
+            k = NZ - 1 - (s - 2)
+            for side in (1, 0):
+                zb = self.z + k if side else self.z - k
+
+                @pl.when(zb < NZ if side else zb >= 0)
+                def _():
+                    self.absorb(zb, side)
+                    self.zcopy(zb, side).start()
+
+        if s == 2 + NZ - 1:
+            self.absorb(self.z, 1)
+            self.absorb(self.z, 0)
+            self.give_y().start()
+            self.give_c().start()
+            self.keep().start()
+        if s == 3 + NZ - 1:
+            self.give_y_in().wait_recv()
+            self.pass_c().start()
+        if s == 4 + NZ - 1:
+            self.keep().wait()
+            self.give_c_in().wait_recv()
+            self.pass_c_in().wait_recv()
+            self.core_copy().wait_send()
+            self.copy1().wait_send()
+            self.copy2().wait_send()
+            self.give_y().wait_send()
+            self.give_c().wait_send()
+            self.pass_c().wait_send()
+            for k in range(1, NZ):
+                for side in (1, 0):
+                    zb = self.z + k if side else self.z - k
+
+                    @pl.when(zb < NZ if side else zb >= 0)
+                    def _():
+                        self.zcopy(zb, side).wait_send()
+
+    def give_y_in(self):
+        return remote(
+            self.own(), self.place(1 - self.y, self.c), self.one.at[8], self.one.at[9],
+            dev(self.z, self.x, 1 - self.y, self.c),
+        )
+
+    def give_c_in(self):
+        return remote(
+            self.own(), self.place(self.y, 1 - self.c), self.one.at[10], self.one.at[11],
+            dev(self.z, self.x, self.y, 1 - self.c),
+        )
+
+    def pass_c_in(self):
+        here = self.place(1 - self.y, 1 - self.c)
+        return remote(
+            here, here, self.one.at[12], self.one.at[13], dev(self.z, self.x, self.y, 1 - self.c)
+        )
+
+    STAGES = 5 + NZ - 1
+
+
+def sums_kernel(*refs):
+    grads = refs[:4]
+    vecs, qvec, drouter, ebias, mgt, condt, ada = refs[4:11]
+    outs = refs[11:15]
+    small, esum, tiles, cgot = refs[15:19]
+    rest = list(refs[19:])
+    z, x, y, c = coords()
+    dp, ex = lax.axis_index("dp"), lax.axis_index("expert")
+    n = NZ * NX
+
+    barrier = pltpu.get_barrier_semaphore()
+
+    def peers(action):
+        for p in range(n):
+
+            @pl.when(p != dp)
+            def _():
+                action(p)
+
+    peers(lambda p: greet(barrier, (p, ex)))
+    mates = (dev(z, x, 1 - y, c), dev(z, x, y, 1 - c), dev(z, x, 1 - y, 1 - c))
+    for mate in mates:
+        greet(barrier, mate)
+    pl.semaphore_wait(barrier, n - 1 + 3)
+
+    plans = []
+    for matrix, part, share, y_first in PIECES:
+        grad = grads[matrix]
+        width = grad.shape[-1] // 2 // share
+        plans.append(
+            Reduce(grad, outs[matrix], part * width, width, y_first, rest[:6], rest[6:8])
+        )
+        rest = rest[8:]
+    ssum, sgot, zgot, esend, egot, mine, csend, sems, dsem, zsem, tsem = rest
+
+    for plan in plans:
+        plan.core_copy().start()
+        plan.load().start()
+
+    rows = vecs.shape[0]
+    ssum[0:rows, :] = vecs[...]
+    ssum[rows : rows + 16, :] = qvec[...]
+    per = drouter.shape[1] // 128
+    for b in range(per):
+        ssum[rows + 16 + 8 * b : rows + 24 + 8 * b, :] = drouter[:, 128 * b : 128 * (b + 1)]
+    hops = (dev(z, x, y, 1 - c), dev(z, x, 1 - y, c), dev(z, 1 - x, y, c))
+
+    def hop(i):
+        return remote(zgot.at[4 + i], sgot.at[i], sems.at[0, i], sems.at[1, i], hops[i])
+
+    def ehop():
+        return remote(esend.at[x], egot.at[z, x], sems.at[0, 3], sems.at[1, 3], hops[2])
+
+    def ehop_in():
+        return remote(esend.at[x], egot.at[z, 1 - x], sems.at[0, 3], sems.at[1, 3], hops[2])
+
+    mine[0:40, :] = mgt[0:40, :]
+    mine[40:48, :] = condt[...]
+
+    def tile(p, at):
+        return remote(mine, tiles.at[ex, at], dsem.at[0, p], dsem.at[1, at], (p, ex))
+
+    def spread(i, theirs=False):
+        e2 = 2 * (1 - y if i != 1 else y) + (1 - c if i != 0 else c)
+        rows = tiles.at[e2 if theirs else ex]
+        return remote(rows, rows, tsem.at[0, i], tsem.at[1, i], mates[i])
+
+    def cond_copy(p, at):
+        return remote(csend.at[p], cgot.at[at], dsem.at[2, p], dsem.at[3, at], (p, ex))
+
+    def zsum(zb, at):
+        return remote(ssum, zgot.at[at], zsem.at[0, zb], zsem.at[1, at], dev(zb, x, y, c))
+
+    def zexp(zb, at):
+        return remote(
+            egot.at[at], egot.at[at], zsem.at[2, zb], zsem.at[3, at], dev(zb, x, y, c)
+        )
+
+    def lines(action):
+        for zb in range(NZ):
+
+            @pl.when(zb != z)
+            def _():
+                action(zb)
+
+    def start_hop(i):
+        zgot[4 + i] = ssum[...]
+        hop(i).start()
+
+    def end_hop(i):
+        hop(i).wait()
+        ssum[...] = ssum[...] + sgot[i]
+
+    def small0():
+        start_hop(0)
+        esend[x] = ebias[...]
+        egot[z, x] = ebias[...]
+        ehop().start()
+        peers(lambda p: tile(p, dp).start())
+        tiles[ex, dp] = mine[...]
+
+    def small1():
+        end_hop(0)
+        start_hop(1)
+        peers(lambda p: tile(p, p).wait_recv())
+        for i in range(3):
+            spread(i).start()
+        acc = jnp.zeros((n, ada.shape[0]), F32)
+        for j in range(ada.shape[1] // 128):
+            acc = acc + dot_nt(tiles[ex, :, j, :].astype(B16), ada[:, 128 * j : 128 * (j + 1)])
+        csend[...] = jnp.zeros_like(csend)
+        csend[:, 0, 0 : ada.shape[0]] = acc
+        peers(lambda p: cond_copy(p, dp).start())
+        cgot[dp] = csend[dp]
+
+    def small2():
+        end_hop(1)
+        start_hop(2)
+        ehop().wait_send()
+        ehop_in().wait_recv()
+        lines(lambda zb: zexp(zb, z).start())
+
+    def small3():
+        end_hop(2)
+        zgot[z] = ssum[...]
+        lines(lambda zb: zsum(zb, z).start())
+
+    def small4():
+        lines(lambda zb: zexp(zb, zb).wait_recv())
+        lines(lambda zb: zsum(zb, zb).wait_recv())
+        total, etotal = zgot[0], egot[0]
+        for i in range(1, NZ):
+            total = total + zgot[i]
+            etotal = etotal + egot[i]
+        small[...] = total
+        esum[...] = etotal
+
+    def small5():
+        peers(lambda p: cond_copy(p, p).wait_recv())
+        for i in range(3):
+            spread(i, True).wait_recv()
+            spread(i).wait_send()
+        peers(lambda p: tile(p, p).wait_send())
+        peers(lambda p: cond_copy(p, p).wait_send())
+        lines(lambda zb: zexp(zb, zb).wait_send())
+        lines(lambda zb: zsum(zb, zb).wait_send())
+
+    steps = [small0, small1, small2, small3, small4, small5]
+    for t in range(Reduce.STAGES + len(plans) - 1):
+        for i, plan in enumerate(plans):
+            if 0 <= t - i < Reduce.STAGES:
+                plan.stage(t - i)
+        if t < len(steps):
+            steps[t]()
+
+
+def device_sums(grads, vecs, qvec, drouter, ebias, mgt, condt, ada):
+    n = NZ * NX
+    dma = pltpu.SemaphoreType.DMA
+    split = [g.reshape(NZ, NX, 2, g.shape[0] // (4 * NZ), g.shape[1]) for g in grads]
+    outs = [sds((2, g.shape[3], g.shape[4]), B16) for g in split]
+    rows = vecs.shape[0] + 16 + 8 * (drouter.shape[1] // 128)
+    scratch = []
+    for matrix, _, share, _ in PIECES:
+        g = split[matrix]
+        scratch += Reduce.scratch(g.shape[3], g.shape[4] // 2 // share)
+    vm = pltpu.VMEM
+    scratch += [
+        vm((rows, 128), F32),
+        vm((3, rows, 128), F32),
+        vm((NZ + 3, rows, 128), F32),
+        vm((2, 32, 128), F32),
+        vm((NZ, 2, 32, 128), F32),
+        vm((48, 128), F32),
+        vm((n, 8, 128), F32),
+        dma((2, 4)),
+        dma((4, n)),
+        dma((4, NZ)),
+        dma((2, 3)),
+    ]
+    out = pl.pallas_call(
+        sums_kernel,
+        out_shape=outs
+        + [
+            sds((rows, 128), F32),
+            sds((2, 32, 128), F32),
+            sds((4, n, 48, 128), F32),
+            sds((n, 8, 128), F32),
+        ],
+        in_specs=[HB] * 4 + [VM] * 7,
+        out_specs=[HB] * 4 + [VM] * 4,
+        scratch_shapes=scratch,
+        compiler_params=params(4),
+        name="device_sums",
+    )(*split, vecs, qvec, drouter, ebias, mgt, condt, ada)
+    return [o.reshape(-1, o.shape[2]).astype(F32) for o in out[:4]], out[4:]
+
+
+def on_block(
+    tokens, conditioning, routes, cotangent, ada_weight, ada_bias, qkv_weight, qv_bias, out_weight, out_bias,
+    shared_in, shared_in_bias, shared_out, shared_out_bias, router,
+    expert_in, expert_in_bias, expert_out, expert_out_bias,
+):
+    n = NZ * NX
+    dp = lax.axis_index("dp")
+    x = lax.rem(dp, NX)
+    width = tokens.shape[2]
+    hidden = shared_in.shape[1]
+    part = width // n
+    tok, cot, route = tokens[0], cotangent[0], routes[0]
+    cond_act, silu_back = jax.vjp(jax.nn.silu, conditioning.astype(F32))
+    cond_low = cond_act.astype(B16).astype(F32)
+
+    def rows_of(v, count):
+        v = v.astype(F32).reshape(-1)
+        return jnp.pad(v, (0, count * 128 - v.shape[0])).reshape(count, 128)
+
+    def wide(v):
+        return jnp.pad(v.astype(F32), ((0, 0), (0, 128 - part)))
+
+    pack = jnp.concatenate(
+        [
+            wide(qv_bias),
+            wide(out_bias[None]),
+            wide(shared_out_bias[None]),
+            rows_of(shared_in_bias, 4),
+            rows_of(ada_bias, 8),
+            rows_of(router, 8),
+            wide(cond_low.reshape(n, part)),
+        ],
+        axis=0,
+    )
+    mod_raw, packs, fulls = gather_dense(
+        ada_weight, pack, (qkv_weight, out_weight, shared_in, shared_out), (True, True, True, False)
+    )
+    qkv_full, out_full, sin_full, sout_full = fulls
+    bias = jnp.pad(packs[:, 0:4, :part].transpose(1, 0, 2).reshape(4, width), ((0, 4), (0, 0)))
+    sinb = packs[:, 4:7, :].reshape(1, hidden)
+    abias = packs[:, 8:16, :].reshape(n, -1)[:, : ada_bias.shape[0]].reshape(6, width)
+    abias = jnp.pad(abias, ((0, 2), (0, 0)))
+    router_full = packs[:, 16:24, :].reshape(n, -1)[:, : part * E].reshape(width, E)
+    router_full = jnp.pad(router_full, ((0, 0), (0, 128 - E))).astype(B16)
+
+    (normed, proj, lsum, mixed, att, resid, second, gates, place, sbuf, gbuf, mod) = front(
+        tok, cot, route, mod_raw, abias, qkv_full, out_full, bias, router_full
+    )
+    dwin, dwout, res, bgr, ebias = expert(
+        sbuf, gbuf, expert_in, expert_out, expert_in_bias.astype(F32), expert_out_bias.astype(F32)
+    )
+    line = [[NX * z + xx for z in range(NZ)] for xx in range(NX)]
+    turn = [(i, i // NX * NX + 1 - i % NX) for i in range(n)]
+
+    def over_z(grad):
+        mine = lax.psum_scatter(
+            grad, "dp", scatter_dimension=0, axis_index_groups=line, tiled=True
+        )
+        pair = mine.reshape(NX, -1, mine.shape[1])
+        keep = lax.dynamic_index_in_dim(pair, x, 0, keepdims=False)
+        give = lax.dynamic_index_in_dim(pair, 1 - x, 0, keepdims=False)
+        came = lax.ppermute(give, "dp", turn)
+        first = x == 0
+        return jnp.stack([jnp.where(first, keep, came), jnp.where(first, came, keep)]).astype(F32)
+
+    dwout_sum = over_z(dwout)
+    dwin_sum = over_z(dwin)
+    (output, rgrad, mgrad, dsin, dsout, dout, drouter, vecs, mg2) = middle(
+        res, bgr, second, resid, att, cot, route, mod, sin_full, sout_full, sinb, bias, router_full, gates, place,
+        mixed, out_full,
+    )
+    tgrad, dqkv, qvec, mgt = back(tok, mod, normed, proj, lsum, mgrad, rgrad, qkv_full, mg2)
+    condt = jnp.pad(cond_low.reshape(-1, 128), ((0, 2), (0, 0)))
+    dense, (small, esum, tiles, cgot) = device_sums(
+        (dqkv, dout, dsin, dsout), vecs, qvec, drouter, ebias, mgt, condt, ada_weight
+    )
+
+    def share(v, size):
+        return lax.dynamic_slice_in_dim(v.reshape(-1), dp * size, size, 0)
+
+    per = width // 128
+    base = hidden // 128
+    sinb_grad = share(small[:base], hidden // n)
+    soutb_grad = share(small[base : base + per], part)
+    outb_grad = share(small[base + per : base + 2 * per], part)
+    qvb_grad = jnp.stack(
+        [share(small[40 : 40 + per], part), share(small[40 + per : 40 + 2 * per], part)]
+    )
+    router_grad = small[56:].reshape(per, E, 128).transpose(0, 2, 1).reshape(width, E)
+    router_grad = lax.dynamic_slice_in_dim(router_grad, dp * part, part, 0)
+    ein_b = lax.dynamic_slice_in_dim(
+        esum[:, :base].reshape(2, hidden), dp * (hidden // n), hidden // n, 1
+    )
+    eout_b = lax.dynamic_slice_in_dim(
+        esum[:, base : base + per].reshape(2, width), dp * part, part, 1
+    )
+    images = tiles.shape[0] * n
+    mods = tiles[:, :, : 6 * per].reshape(images, 6 * width)
+    conds = lax.dynamic_slice_in_dim(
+        tiles[:, :, 40 : 40 + per].reshape(images, width), dp * part, part, 1
+    )
+    ada_grad = lax.dot_general(
+        conds.astype(B16), mods.astype(B16), (((0,), (0,)), ((), ())), preferred_element_type=F32
+    )
+    adab_grad = share(jnp.sum(mods, axis=0), ada_bias.shape[0])
+    cond_grad = silu_back(cgot[:, 0, :part].reshape(1, width))[0]
+    return (
+        output[None],
+        tgrad[None],
+        cond_grad,
+        ada_grad,
+        adab_grad,
+        dense[0],
+        qvb_grad,
+        dense[1],
+        outb_grad,
+        dense[2],
+        sinb_grad,
+        dense[3],
+        soutb_grad,
+        router_grad,
+        dwin_sum,
+        ein_b,
+        dwout_sum,
+        eout_b,
+    )
 
 
 def layer_norm(rows):
@@ -421,6 +1765,9 @@
         P("expert", "dp", None),
         P("expert", "dp"),
     )
+    body = on_device
+    if dict(mesh.shape) == {"dp": NZ * NX, "expert": 4}:
+        body = on_block
     return jax.shard_map(
-        on_device, mesh=mesh, in_specs=in_specs, out_specs=out_specs, check_vma=False
-    )
+        body, mesh=mesh, in_specs=in_specs, out_specs=out_specs, check_vma=False
+    )

time: 1520 us -> 439 us (0.29)
  waiting for transfers between devices: 969 us -> 16.8 us
  Pallas kernels: 0 us -> 358 us
  blocking collectives: 240 us -> 0 us
  matrix products: 131 us -> 1.69 us
  local copies, waits for them, and re-layouts: 80.1 us -> 29.4 us
  other arithmetic: 47.6 us -> 15.5 us
  starting transfers between devices: 18.9 us -> 2.43 us
    reduce_scatter x7 -> x2, waiting for transfers between devices: 713 us -> 0.01 us  [over_z(): lax.psum_scatter(grad, 'dp', scatter_dimension=0, axis_index_groups=line,...]
    pallas_call x0 -> x6, Pallas kernels: none -> 358 us  [the longest x1 156 us: device_sums(): pl.pallas_call(sums_kernel, out_shape=outs + [sds((rows, 128), F32), sds(...]
    all_gather x5 -> x0, waiting for transfers between devices: 155 us -> none  [the longest x1 60.9 us: on_device(): lax.all_gather(qkv_weight, 'dp', axis=0, tiled=True)]
    dot_general x29 -> x1, matrix products: 131 us -> 1.69 us  [on_block(): lax.dot_general(conds.astype(B16), mods.astype(B16), (((0,), (0,)), ((),...]
    unnamed x20 -> x2, waiting for transfers between devices: 101 us -> 0.53 us
    psum x1 -> x0, blocking collectives: 95.3 us -> none  [on_device(): lax.psum((dense_parts[0], dense_parts[1], dense_parts[2], dense_parts[3],...]
    all_gather x3 -> x0, blocking collectives: 75.1 us -> none  [the longest x1 26.4 us: on_device(): lax.all_gather(router, 'dp', axis=0, tiled=True)]
    unnamed x2 -> x0, blocking collectives: 69.6 us -> none
  transfers between devices with their start and end apart: 20 -> 4, of which waited for: 14 -> 2; matrix products, arithmetic and copies ran while one was open for 15% -> 7% of each run, Pallas kernels for 0% -> 47%
where the time goes in v1:
time: 439 us; the launch traced here: 438 us
  Pallas kernels  358 us (82%)
  local copies, waits for them, and re-layouts  29.4 us (7%)
  waiting for transfers between devices  16.8 us (4%)
  other arithmetic  15.5 us (4%)
  between operations  14.2 us (3%)
    pallas_call x1, Pallas kernels, device_sums(): pl.pallas_call(sums_kernel, out_shape=outs + [sds((rows, 128), F32), sds(...  156 us
    pallas_call x1, Pallas kernels, gather_dense(): pl.pallas_call(functools.partial(gather_kernel, splits), out_shape=[sds((...  88.9 us
    pallas_call x1, Pallas kernels, expert(): pl.pallas_call(expert_kernel, out_shape=[sds((width, hidden), B16), sds((...  54 us
    pallas_call x1, Pallas kernels, middle(): pl.pallas_call(middle_kernel, out_shape=[sds((length, width), B16), sds((...  38.5 us
    ppermute x2, waiting for transfers between devices, over_z(): came = lax.ppermute(give, 'dp', turn)  16.3 us
    pallas_call x1, Pallas kernels, back(): pl.pallas_call(back_kernel, out_shape=[sds((length, width), F32), sds(qkv...  12.1 us
    pallas_call x1, Pallas kernels, front(): pl.pallas_call(front_kernel, out_shape=[sds((length, width), B16), sds((l...  8.93 us
  transfers between devices with their start and end apart: 4, of which 2 were waited for; matrix products, arithmetic and copies ran while one was open for 7% of the time, Pallas kernels for 47%

profile of v1, /device:TPU:0, one launch (start us, length us, event | category | flops | bytes accessed | tf_op | source)
XLA Modules:
  0.0 438.3 jit_solution(16933590614649689987)
XLA Ops:
  7.2 0.7 convert_reduce_fusion
  8.0 0.8 copy.40
  8.9 0.7 bitcast_convert_fusion.6
  9.6 0.7 pad_convert_fusion.2
  10.3 0.7 bitcast_convert_fusion.4
  11.0 0.7 pad_convert_fusion
  11.6 2.4 concatenate.3.refs_1_
  14.0 88.9 %gather_dense.1 = (f32[8,768]{1,0:T(8,128)}, f32[8,32,128]{2,1,0:T(8,128)}, bf16[768,2304]{1,0:T(8,128)(2,1)}, bf16[768,768]{1,0:T(8,128)(2,1)}, bf16[768,3072]{1,0:T(8,128)(2,1)}, /*index=5*/bf16[3072,768]{1,0:T(8,128)(2,1)}) custom-call(bf16[96,4608]{1,0:T(8,128)(2,1)} %refs_10_.1, f32[32,128]{1,0:T(8,128)} %concatenate.3.refs_1_, ...), custom_call_target="tpu_custom_call" | custom-call | tf_op jit(solution)/shard_map/gather_dense/pallas_call | solution.py:376
  102.9 0.8 fusion.8
  103.7 0.8 slice_bitcast_fusion.4
  104.5 0.8 slice_bitcast_fusion.1
  106.9 0.8 copy.39
  108.9 0.7 pad.68.router
  109.6 8.9 %attention_front.1 = (bf16[256,768]{1,0:T(8,128)(2,1)}, bf16[256,2304]{1,0:T(8,128)(2,1)}, f32[256,128]{1,0:T(8,128)}, bf16[256,768]{1,0:T(8,128)(2,1)}, f32[256...) custom-call(bf16[256,768]{1,0:T(8,128)(2,1)} %bitcast.121, ...), custom_call_target="tpu_custom_call" | custom-call | tf_op jit(solution)/shard_map/attention_front/pallas_call | solution.py:471
  118.6 54.0 %routed_expert.1 = (bf16[768,3072]{1,0:T(8,128)(2,1)}, bf16[3072,768]{1,0:T(8,128)(2,1)}, bf16[640,768]{1,0:T(8,128)(2,1)}, bf16[640,768]{1,0:T(8,128)(2,1)}, f32[32,128]{1,0:T(8,128)}) custom-call(bf16[640,768]{1,0:T(8,128)(2,1)} %get-tuple-element.66.sbuf, bf16[640,768]{1,0:T(8,128)(2,1)} %get-tuple-element.67.gbuf, bf16[2,768,3072]{2,1,0:T(8,128)(2,1)} %win_h.1, ...), custom_call_target="tpu_custom_call" | custom-call | tf_op jit(solution)/shard_map/routed_expert/pallas_call | solution.py:615
  173.4 0.8 slice.58
  175.3 38.5 %shared_expert_combine.1 = (bf16[256,768]{1,0:T(8,128)(2,1)}, f32[256,768]{1,0:T(8,128)}, bf16[256,768]{1,0:T(8,128)(2,1)}, bf16[768,3072]{1,0:T(8,128)(2,1)}, b...) custom-call(bf16[640,768]{1,0:T(8,128)(2,1)} %get-tuple-element.68.r, ...), custom_call_target="tpu_custom_call" | custom-call | tf_op jit(solution)/shard_map/shared_expert_combine/pallas_call | solution.py:733
  213.8 12.1 %attention_back.1 = (f32[256,768]{1,0:T(8,128)}, bf16[768,2304]{1,0:T(8,128)(2,1)}, f32[16,128]{1,0:T(8,128)}, f32[48,128]{1,0:T(8,128)}) custom-call(bf16[256,768]{1,0:T(8,128)(2,1)} %bitcast.122, f32[8,768]{1,0:T(8,128)} %get-tuple-element.73.mod, bf16[256,768]{1,0:T(8,128)(2,1)} %get-tuple-element.80.normed, bf16[256,2304]{1,0:T(8,128)(2,1)} %get-tuple-element.81.proj, ...), custom_call_target="tpu_custom_call" | custom-call | tf_op jit(solution)/shard_map/attention_back/pallas_call | solution.py:817
  225.9 155.8 %device_sums.1 = (bf16[2,48,2304]{2,1,0:T(8,128)(2,1)}, bf16[2,48,768]{2,1,0:T(8,128)(2,1)}, bf16[2,48,3072]{2,1,0:T(8,128)(2,1)}, bf16[2,192,768]{2,1,0:T(8,128...) custom-call(bf16[4,2,2,48,2304]{4,3,2,1,0:T(8,128)(2,1)} %bitcast.118, ...), custom_call_target="tpu_custom_call" | custom-call | tf_op jit(solution)/shard_map/device_sums/pallas_call | solution.py:1210
  381.7 1.0 slice_bitcast_fusion
  382.8 0.7 slice_bitcast_fusion.2
  383.5 0.7 slice_bitcast_fusion.6
  384.2 0.8 slice_reduce_fusion.1
  385.1 1.4 slice_bitcast_fusion.7
  387.0 0.6 constant_dynamic-slice_fusion
  388.2 1.8 slice_reduce_fusion
  390.6 0.7 slice_bitcast_fusion.5
  391.3 1.3 slice_bitcast_fusion.3
  392.6 0.7 bitcast_convert_fusion.3
  393.4 1.1 fusion.4
  394.5 1.1 bitcast_convert_fusion
  395.7 1.7 fusion.5
  397.4 1.2 bitcast_convert_fusion.1
  398.5 1.0 bitcast_convert_fusion.2
  399.5 1.2 dynamic-slice_bitcast_fusion
  400.7 0.7 collective-permute-start.1
  402.0 1.1 dynamic-slice_bitcast_fusion.1
  403.1 1.5 collective-permute-start
  404.6 1.2 pad_maximum_fusion
  405.8 1.3 dynamic_slice.48
  407.7 0.7 dynamic_slice.49
  408.3 1.4 dynamic_slice.45
  409.7 1.4 constant_dynamic-slice_fusion.2
  411.0 5.9 %collective-permute-done.1 = bf16[384,768]{1,0:T(8,128)(2,1)S(1)} collective-permute-done((bf16[384,768]{1,0:T(8,128)(2,1)S(1)}, bf16[384,768]{1,0:T(8,128)(2,1)S(1)}, u32[]{:S(2)}, u32[]{:S(2)}) %collective-permute-start.1) | collective-permute-done | bytes 589856 | tf_op jit(solution)/shard_map/ppermute | solution.py:1289
  417.0 1.6 maximum_convert_fusion.1
  418.6 10.4 %collective-permute-done = bf16[96,3072]{1,0:T(8,128)(2,1)S(1)} collective-permute-done((bf16[96,3072]{1,0:T(8,128)(2,1)S(1)}, bf16[96,3072]{1,0:T(8,128)(2,1)S(1)}, u32[]{:S(2)}, u32[]{:S(2)}) %collective-permute-start) | collective-permute-done | bytes 589856 | tf_op jit(solution)/shard_map/ppermute | solution.py:1289
  429.1 1.6 maximum_convert_fusion
  430.7 0.7 copy.63
  (58 shorter events, 8.3 us)
Async XLA Ops:
  7.2 392.3 %reduce-scatter.5.cloned.1.call-start = ((), (), s32[]{:S(2)}) async-start(), calls=%async_computation.3 | async-start | bytes 5898240 | tf_op jit(solution)/shard_map/reduce_scatter | solution.py:1283
  14.0 92.9 %copy-start.10 = (s32[1,256,2]{1,2,0:T(2,128)S(1)}, s32[1,256,2]{1,2,0:T(2,128)}, u32[]{:S(2)}) copy-start(s32[1,256,2]{1,2,0:T(2,128)} %param.21) | copy-start | bytes 6148
  14.0 93.7 %copy-start.7 = (bf16[2,3072]{1,0:T(2,128)(2,1)S(1)}, bf16[2,3072]{1,0:T(2,128)(2,1)}, u32[]{:S(2)}) copy-start(bf16[2,3072]{1,0:T(2,128)(2,1)} %param.35) | copy-start | bytes 36868
  14.0 94.3 %copy-start.9 = (bf16[2,768]{1,0:T(2,128)(2,1)S(1)}, bf16[2,768]{1,0:T(2,128)(2,1)}, u32[]{:S(2)}) copy-start(bf16[2,768]{1,0:T(2,128)(2,1)} %param.37) | copy-start | bytes 9220
  172.6 229.4 %reduce-scatter.3.cloned.1.call-start = ((), (), s32[]{:S(2)}) async-start(), calls=%async_computation.2 | async-start | bytes 5898240 | tf_op jit(solution)/shard_map/reduce_scatter | solution.py:1283
  225.9 164.1 %copy-start.8 = (bf16[1,768]{1,0:T(2,128)(2,1)S(1)}, bf16[1,768]{1,0:T(2,128)(2,1)}, u32[]{:S(2)}) copy-start(bf16[1,768]{1,0:T(2,128)(2,1)} %param.20) | copy-start | bytes 4612
  381.7 10.9 %copy-start.6 = (bf16[2,48,768]{2,1,0:T(8,128)(2,1)S(1)}, bf16[2,48,768]{2,1,0:T(8,128)(2,1)}, u32[]{:S(2)}) copy-start(bf16[2,48,768]{2,1,0:T(8,128)(2,1)} %get-tuple-element.100) | copy-start | bytes 442372
  381.7 12.8 %copy-start.3 = (bf16[2,192,768]{2,1,0:T(8,128)(2,1)S(1)}, bf16[2,192,768]{2,1,0:T(8,128)(2,1)}, u32[]{:S(2)}) copy-start(bf16[2,192,768]{2,1,0:T(8,128)(2,1)} %get-tuple-element.102) | copy-start | bytes 1769476
  395.7 1.7 copy-start.2
  397.4 1.2 copy-start.4
  399.5 17.4 %copy-start.1 = (bf16[768,768]{1,0:T(8,128)(2,1)S(1)}, bf16[768,768]{1,0:T(8,128)(2,1)}, u32[]{:S(2)}) copy-start(bf16[768,768]{1,0:T(8,128)(2,1)} %reduce-scatter.5.cloned.1.call-done) | copy-start | bytes 3538948
  400.7 16.2 %collective-permute-start.1 = (bf16[384,768]{1,0:T(8,128)(2,1)S(1)}, bf16[384,768]{1,0:T(8,128)(2,1)S(1)}, u32[]{:S(2)}, u32[]{:S(2)}) collective-permute-start(bf16[384,768]{1,0:T(8,128)(2,1)S(1)} %dynamic-slice_bitcast_fusion), channel_id=1, source_target_pairs={{0,4},{4,0},{8,12},{12,8},{16,20},{20,16},{24,28},{28,24},{1,5},{5... | collective-permute-start | bytes 1769480 | tf_op jit(solution)/shard_map/ppermute | solution.py:1289
  402.0 2.6 copy-start.11
  403.1 25.9 %collective-permute-start = (bf16[96,3072]{1,0:T(8,128)(2,1)S(1)}, bf16[96,3072]{1,0:T(8,128)(2,1)S(1)}, u32[]{:S(2)}, u32[]{:S(2)}) collective-permute-start(bf16[96,3072]{1,0:T(8,128)(2,1)S(1)} %dynamic-slice_bitcast_fusion.1), channel_id=1, source_target_pairs={{0,4},{4,0},{8,12},{12,8},{16,20},{20,16},{24,28},{28,24},{1,5},{5... | collective-permute-start | bytes 1769480 | tf_op jit(solution)/shard_map/ppermute | solution.py:1289
  417.0 12.0 %copy-start = (bf16[192,3072]{1,0:T(8,128)(2,1)S(1)}, bf16[192,3072]{1,0:T(8,128)(2,1)}, u32[]{:S(2)}) copy-start(bf16[192,3072]{1,0:T(8,128)(2,1)} %reduce-scatter.3.cloned.1.call-done) | copy-start | bytes 3538948
  429.1 1.6 copy-start.5
Sparse Core Ops, SparseCore 0:
  172.7 86.9 reduce-scatter.4
  262.0 118.6 reduce-scatter.2

commit v2 on v1

--- a/solution.py
+++ b/solution.py
@@ -283,54 +283,246 @@
         self.xcopy(m, self.z, True).wait_send()
         self.local(m).wait()
 
-    def run(self, mats):
-        for step in range(NZ):
-            for m in mats:
-                if step:
-                    self.take_z(m, step)
-                self.take_x(m, step)
-            if step:
-                for m in mats:
-                    self.take_y(m, step - 1)
-        for m in mats:
-            self.take_y(m, NZ - 1)
-        for m in mats:
-            self.finish(m)
-
-
-def gather_kernel(splits, *refs):
-    count = len(splits)
-    ada, pack = refs[:2]
-    shards = refs[2 : 2 + count]
-    rest = refs[2 + count :]
-    mod_ref, packs = rest[:2]
-    fulls = rest[2 : 2 + count]
-    sent, got, s1, r1, s2, r2 = rest[2 + count : 8 + count]
-    plan = Gather(shards, fulls, splits, rest[8 + count :])
+
+class Column:
+    def __init__(self, shard, column, send, recv, local):
+        self.z, self.x, self.y, self.c = coords()
+        self.shard, self.column, self.send, self.recv, self.local = shard, column, send, recv, local
+
+    def block(self, zb):
+        rows = self.shard.shape[0]
+        return self.column.at[pl.ds(pl.multiple_of(zb * rows, 16), rows), :]
+
+    def own(self):
+        width = self.shard.shape[1] // 2
+        return self.shard.at[:, pl.ds(pl.multiple_of(self.c * width, 128), width)]
+
+    def copy(self, zb, side, mine=False):
+        here = self.block(zb)
+        to = lax.rem(self.z + (1 if side else NZ - 1), NZ)
+        return remote(
+            self.own() if mine else here,
+            here,
+            self.send.at[side, zb],
+            self.recv.at[zb],
+            dev(to, self.x, self.y, self.c),
+        )
+
+    def keep(self):
+        return pltpu.make_async_copy(self.own(), self.block(self.z), self.local.at[0])
+
+    def more(self, side):
+        return self.z + 1 < NZ if side else self.z - 1 >= 0
+
+    def blocks(self, step):
+        return [(self.z - step, self.z - step >= 0, 1), (self.z + step, self.z + step < NZ, 0)]
+
+    def begin(self):
+        for side in (1, 0):
+
+            @pl.when(self.more(side))
+            def _():
+                self.copy(self.z, side, True).start()
+
+        self.keep().start()
+
+    def take(self, step):
+        for zb, exists, side in self.blocks(step):
+
+            @pl.when(exists)
+            def _():
+                self.copy(zb, side).wait_recv()
+                if step < NZ - 1:
+
+                    @pl.when(self.more(side))
+                    def _():
+                        self.copy(zb, side).start()
+
+    def finish(self):
+        for side in (1, 0):
+
+            @pl.when(self.more(side))
+            def _():
+                self.copy(self.z, side, True).wait_send()
+
+        for step in range(1, NZ - 1):
+            for zb, exists, side in self.blocks(step):
+
+                @pl.when(jnp.logical_and(exists, self.more(side)))
+                def _():
+                    self.copy(zb, side).wait_send()
+
+        self.keep().wait()
+
+
+class Spread:
+    def __init__(self, column, full, xs, xr, ys, yr, cs, cr, local):
+        self.z, self.x, self.y, self.c = coords()
+        self.column, self.full, self.local = column, full, local
+        self.xs, self.xr, self.ys, self.yr, self.cs, self.cr = xs, xr, ys, yr, cs, cr
+
+    @staticmethod
+    def semaphores():
+        dma = pltpu.SemaphoreType.DMA
+        return [dma((NZ,))] * 4 + [dma((3, NZ))] * 2 + [dma((NZ,))]
+
+    def cols(self, c):
+        width = self.full.shape[3] // 2
+        return pl.ds(pl.multiple_of(c * width, 128), width)
+
+    def half(self, y):
+        rows = self.full.shape[2] // 2
+        return pl.ds(pl.multiple_of(y * rows, 16), rows)
+
+    def source(self, zb):
+        rows = self.full.shape[2]
+        return self.column.at[zb * rows : (zb + 1) * rows, :]
+
+    def source_half(self, zb):
+        rows = self.full.shape[2]
+        start = zb * rows + self.y * (rows // 2)
+        return self.column.at[pl.ds(pl.multiple_of(start, 16), rows // 2), :]
+
+    def xcopy(self, zb, came=False):
+        at = self.full.at[zb, 1 - self.x if came else self.x, self.half(self.y), self.cols(self.c)]
+        return remote(
+            self.source_half(zb), at, self.xs.at[zb], self.xr.at[zb],
+            dev(self.z, 1 - self.x, self.y, self.c),
+        )
+
+    def ycopy(self, zb, came=False):
+        at = self.full.at[zb, 1 - self.x, self.half(1 - self.y if came else self.y), self.cols(self.c)]
+        return remote(
+            at, at, self.ys.at[zb], self.yr.at[zb], dev(self.z, self.x, 1 - self.y, self.c)
+        )
+
+    def ccopy(self, kind, zb, came=False):
+        cols = self.cols(1 - self.c if came else self.c)
+        if kind == 0:
+            at = self.full.at[zb, self.x, :, cols]
+        else:
+            at = self.full.at[zb, 1 - self.x, self.half(self.y if kind == 1 else 1 - self.y), cols]
+        return remote(
+            self.source(zb) if kind == 0 else at, at, self.cs.at[kind, zb], self.cr.at[kind, zb],
+            dev(self.z, self.x, self.y, 1 - self.c),
+        )
+
+    def keep(self, zb):
+        return pltpu.make_async_copy(
+            self.source(zb), self.full.at[zb, self.x, :, self.cols(self.c)], self.local.at[zb]
+        )
+
+    def begin(self):
+        for zb in range(NZ):
+            self.xcopy(zb).start()
+
+    def near(self):
+        for zb in range(NZ):
+            self.ccopy(0, zb).start()
+            self.keep(zb).start()
+
+    def take_x(self):
+        for zb in range(NZ):
+            self.xcopy(zb, True).wait_recv()
+            self.ycopy(zb).start()
+            self.ccopy(1, zb).start()
+
+    def take_y(self):
+        for zb in range(NZ):
+            self.ycopy(zb, True).wait_recv()
+            self.ccopy(2, zb).start()
+
+    def finish(self):
+        for zb in range(NZ):
+            for kind in range(3):
+                self.ccopy(kind, zb, True).wait_recv()
+            self.keep(zb).wait()
+
+    def close(self):
+        for zb in range(NZ):
+            self.xcopy(zb).wait_send()
+            self.ycopy(zb).wait_send()
+            for kind in range(3):
+                self.ccopy(kind, zb).wait_send()
+
+
+def choose_rows(place, slots):
+    return place == lax.broadcasted_iota(jnp.int32, (place.shape[0], slots), 1)
+
+
+def plane_peer(k):
+    z, x, y, c = coords()
+    xt = 1 - x if k & 1 else x
+    ct = 1 - c if k & 2 else c
+    yt = 1 - y if k & 4 else y
+    return dev(z, xt, yt, ct), 4 * yt + 2 * ct + xt
+
+
+def plane_rank():
+    _, x, y, c = coords()
+    return 4 * y + 2 * c + x
+
+
+def slot_rows(ref, rank):
+    return ref.at[pl.ds(pl.multiple_of(rank * CAP, 16), CAP), :]
+
+
+class PlaneExchange:
+    ORDER = (7, 5, 6, 4, 3, 1, 2)
+
+    def __init__(self, source, target, send, recv):
+        self.source, self.target, self.send, self.recv = source, target, send, recv
+
+    def copy(self, k, into=None):
+        peer, other = plane_peer(k)
+        return remote(
+            slot_rows(self.source, other),
+            slot_rows(self.target, plane_rank() if into is None else other),
+            self.send.at[k],
+            self.recv.at[k],
+            peer,
+        )
+
+    def start(self):
+        for k in self.ORDER:
+            self.copy(k).start()
+        mine = pl.ds(pl.multiple_of(plane_rank() * CAP, 16), CAP)
+        self.target[mine, :] = self.source[mine, :]
+
+    def wait_in(self):
+        for k in self.ORDER:
+            self.copy(k, True).wait_recv()
+
+    def wait_out(self):
+        for k in self.ORDER:
+            self.copy(k).wait_send()
+
+
+CHUNK = 512
+
+
+def lead_kernel(
+    tok, cot, routes, cond, ada, adab, qvb, outb, soutb, sinb_s, router_s, bin_r, bout_r,
+    qkv_s, out_s, sin_s, sout_s, win_h, wout_h,
+    normed_o, proj_o, lsum_o, mixed_o, att_o, resid_o, second_o, gates_o, place_o, mod_o, bias_o, sinb_o, rt_o,
+    condt_o, rows, grads, res_o, qkv_o, outw_o, sin_o, sout_o, slopes_o, dwout_o,
+    pack, packs, sent, got, qkv, outw, sbuf, gbuf, win, wout, dwout, lows, slopes, acc,
+    s1, r1, s2, r2, ds0, dr0, ds1, dr1, wsem, osem, *gsems,
+):
+    z, x, y, c = coords()
     dp, ex = lax.axis_index("dp"), lax.axis_index("expert")
     n = NZ * NX
-    barrier = pltpu.get_barrier_semaphore()
-    for p in range(n):
-
-        @pl.when(p != dp)
-        def _():
-            greet(barrier, (p, ex))
-
-    greet(barrier, dev(plan.z, plan.x, 1 - plan.y, plan.c))
-    greet(barrier, dev(plan.z, plan.x, plan.y, 1 - plan.c))
-    pl.semaphore_wait(barrier, n + 1)
-
-    def first(p):
-        return remote(pack, packs.at[dp], s1.at[p], r1.at[dp], (p, ex))
-
-    def first_from(p):
-        return remote(pack, packs.at[p], s1.at[p], r1.at[p], (p, ex))
-
-    def second(p):
-        return remote(sent.at[p], got.at[dp], s2.at[p], r2.at[dp], (p, ex))
-
-    def second_from(p):
-        return remote(sent.at[p], got.at[p], s2.at[p], r2.at[p], (p, ex))
+    length, width = tok.shape
+    hidden = win.shape[1]
+    part = width // n
+    per = width // 128
+    lead = Gather((qkv_s, out_s), (qkv, outw), (True, False), gsems[:-6])
+    later = (Column(sin_s, sin_o, *gsems[-6:-3]), Column(sout_s, sout_o, *gsems[-3:]))
+
+    loads = [
+        pltpu.make_async_copy(win_h.at[x], win, wsem.at[0]),
+        pltpu.make_async_copy(wout_h.at[x], wout, wsem.at[1]),
+    ]
 
     def peers(action):
         for p in range(n):
@@ -339,82 +531,117 @@
             def _():
                 action(p)
 
-    peers(lambda p: first(p).start())
-    for m in range(count):
-        plan.begin(m)
+    barrier = pltpu.get_barrier_semaphore()
+    peers(lambda p: greet(barrier, (p, ex)))
+    for k in range(2, E):
+        greet(barrier, plane_peer(k)[0])
+
+    pack[...] = jnp.zeros_like(pack)
+    pack[0:2, 0:part] = qvb[...].astype(F32)
+    pack[2:3, 0:part] = outb[...].astype(F32)
+    pack[3:4, 0:part] = soutb[...].astype(F32)
+    for j in range(hidden // n // 128):
+        pack[4 + j : 5 + j, :] = sinb_s[:, 128 * j : 128 * (j + 1)].astype(F32)
+    long = adab.shape[1]
+    for j in range(-(-long // 128)):
+        size = min(128, long - 128 * j)
+        pack[8 + j : 9 + j, 0:size] = adab[:, 128 * j : 128 * j + size].astype(F32)
+    pack[16:24, 0:part] = router_s[...].astype(F32)
+    cv = cond[...].astype(F32)
+    cond_low = (cv / (1.0 + jnp.exp(-cv))).astype(B16).astype(F32)
+    for p in range(n):
+        pack[24 + p : 25 + p, 0:part] = cond_low[:, part * p : part * (p + 1)]
+    condt_o[...] = jnp.zeros_like(condt_o)
+    for j in range(per):
+        condt_o[j : j + 1, :] = cond_low[:, 128 * j : 128 * (j + 1)]
+
+    pl.semaphore_wait(barrier, n - 1 + E - 2)
+
+    def first(p, at):
+        return remote(pack, packs.at[at], s1.at[p], r1.at[at], (p, ex))
+
+    def second_hop(p, at):
+        return remote(sent.at[p], got.at[at], s2.at[p], r2.at[at], (p, ex))
+
+    peers(lambda p: first(p, dp).start())
+    lead.begin(0)
+    lead.begin(1)
+    for column in later:
+        column.begin()
+    for load in loads:
+        load.start()
     packs[dp] = pack[...]
-    peers(lambda p: first_from(p).wait_recv())
-    rows = jnp.concatenate([packs[p, pl.ds(24 + dp, 1), :] for p in range(n)], axis=0)
-    width = ada.shape[0]
-    partial = dot(rows[:, :width].astype(B16), ada[...])
+    peers(lambda p: first(p, p).wait_recv())
+    cond_rows = jnp.concatenate([packs[p, pl.ds(24 + dp, 1), :] for p in range(n)], axis=0)
+    partial = dot(cond_rows[:, :part].astype(B16), ada[...])
     for j in range(partial.shape[1] // 128):
         sent[:, j, :] = partial[:, 128 * j : 128 * (j + 1)]
-    peers(lambda p: second(p).start())
+    peers(lambda p: second_hop(p, dp).start())
     got[dp] = sent[dp]
 
-    plan.run(range(count))
-
-    peers(lambda p: second_from(p).wait_recv())
+    both_mats = (0, 1)
+
+    def step_of(plan, step):
+        for m in both_mats:
+            if step:
+                plan.take_z(m, step)
+            plan.take_x(m, step)
+        if step:
+            for m in both_mats:
+                plan.take_y(m, step - 1)
+
+    for step in range(NZ):
+        step_of(lead, step)
+
+    bias_o[...] = jnp.zeros_like(bias_o)
+    for p in range(n):
+        bias_o[0:4, part * p : part * (p + 1)] = packs[p, 0:4, 0:part]
+        rt_o[:, part * p : part * (p + 1)] = packs[p, 16:24, 0:part]
+        for j in range(hidden // n // 128):
+            at = hidden // n * p + 128 * j
+            sinb_o[:, at : at + 128] = packs[p, 4 + j : 5 + j, :]
+    peers(lambda p: second_hop(p, p).wait_recv())
     total = got[0]
     for p in range(1, n):
         total = total + got[p]
-    per = mod_ref.shape[1] // 128
-    mod_ref[...] = jnp.zeros_like(mod_ref)
+    mod_o[...] = jnp.zeros_like(mod_o)
     for i in range(6):
         for b in range(per):
-            mod_ref[i : i + 1, 128 * b : 128 * (b + 1)] = total[per * i + b : per * i + b + 1, :]
-    peers(lambda p: first(p).wait_send())
-    peers(lambda p: second(p).wait_send())
-
-
-def gather_dense(ada, pack, shards, splits):
-    n = NZ * NX
-    dma = pltpu.SemaphoreType.DMA
-    tiles = ada.shape[1] // 128
-    tiles = (tiles + 7) // 8 * 8
-    fulls = [sds((n * s.shape[0], s.shape[1]), s.dtype) for s in shards]
-    out = pl.pallas_call(
-        functools.partial(gather_kernel, splits),
-        out_shape=[sds((8, ada.shape[1] // 6), F32), sds((n,) + pack.shape, F32)] + fulls,
-        in_specs=[VM, VM] + [HB] * len(shards),
-        out_specs=[VM, VM] + [HB] * len(shards),
-        scratch_shapes=[
-            pltpu.VMEM((n, tiles, 128), F32),
-            pltpu.VMEM((n, tiles, 128), F32),
-            dma((n,)),
-            dma((n,)),
-            dma((n,)),
-            dma((n,)),
-        ]
-        + Gather.semaphores(len(shards)),
-        compiler_params=params(1),
-        name="gather_dense",
-    )(ada, pack, *shards)
-    return out[0], out[1], out[2:]
-
-
-def choose_rows(place, slots):
-    return place == lax.broadcasted_iota(jnp.int32, (place.shape[0], slots), 1)
-
-
-def front_kernel(
-    tok, cot, routes, mod_in, abias, qkv, outw, bias, router,
-    normed_o, proj_o, lsum_o, mixed_o, att_o, resid_o, second_o, gates_o, place_o, sbuf_o, gbuf_o, mod_o,
-):
-    length, width = tok.shape
-    mod = mod_in[...] + abias[...]
-    mod_o[...] = mod
+            mod_o[i : i + 1, 128 * b : 128 * (b + 1)] = total[per * i + b : per * i + b + 1, :]
+    unit = 64
+    for p in range(n):
+        for u in range(long // unit):
+            at = long * p + unit * u
+            i, b = at // width, at % width
+            mod_o[i : i + 1, b : b + unit] += packs[
+                p, 8 + unit * u // 128 : 9 + unit * u // 128, unit * u % 128 : unit * u % 128 + unit
+            ]
+
+    mod = mod_o[...]
     source = tok[...].astype(F32)
     n1, _ = norm_parts(source)
     normed = (n1 * (1.0 + mod[1:2]) + mod[0:1]).astype(B16)
     normed_o[...] = normed
+    for m in both_mats:
+        lead.take_y(m, NZ - 1)
+    for m in both_mats:
+        lead.finish(m)
+    for column in later:
+        column.take(1)
+    keep = [
+        pltpu.make_async_copy(qkv, qkv_o, wsem.at[2]),
+        pltpu.make_async_copy(outw, outw_o, wsem.at[3]),
+    ]
+    for copy in keep:
+        copy.start()
+
     for k in range(3):
-        part = dot(normed, qkv[:, k * width : (k + 1) * width])
+        part_k = dot(normed, qkv[:, k * width : (k + 1) * width])
         if k != 1:
-            part = part + bias[k // 2 : k // 2 + 1, :]
-        proj_o[:, k * width : (k + 1) * width] = part.astype(B16)
-    low_lane = lax.broadcasted_iota(jnp.int32, (length, 128), 1) < HEAD_DIM
+            part_k = part_k + bias_o[k // 2 : k // 2 + 1, :]
+        proj_o[:, k * width : (k + 1) * width] = part_k.astype(B16)
     lane = lax.broadcasted_iota(jnp.int32, (length, 128), 1)
+    low_lane = lane < HEAD_DIM
     lsum = jnp.zeros((length, 128), F32)
     for p in range(HEADS // 2):
         q2 = proj_o[:, 128 * p : 128 * (p + 1)]
@@ -426,25 +653,28 @@
             s = dot_nt(jnp.where(mine, q2, jnp.zeros_like(q2)), k2) * SCALE
             peak = jnp.max(s, axis=-1, keepdims=True)
             e = jnp.exp(s - peak)
-            total = jnp.sum(e, axis=-1, keepdims=True)
-            lsum = jnp.where(lane == 2 * p + h, peak + jnp.log(total), lsum)
-            outs.append(dot((e / total).astype(B16), v2))
+            tot = jnp.sum(e, axis=-1, keepdims=True)
+            lsum = jnp.where(lane == 2 * p + h, peak + jnp.log(tot), lsum)
+            outs.append(dot((e / tot).astype(B16), v2))
         mixed_o[:, 128 * p : 128 * (p + 1)] = jnp.where(low_lane, outs[0], outs[1]).astype(B16)
     lsum_o[...] = lsum
-    att = dot(mixed_o[...], outw[...]) + bias[2:3, :]
+    att = dot(mixed_o[...], outw[...]) + bias_o[2:3, :]
     att_o[...] = att
     resid = source + mod[2:3] * att
     resid_o[...] = resid
     n2, _ = norm_parts(resid)
     second = (n2 * (1.0 + mod[4:5]) + mod[3:4]).astype(B16)
     second_o[...] = second
-    logits = dot(second, router[...])
-    picks = [(routes[:, k : k + 1] == lane) for k in range(2)]
-    chosen = [jnp.sum(jnp.where(pick, logits, 0.0), axis=-1, keepdims=True) for pick in picks]
-    top = jnp.maximum(chosen[0], chosen[1])
-    ex = [jnp.exp(v - top) for v in chosen]
-    gates = [v / (ex[0] + ex[1]) for v in ex]
-    gates_o[...] = jnp.where(lane == 0, gates[0], jnp.where(lane == 1, gates[1], 0.0))
+
+    lane8 = lax.broadcasted_iota(jnp.int32, (length, E), 1)
+    two = (
+        lax.broadcasted_iota(jnp.int32, (2, 128), 0) == lax.broadcasted_iota(jnp.int32, (2, 128), 1)
+    )
+    route_cols = dot_tn(
+        routes[...].astype(F32).astype(B16), jnp.where(two, 1.0, 0.0).astype(B16)
+    ).astype(jnp.int32)
+    route = [route_cols[:, k : k + 1] for k in range(2)]
+    picks = [(r == lane8) for r in route]
     both = jnp.where(picks[0], 1.0, 0.0) + jnp.where(picks[1], 1.0, 0.0)
     earlier = (
         lax.broadcasted_iota(jnp.int32, (length, length), 1)
@@ -454,205 +684,226 @@
     places = []
     for k in range(2):
         slot = jnp.sum(jnp.where(picks[k], rank, 0.0), axis=-1, keepdims=True).astype(jnp.int32)
-        places.append(jnp.where(slot < CAP, routes[:, k : k + 1] * CAP + slot, -1))
-    place_o[...] = jnp.where(lane == 0, places[0], jnp.where(lane == 1, places[1], -1))
+        places.append(jnp.where(slot < CAP, route[k] * CAP + slot, -1))
+    place_o[...] = jnp.where(
+        lane == 0,
+        places[0],
+        jnp.where(lane == 1, places[1], jnp.where(lane == 2, route[0], route[1])),
+    )
     maps = [jnp.where(choose_rows(v, E * CAP), 1.0, 0.0) for v in places]
-    sbuf_o[...] = dot_tn((maps[0] + maps[1]).astype(B16), second).astype(B16)
+    sbuf[...] = dot_tn((maps[0] + maps[1]).astype(B16), second).astype(B16)
+    give_rows = PlaneExchange(sbuf, rows, ds0, dr0)
+    give_rows.start()
+    logits = dot_nt(second, rt_o[...].astype(B16))
+    chosen = [jnp.sum(jnp.where(pick, logits, 0.0), axis=-1, keepdims=True) for pick in picks]
+    top = jnp.maximum(chosen[0], chosen[1])
+    e2 = [jnp.exp(v - top) for v in chosen]
+    gates = [v / (e2[0] + e2[1]) for v in e2]
+    gates_o[...] = jnp.where(lane == 0, gates[0], jnp.where(lane == 1, gates[1], 0.0))
     moe_grad = (mod[5:6] * cot[...].astype(F32)).astype(B16).astype(F32)
     pair = [(g * moe_grad).astype(B16) for g in gates]
-    gbuf_o[...] = (
+    gbuf[...] = (
         dot_tn(maps[0].astype(B16), pair[0]) + dot_tn(maps[1].astype(B16), pair[1])
     ).astype(B16)
-
-
-def front(tok, cot, routes, mod_in, abias, qkv, outw, bias, router):
+    give_grads = PlaneExchange(gbuf, grads, ds1, dr1)
+    give_grads.start()
+    for column in later:
+        column.take(2)
+
+    first_x = x == 0
+    acc[...] = jnp.zeros_like(acc) + jnp.where(first_x, bout_r[0:1, :], bout_r[1:2, :]).astype(F32)
+    for load in loads:
+        load.wait()
+    give_rows.wait_in()
+
+    def span(f):
+        return pl.ds(pl.multiple_of(f * CHUNK, 128), CHUNK)
+
+    def put_slope(f):
+        return pltpu.make_async_copy(slopes.at[:, span(f)], slopes_o.at[:, span(f)], osem.at[1, f])
+
+    def put_out(f):
+        return pltpu.make_async_copy(dwout.at[span(f), :], dwout_o.at[span(f), :], osem.at[0, f])
+
+    def forward(f, carry):
+        cols = span(f)
+        bias = jnp.where(first_x, bin_r[0:1, cols], bin_r[1:2, cols]).astype(F32)
+        act, slope = gelu_parts(dot(rows[...], win[:, cols]) + bias)
+        low = act.astype(B16)
+        lows[:, cols] = low
+        slopes[:, cols] = slope
+        put_slope(f).start()
+        acc[...] += dot(low, wout[cols, :])
+        return carry
+
+    count = hidden // CHUNK
+    lax.fori_loop(0, count, forward, 0)
+    res_o[...] = acc[...].astype(B16)
+    give_grads.wait_in()
+    for column in later:
+        column.take(3)
+
+    def outer(f, carry):
+        cols = span(f)
+        dwout[cols, :] = dot_tn(lows[:, cols], grads[...]).astype(B16)
+        put_out(f).start()
+        return carry
+
+    lax.fori_loop(0, count, outer, 0)
+    for column in later:
+        column.finish()
+    for exchange in (give_rows, give_grads):
+        exchange.wait_out()
+    peers(lambda p: first(p, p).wait_send())
+    peers(lambda p: second_hop(p, p).wait_send())
+    for copy in keep:
+        copy.wait()
+    for f in range(count):
+        put_slope(f).wait()
+        put_out(f).wait()
+
+
+def lead_part(tok, cot, route, cond, ada, adab, qvb, outb, soutb, sinb, router, bin_r, bout_r, shards, win, wout):
+    n = NZ * NX
     length, width = tok.shape
-    rows = E * CAP
+    hidden = win.shape[2]
+    slots = E * CAP
+    dma = pltpu.SemaphoreType.DMA
+    vm = pltpu.VMEM
+    tiles = (ada.shape[1] // 128 + 7) // 8 * 8
+    wide = [sds((n * s.shape[0], s.shape[1]), B16) for s in shards[:2]]
+    wide += [sds((NZ * s.shape[0], s.shape[1] // 2), B16) for s in shards[2:]]
+    outs = [
+        sds((length, width), B16),
+        sds((length, 3 * width), B16),
+        sds((length, 128), F32),
+        sds((length, width), B16),
+        sds((length, width), F32),
+        sds((length, width), F32),
+        sds((length, width), B16),
+        sds((length, 128), F32),
+        sds((length, 128), jnp.int32),
+        sds((8, width), F32),
+        sds((8, width), F32),
+        sds((1, hidden), F32),
+        sds((E, width), F32),
+        sds((8, 128), F32),
+        sds((slots, width), B16),
+        sds((slots, width), B16),
+        sds((slots, width), B16),
+    ]
+    far = wide + [sds((slots, hidden), F32), sds((hidden, width), B16)]
     return pl.pallas_call(
-        front_kernel,
-        out_shape=[
-            sds((length, width), B16),
-            sds((length, 3 * width), B16),
-            sds((length, 128), F32),
-            sds((length, width), B16),
-            sds((length, width), F32),
-            sds((length, width), F32),
-            sds((length, width), B16),
-            sds((length, 128), F32),
-            sds((length, 128), jnp.int32),
-            sds((rows, width), B16),
-            sds((rows, width), B16),
-            sds((8, width), F32),
-        ],
-        in_specs=[VM] * 9,
-        out_specs=[VM] * 12,
+        lead_kernel,
+        out_shape=outs + far,
+        in_specs=[VM] * 13 + [HB] * 6,
+        out_specs=[VM] * len(outs) + [HB] * len(far),
+        scratch_shapes=[
+            vm((32, 128), F32),
+            vm((n, 32, 128), F32),
+            vm((n, tiles, 128), F32),
+            vm((n, tiles, 128), F32),
+            vm(wide[0].shape, B16),
+            vm(wide[1].shape, B16),
+            vm((slots, width), B16),
+            vm((slots, width), B16),
+            vm((width, hidden), B16),
+            vm((hidden, width), B16),
+            vm((hidden, width), B16),
+            vm((slots, hidden), B16),
+            vm((slots, hidden), F32),
+            vm((slots, width), F32),
+            dma((n,)),
+            dma((n,)),
+            dma((n,)),
+            dma((n,)),
+        ]
+        + [dma((E,))] * 4
+        + [dma((4,)), dma((2, hidden // CHUNK))]
+        + Gather.semaphores(2)
+        + [dma((2, NZ)), dma((NZ,)), dma((1,))] * 2,
+        compiler_params=params(1),
+        name="front_and_expert",
+    )(tok, cot, route, cond, ada, adab, qvb, outb, soutb, sinb, router, bin_r, bout_r, *shards, win, wout)
+
+
+def expert_back_kernel(which, rows, grads, slopes, win, wout, dwin, bgr, ebias, back):
+    f = pl.program_id(0)
+    last = pl.num_programs(0) - 1
+    width, chunk = rows.shape[1], slopes.shape[1]
+    tiles = chunk // 128
+
+    @pl.when(f == 0)
+    def _():
+        back[...] = jnp.zeros_like(back)
+        ebias[...] = jnp.zeros_like(ebias)
+        column = jnp.sum(grads[...].astype(F32), axis=0, keepdims=True)
+        for j in range(width // 128):
+            ebias[pl.ds((last + 1) * tiles + j, 1), :] = column[:, 128 * j : 128 * (j + 1)]
+
+    pre = (dot_nt(grads[...], wout[0]) * slopes[...]).astype(B16)
+    dwin[...] = dot_tn(rows[...], pre).astype(B16)
+    back[...] += dot_nt(pre, win[0])
+    col = jnp.sum(pre.astype(F32), axis=0, keepdims=True)
+    for j in range(tiles):
+        ebias[pl.ds(f * tiles + j, 1), :] = col[:, 128 * j : 128 * (j + 1)]
+
+    @pl.when(f == last)
+    def _():
+        bgr[...] = back[...].astype(B16)
+
+
+def expert_back(which, rows, grads, slopes, win, wout):
+    slots, width = rows.shape
+    hidden = slopes.shape[1]
+    whole = lambda f, w: (0, 0)
+    return pl.pallas_call(
+        expert_back_kernel,
+        out_shape=[sds((width, hidden), B16), sds((slots, width), B16), sds((32, 128), F32)],
+        grid_spec=pltpu.PrefetchScalarGridSpec(
+            num_scalar_prefetch=1,
+            grid=(hidden // CHUNK,),
+            in_specs=[
+                pl.BlockSpec((slots, width), whole),
+                pl.BlockSpec((slots, width), whole),
+                pl.BlockSpec((slots, CHUNK), lambda f, w: (0, f)),
+                pl.BlockSpec((1, width, CHUNK), lambda f, w: (w[0], 0, f)),
+                pl.BlockSpec((1, CHUNK, width), lambda f, w: (w[0], f, 0)),
+            ],
+            out_specs=[
+                pl.BlockSpec((width, CHUNK), lambda f, w: (0, f)),
+                pl.BlockSpec((slots, width), whole),
+                pl.BlockSpec((32, 128), whole),
+            ],
+            scratch_shapes=[pltpu.VMEM((slots, width), F32)],
+        ),
         compiler_params=params(),
-        name="attention_front",
-    )(tok, cot, routes, mod_in, abias, qkv, outw, bias, router)
-
-
-def plane_peer(k):
-    z, x, y, c = coords()
-    xt = 1 - x if k & 1 else x
-    ct = 1 - c if k & 2 else c
-    yt = 1 - y if k & 4 else y
-    return dev(z, xt, yt, ct), 4 * yt + 2 * ct + xt
-
-
-def plane_rank():
-    _, x, y, c = coords()
-    return 4 * y + 2 * c + x
-
-
-def greet_plane():
+        name="expert_back",
+    )(which, rows, grads, slopes, win, wout)
+
+
+def middle_kernel(
+    res, bgr, second_r, resid_r, att_r, cot, mod, sin_c, sout_c, sinb, bias, router, gates_r, place_r,
+    mixed, outw,
+    out_o, rgrad_o, mgrad_o, dsin, dsout, dout, drouter, vecs, mg2,
+    ret, retg, shared, sgrad, sin, sout, send, recv, send2, recv2, *ssems,
+):
     barrier = pltpu.get_barrier_semaphore()
     for k in range(1, E):
         greet(barrier, plane_peer(k)[0])
     pl.semaphore_wait(barrier, E - 1)
-
-
-def slot_rows(ref, rank):
-    return ref.at[pl.ds(pl.multiple_of(rank * CAP, 16), CAP), :]
-
-
-def plane_exchange(sources, targets, send, recv):
-    rank = plane_rank()
-
-    def copy(k, i, to=None):
-        peer, other = plane_peer(k)
-        return remote(
-            slot_rows(sources[i], other), slot_rows(targets[i], rank), send.at[i, k], recv.at[i, k], peer
-        )
-
-    pairs = [(k, i) for k in (7, 5, 6, 4, 3, 1, 2) for i in range(len(sources))]
-    for k, i in pairs:
-        copy(k, i).start()
-    for source, target in zip(sources, targets):
-        start = pl.multiple_of(rank * CAP, 16)
-        target[pl.ds(start, CAP), :] = source[pl.ds(start, CAP), :]
-
-    def take(k, i):
-        _, other = plane_peer(k)
-        return remote(
-            slot_rows(sources[i], other), slot_rows(targets[i], other), send.at[i, k], recv.at[i, k],
-            plane_peer(k)[0],
-        )
-
-    def wait_in():
-        for k, i in pairs:
-            take(k, i).wait_recv()
-
-    def wait_out():
-        for k, i in pairs:
-            take(k, i).wait_send()
-
-    return wait_in, wait_out
-
-
-EXPERT_CHUNK = 512
-
-
-def expert_kernel(
-    sbuf, gbuf, win_h, wout_h, bin_r, bout_r,
-    dwin, dwout, res, bgr, ebias,
-    rows, grads, win, wout, acc, back, send, recv, wsem,
-):
-    x = coords()[1]
-    loads = [
-        pltpu.make_async_copy(win_h.at[x], win, wsem.at[0]),
-        pltpu.make_async_copy(wout_h.at[x], wout, wsem.at[1]),
-    ]
-    for load in loads:
-        load.start()
-    greet_plane()
-    wait_in, wait_out = plane_exchange((sbuf, gbuf), (rows, grads), send, recv)
-    for load in loads:
-        load.wait()
-    first_x = x == 0
-    bout = jnp.where(first_x, bout_r[0:1, :], bout_r[1:2, :])
-    acc[...] = jnp.zeros_like(acc) + bout
-    back[...] = jnp.zeros_like(back)
-    ebias[...] = jnp.zeros_like(ebias)
-    wait_in()
-    width = rows.shape[1]
-    hidden = win.shape[1]
-    chunk = EXPERT_CHUNK
-    tiles = chunk // 128
-    column = jnp.sum(grads[...].astype(F32), axis=0, keepdims=True)
-    for j in range(width // 128):
-        at = hidden // 128 + j
-        ebias[at : at + 1, :] = column[:, 128 * j : 128 * (j + 1)]
-
-    def body(f, carry):
-        cols = pl.ds(pl.multiple_of(f * chunk, 128), chunk)
-        bias = jnp.where(first_x, bin_r[0:1, cols], bin_r[1:2, cols])
-        w1 = win[:, cols]
-        w2 = wout[cols, :]
-        data = rows[...]
-        grad = grads[...]
-        act, slope = gelu_parts(dot(data, w1) + bias)
-        low = act.astype(B16)
-        acc[...] += dot(low, w2)
-        pre = (dot_nt(grad, w2) * slope).astype(B16)
-        dwout[cols, :] = dot_tn(low, grad).astype(B16)
-        dwin[:, cols] = dot_tn(data, pre).astype(B16)
-        back[...] += dot_nt(pre, w1)
-        col = jnp.sum(pre.astype(F32), axis=0, keepdims=True)
-        for j in range(tiles):
-            ebias[pl.ds(f * tiles + j, 1), :] = col[:, 128 * j : 128 * (j + 1)]
-        return carry
-
-    lax.fori_loop(0, hidden // chunk, body, 0)
-    res[...] = acc[...].astype(B16)
-    bgr[...] = back[...].astype(B16)
-    wait_out()
-
-
-def expert(sbuf, gbuf, win, wout, bin_r, bout_r):
-    rows, width = sbuf.shape
-    hidden = win.shape[2]
-    dma = pltpu.SemaphoreType.DMA
-    return pl.pallas_call(
-        expert_kernel,
-        out_shape=[
-            sds((width, hidden), B16),
-            sds((hidden, width), B16),
-            sds((rows, width), B16),
-            sds((rows, width), B16),
-            sds((32, 128), F32),
-        ],
-        in_specs=[VM, VM, HB, HB, VM, VM],
-        out_specs=[VM] * 5,
-        scratch_shapes=[
-            pltpu.VMEM((rows, width), B16),
-            pltpu.VMEM((rows, width), B16),
-            pltpu.VMEM((width, hidden), B16),
-            pltpu.VMEM((hidden, width), B16),
-            pltpu.VMEM((rows, width), F32),
-            pltpu.VMEM((rows, width), F32),
-            dma((2, E)),
-            dma((2, E)),
-            dma((2,)),
-        ],
-        compiler_params=params(2),
-        name="routed_expert",
-    )(sbuf, gbuf, win, wout, bin_r, bout_r)
-
-
-SHARED_CHUNK = 768
-
-
-def middle_kernel(
-    res, bgr, second_r, resid_r, att_r, cot, routes, mod, sin, sout, sinb, bias, router, gates_r, place_r,
-    mixed, outw,
-    out_o, rgrad_o, mgrad_o, dsin, dsout, dout, drouter, vecs, mg2,
-    ret, retg, shared, sgrad, send, recv,
-):
-    greet_plane()
-    wait_in, wait_out = plane_exchange((res, bgr), (ret, retg), send, recv)
+    count = len(ssems) // 2
+    spreads = (Spread(sin_c, sin, *ssems[:count]), Spread(sout_c, sout, *ssems[count:]))
+    for spread in spreads:
+        spread.begin()
+    gives = (PlaneExchange(res, ret, send, recv), PlaneExchange(bgr, retg, send2, recv2))
+    for give in gives:
+        give.start()
+    for spread in spreads:
+        spread.near()
     length, width = second_r.shape
-    hidden = sin.shape[1]
-    chunk = SHARED_CHUNK
+    hidden = sin.shape[3]
+    chunk = hidden // NZ
     second = second_r[...]
     grad_out = cot[...].astype(F32)
     moe_low = (mod[5:6] * grad_out).astype(B16)
@@ -660,11 +911,17 @@
     shared[...] = jnp.zeros_like(shared) + bias[3:4, :]
     sgrad[...] = jnp.zeros_like(sgrad)
     vecs[...] = jnp.zeros_like(vecs)
+    for spread in spreads:
+        spread.take_x()
+    for spread in spreads:
+        spread.take_y()
+    for spread in spreads:
+        spread.finish()
 
     def body(f, carry):
         cols = pl.ds(pl.multiple_of(f * chunk, 128), chunk)
-        w1 = sin[:, cols]
-        w2 = sout[cols, :]
+        w1 = sin[:, :, :, cols].reshape(width, chunk)
+        w2 = sout[f].reshape(chunk, width)
         act, slope = gelu_parts(dot(second, w1) + sinb[:, cols])
         low = act.astype(B16)
         shared[...] += dot(low, w2)
@@ -678,12 +935,13 @@
         return carry
 
     lax.fori_loop(0, hidden // chunk, body, 0)
-    lane = lax.broadcasted_iota(jnp.int32, (length, 128), 1)
+    lane = lax.broadcasted_iota(jnp.int32, (length, E), 1)
     gates = [gates_r[:, k : k + 1] for k in range(2)]
     maps = [
         jnp.where(choose_rows(place_r[:, k : k + 1], E * CAP), 1.0, 0.0) for k in range(2)
     ]
-    wait_in()
+    for give in gives:
+        give.wait_in()
     back = ret[...]
     rows = [dot(m.astype(B16), back) for m in maps]
     moe = shared[...] + (gates[0] * rows[0] + gates[1] * rows[1])
@@ -693,16 +951,16 @@
     mg2[5:6, :] = jnp.sum(grad_out * moe, axis=0, keepdims=True)
     ggrad = [jnp.sum(moe_grad * r, axis=-1, keepdims=True) for r in rows]
     inner = gates[0] * ggrad[0] + gates[1] * ggrad[1]
-    lgrad = jnp.zeros((length, 128), F32)
+    lgrad = jnp.zeros((length, E), F32)
     for k in range(2):
-        pick = routes[:, k : k + 1] == lane
+        pick = place_r[:, 2 + k : 3 + k] == lane
         lgrad = lgrad + jnp.where(pick, gates[k] * (ggrad[k] - inner), 0.0)
     lgrad = lgrad.astype(B16)
-    drouter[...] = dot_tn(lgrad, second)[0:E, :]
+    drouter[...] = dot_tn(lgrad, second)
     grad = (
         sgrad[...]
         + dot((maps[0] + maps[1]).astype(B16), retg[...])
-        + dot_nt(lgrad, router[...])
+        + dot(lgrad, router[...].astype(B16))
     )
     n2, r2 = norm_parts(resid)
     mg2[3:4, :] = jnp.sum(grad, axis=0, keepdims=True)
@@ -722,13 +980,16 @@
         for j in range(width // 128):
             at = base + i * (width // 128) + j
             vecs[at : at + 1, :] = row[:, 128 * j : 128 * (j + 1)]
-    wait_out()
+    for give in gives:
+        give.wait_out()
+    for spread in spreads:
+        spread.close()
 
 
 def middle(*args):
-    res, second, sin = args[0], args[2], args[8]
+    res, second, sin = args[0], args[2], args[7]
     length, width = second.shape
-    rows, hidden = res.shape[0], sin.shape[1]
+    rows, hidden = res.shape[0], 2 * sin.shape[1]
     dma = pltpu.SemaphoreType.DMA
     return pl.pallas_call(
         middle_kernel,
@@ -743,16 +1004,22 @@
             sds((40, 128), F32),
             sds((8, width), F32),
         ],
-        in_specs=[VM] * 17,
+        in_specs=[VM] * 7 + [HB] * 2 + [VM] * 7,
         out_specs=[VM] * 9,
         scratch_shapes=[
             pltpu.VMEM((rows, width), B16),
             pltpu.VMEM((rows, width), B16),
             pltpu.VMEM((length, width), F32),
             pltpu.VMEM((length, width), F32),
-            dma((2, E)),
-            dma((2, E)),
-        ],
+            pltpu.VMEM((NZ, NX, width // NZ // NX, hidden), B16),
+            pltpu.VMEM((NZ, NX, hidden // NZ // NX, width), B16),
+            dma((E,)),
+            dma((E,)),
+            dma((E,)),
+            dma((E,)),
+        ]
+        + Spread.semaphores()
+        + Spread.semaphores(),
         compiler_params=params(3),
         name="shared_expert_combine",
     )(*args)
@@ -857,7 +1124,7 @@
         self.grad, self.out, self.width, self.y_first = grad, out, width, y_first
         self.half = grad.shape[-1] // 2
         self.col = col
-        self.cbuf, self.lbuf, self.ebuf, self.fbuf, self.zl, self.zr = bufs
+        self.cbuf, self.lbuf, self.ebuf, self.fbuf, self.zin = bufs
         self.one, self.zsem = sems
 
     @staticmethod
@@ -869,9 +1136,8 @@
             vm(NZ, 2),
             vm(NZ),
             vm(NZ),
-            vm(NZ),
             pltpu.SemaphoreType.DMA((14,)),
-            pltpu.SemaphoreType.DMA((4, NZ)),
+            pltpu.SemaphoreType.DMA((2, NZ)),
         ]
 
     def cols(self, c):
@@ -905,16 +1171,21 @@
             source, to = self.ebuf.at[:, 1 - self.y], dev(self.z, self.x, 1 - self.y, self.c)
         return remote(source, self.fbuf, self.one.at[5], self.one.at[6], to)
 
-    def zcopy(self, zb, side):
-        into = self.zl if side else self.zr
-        to = lax.rem(self.z + (1 if side else NZ - 1), NZ)
+    def zcopy(self, zb, at):
         return remote(
             self.fbuf.at[zb],
-            into.at[zb],
-            self.zsem.at[side, zb],
-            self.zsem.at[2 + side, zb],
-            dev(to, self.x, self.y, self.c),
-        )
+            self.zin.at[at],
+            self.zsem.at[0, zb],
+            self.zsem.at[1, at],
+            dev(zb, self.x, self.y, self.c),
+        )
+
+    def others(self, action):
+        for zb in range(NZ):
+
+            @pl.when(zb != self.z)
+            def _():
+                action(zb)
 
     def own(self):
         return self.fbuf.at[self.z]
@@ -942,15 +1213,6 @@
         return remote(
             here, here, self.one.at[12], self.one.at[13], dev(self.z, self.x, self.y, 1 - self.c)
         )
-
-    def absorb(self, zb, side):
-        into = self.zl if side else self.zr
-        has = self.z > 0 if side else self.z < NZ - 1
-
-        @pl.when(has)
-        def _():
-            self.zcopy(zb, side).wait_recv()
-            self.fbuf[zb] = (self.fbuf[zb].astype(F32) + into[zb].astype(F32)).astype(B16)
 
     def stage(self, s):
         if s == 0:
@@ -969,26 +1231,21 @@
             self.copy2().wait_recv()
             side = self.x if self.y_first else self.y
             add_into(self.fbuf, lambda i: self.ebuf[i[0], side], (NZ,))
-        if 2 <= s < 2 + NZ - 1:
-            k = NZ - 1 - (s - 2)
-            for side in (1, 0):
-                zb = self.z + k if side else self.z - k
-
-                @pl.when(zb < NZ if side else zb >= 0)
-                def _():
-                    self.absorb(zb, side)
-                    self.zcopy(zb, side).start()
-
-        if s == 2 + NZ - 1:
-            self.absorb(self.z, 1)
-            self.absorb(self.z, 0)
+            self.others(lambda zb: self.zcopy(zb, self.z).start())
+        elif s == 3:
+            self.zin[self.z] = self.fbuf[self.z]
+            self.others(lambda zb: self.zcopy(zb, zb).wait_recv())
+            total = self.zin[0].astype(F32)
+            for zb in range(1, NZ):
+                total = total + self.zin[zb].astype(F32)
+            self.fbuf[self.z] = total.astype(B16)
             self.give_y().start()
             self.give_c().start()
             self.keep().start()
-        if s == 3 + NZ - 1:
+        elif s == 4:
             self.give_y_in().wait_recv()
             self.pass_c().start()
-        if s == 4 + NZ - 1:
+        elif s == 5:
             self.keep().wait()
             self.give_c_in().wait_recv()
             self.pass_c_in().wait_recv()
@@ -998,13 +1255,7 @@
             self.give_y().wait_send()
             self.give_c().wait_send()
             self.pass_c().wait_send()
-            for k in range(1, NZ):
-                for side in (1, 0):
-                    zb = self.z + k if side else self.z - k
-
-                    @pl.when(zb < NZ if side else zb >= 0)
-                    def _():
-                        self.zcopy(zb, side).wait_send()
+            self.others(lambda zb: self.zcopy(zb, zb).wait_send())
 
     def give_y_in(self):
         return remote(
@@ -1024,15 +1275,17 @@
             here, here, self.one.at[12], self.one.at[13], dev(self.z, self.x, self.y, 1 - self.c)
         )
 
-    STAGES = 5 + NZ - 1
+    STAGES = 6
 
 
 def sums_kernel(*refs):
     grads = refs[:4]
-    vecs, qvec, drouter, ebias, mgt, condt, ada = refs[4:11]
-    outs = refs[11:15]
-    small, esum, tiles, cgot = refs[15:19]
-    rest = list(refs[19:])
+    mine_out = refs[4]
+    vecs, qvec, drouter, ebias, mgt, condt, ada = refs[5:12]
+    outs = refs[12:16]
+    pair_out = refs[16]
+    small, esum, tiles, cgot = refs[17:21]
+    rest = list(refs[21:])
     z, x, y, c = coords()
     dp, ex = lax.axis_index("dp"), lax.axis_index("expert")
     n = NZ * NX
@@ -1057,14 +1310,28 @@
         grad = grads[matrix]
         width = grad.shape[-1] // 2 // share
         plans.append(
-            Reduce(grad, outs[matrix], part * width, width, y_first, rest[:6], rest[6:8])
-        )
-        rest = rest[8:]
-    ssum, sgot, zgot, esend, egot, mine, csend, sems, dsem, zsem, tsem = rest
+            Reduce(grad, outs[matrix], part * width, width, y_first, rest[:5], rest[5:7])
+        )
+        rest = rest[7:]
+    ssum, sgot, zgot, esend, egot, mine, csend, sems, dsem, zsem, tsem, wsem = rest
 
     for plan in plans:
         plan.core_copy().start()
         plan.load().start()
+
+    def swap():
+        return remote(
+            mine_out.at[1 - x], pair_out.at[x], wsem.at[0], wsem.at[1], dev(z, 1 - x, y, c)
+        )
+
+    def swap_in():
+        return remote(
+            mine_out.at[1 - x], pair_out.at[1 - x], wsem.at[0], wsem.at[1], dev(z, 1 - x, y, c)
+        )
+
+    swap().start()
+    swap_keep = pltpu.make_async_copy(mine_out.at[x], pair_out.at[x], wsem.at[2])
+    swap_keep.start()
 
     rows = vecs.shape[0]
     ssum[0:rows, :] = vecs[...]
@@ -1175,15 +1442,16 @@
         lines(lambda zb: zsum(zb, zb).wait_send())
 
     steps = [small0, small1, small2, small3, small4, small5]
-    for t in range(Reduce.STAGES + len(plans) - 1):
-        for i, plan in enumerate(plans):
-            if 0 <= t - i < Reduce.STAGES:
-                plan.stage(t - i)
-        if t < len(steps):
-            steps[t]()
-
-
-def device_sums(grads, vecs, qvec, drouter, ebias, mgt, condt, ada):
+    for t in range(Reduce.STAGES):
+        steps[t]()
+        for plan in plans:
+            plan.stage(t)
+    swap_in().wait_recv()
+    swap().wait_send()
+    swap_keep.wait()
+
+
+def device_sums(grads, mine_out, vecs, qvec, drouter, ebias, mgt, condt, ada):
     n = NZ * NX
     dma = pltpu.SemaphoreType.DMA
     split = [g.reshape(NZ, NX, 2, g.shape[0] // (4 * NZ), g.shape[1]) for g in grads]
@@ -1206,23 +1474,25 @@
         dma((4, n)),
         dma((4, NZ)),
         dma((2, 3)),
+        dma((3,)),
     ]
     out = pl.pallas_call(
         sums_kernel,
         out_shape=outs
         + [
+            sds(mine_out.shape, B16),
             sds((rows, 128), F32),
             sds((2, 32, 128), F32),
             sds((4, n, 48, 128), F32),
             sds((n, 8, 128), F32),
         ],
-        in_specs=[HB] * 4 + [VM] * 7,
-        out_specs=[HB] * 4 + [VM] * 4,
+        in_specs=[HB] * 5 + [VM] * 7,
+        out_specs=[HB] * 5 + [VM] * 4,
         scratch_shapes=scratch,
         compiler_params=params(4),
         name="device_sums",
-    )(*split, vecs, qvec, drouter, ebias, mgt, condt, ada)
-    return [o.reshape(-1, o.shape[2]).astype(F32) for o in out[:4]], out[4:]
+    )(*split, mine_out, vecs, qvec, drouter, ebias, mgt, condt, ada)
+    return [o.reshape(-1, o.shape[2]).astype(F32) for o in out[:4]], out[4], out[5:]
 
 
 def on_block(
@@ -1237,70 +1507,47 @@
     hidden = shared_in.shape[1]
     part = width // n
     tok, cot, route = tokens[0], cotangent[0], routes[0]
-    cond_act, silu_back = jax.vjp(jax.nn.silu, conditioning.astype(F32))
-    cond_low = cond_act.astype(B16).astype(F32)
-
-    def rows_of(v, count):
-        v = v.astype(F32).reshape(-1)
-        return jnp.pad(v, (0, count * 128 - v.shape[0])).reshape(count, 128)
-
-    def wide(v):
-        return jnp.pad(v.astype(F32), ((0, 0), (0, 128 - part)))
-
-    pack = jnp.concatenate(
-        [
-            wide(qv_bias),
-            wide(out_bias[None]),
-            wide(shared_out_bias[None]),
-            rows_of(shared_in_bias, 4),
-            rows_of(ada_bias, 8),
-            rows_of(router, 8),
-            wide(cond_low.reshape(n, part)),
-        ],
-        axis=0,
-    )
-    mod_raw, packs, fulls = gather_dense(
-        ada_weight, pack, (qkv_weight, out_weight, shared_in, shared_out), (True, True, True, False)
-    )
-    qkv_full, out_full, sin_full, sout_full = fulls
-    bias = jnp.pad(packs[:, 0:4, :part].transpose(1, 0, 2).reshape(4, width), ((0, 4), (0, 0)))
-    sinb = packs[:, 4:7, :].reshape(1, hidden)
-    abias = packs[:, 8:16, :].reshape(n, -1)[:, : ada_bias.shape[0]].reshape(6, width)
-    abias = jnp.pad(abias, ((0, 2), (0, 0)))
-    router_full = packs[:, 16:24, :].reshape(n, -1)[:, : part * E].reshape(width, E)
-    router_full = jnp.pad(router_full, ((0, 0), (0, 128 - E))).astype(B16)
-
-    (normed, proj, lsum, mixed, att, resid, second, gates, place, sbuf, gbuf, mod) = front(
-        tok, cot, route, mod_raw, abias, qkv_full, out_full, bias, router_full
-    )
-    dwin, dwout, res, bgr, ebias = expert(
-        sbuf, gbuf, expert_in, expert_out, expert_in_bias.astype(F32), expert_out_bias.astype(F32)
+    _, silu_back = jax.vjp(jax.nn.silu, conditioning.astype(F32))
+    (
+        normed, proj, lsum, mixed, att, resid, second, gates, place, mod, bias, sinb, router_t,
+        condt, rows, grads, res, qkv_full, out_full, sin_full, sout_full, slopes, dwout,
+    ) = lead_part(
+        tok, cot, route.T, conditioning, ada_weight, ada_bias[None], qv_bias, out_bias[None], shared_out_bias[None],
+        shared_in_bias[None], router.T, expert_in_bias, expert_out_bias,
+        (qkv_weight, out_weight, shared_in, shared_out), expert_in, expert_out,
     )
     line = [[NX * z + xx for z in range(NZ)] for xx in range(NX)]
     turn = [(i, i // NX * NX + 1 - i % NX) for i in range(n)]
 
+    first = x == 0
+
     def over_z(grad):
-        mine = lax.psum_scatter(
-            grad, "dp", scatter_dimension=0, axis_index_groups=line, tiled=True
-        )
-        pair = mine.reshape(NX, -1, mine.shape[1])
-        keep = lax.dynamic_index_in_dim(pair, x, 0, keepdims=False)
-        give = lax.dynamic_index_in_dim(pair, 1 - x, 0, keepdims=False)
+        return lax.psum_scatter(grad, "dp", scatter_dimension=0, axis_index_groups=line, tiled=True)
+
+    def swap(pair, axis):
+        keep = lax.dynamic_index_in_dim(pair, x, axis, keepdims=False)
+        give = lax.dynamic_index_in_dim(pair, 1 - x, axis, keepdims=False)
         came = lax.ppermute(give, "dp", turn)
-        first = x == 0
-        return jnp.stack([jnp.where(first, keep, came), jnp.where(first, came, keep)]).astype(F32)
-
-    dwout_sum = over_z(dwout)
-    dwin_sum = over_z(dwin)
+        return jnp.stack(
+            [jnp.where(first, keep, came), jnp.where(first, came, keep)], axis=axis
+        )
+
+    dwout_mine = over_z(dwout)
+    dwin, bgr, ebias = expert_back(
+        jnp.reshape(x, (1,)), rows, grads, slopes, expert_in, expert_out
+    )
+    dwin_mine = over_z(dwin)
     (output, rgrad, mgrad, dsin, dsout, dout, drouter, vecs, mg2) = middle(
-        res, bgr, second, resid, att, cot, route, mod, sin_full, sout_full, sinb, bias, router_full, gates, place,
+        res, bgr, second, resid, att, cot, mod, sin_full, sout_full, sinb, bias, router_t, gates, place,
         mixed, out_full,
     )
     tgrad, dqkv, qvec, mgt = back(tok, mod, normed, proj, lsum, mgrad, rgrad, qkv_full, mg2)
-    condt = jnp.pad(cond_low.reshape(-1, 128), ((0, 2), (0, 0)))
-    dense, (small, esum, tiles, cgot) = device_sums(
-        (dqkv, dout, dsin, dsout), vecs, qvec, drouter, ebias, mgt, condt, ada_weight
-    )
+    dense, dwout_pair, (small, esum, tiles, cgot) = device_sums(
+        (dqkv, dout, dsin, dsout), dwout_mine.reshape(NX, hidden // n, width), vecs, qvec, drouter, ebias, mgt, condt, ada_weight
+    )
+
+    dwout_sum = dwout_pair.astype(F32)
+    dwin_sum = swap(dwin_mine.reshape(NX, part, hidden), 0).astype(F32)
 
     def share(v, size):
         return lax.dynamic_slice_in_dim(v.reshape(-1), dp * size, size, 0)

time: 439 us -> 360 us (0.82)
  Pallas kernels: 358 us -> 315 us
  waiting for transfers between devices: 16.8 us -> 0.06 us
  local copies, waits for them, and re-layouts: 29.4 us -> 16.6 us
  other arithmetic: 15.5 us -> 9.57 us
    pallas_call x4 -> x3, Pallas kernels: 308 us -> 232 us  [the longest x1 126 us: device_sums(): pl.pallas_call(sums_kernel, out_shape=outs + [sds(mine_out.shape, B16), s...]
    pallas_call x1, Pallas kernels: 38.5 us -> 71.5 us  [middle(): pl.pallas_call(middle_kernel, out_shape=[sds((length, width), B16), sds((...]
    ppermute x2 -> x1, waiting for transfers between devices: 16.3 us -> 0.01 us  [swap(): came = lax.ppermute(give, 'dp', turn)]
    convert_element_type x9 -> x6, other arithmetic: 9.05 us -> 7.16 us  [the longest x4 4.02 us: device_sums(): o.reshape(-1, o.shape[2]).astype(F32)]
  transfers between devices with their start and end apart: 4 -> 3, of which waited for: 2 -> 0; matrix products, arithmetic and copies ran while one was open for 7% -> 6% of each run, Pallas kernels for 47% -> 63%
where the time goes in v2:
time: 360 us; the launch traced here: 359 us
  Pallas kernels  315 us (88%)
  local copies, waits for them, and re-layouts  16.6 us (5%)
  between operations  14.2 us (4%)
  other arithmetic  9.57 us (3%)
    pallas_call x1, Pallas kernels, device_sums(): pl.pallas_call(sums_kernel, out_shape=outs + [sds(mine_out.shape, B16), s...  126 us
    pallas_call x1, Pallas kernels, lead_part(): pl.pallas_call(lead_kernel, out_shape=outs + far, in_specs=[VM] * 13 + [H...  90.1 us
    pallas_call x1, Pallas kernels, middle(): pl.pallas_call(middle_kernel, out_shape=[sds((length, width), B16), sds((...  71.5 us
    pallas_call x1, Pallas kernels, expert_back(): pl.pallas_call(expert_back_kernel, out_shape=[sds((width, hidden), B16),...  15.9 us
    pallas_call x1, Pallas kernels, back(): pl.pallas_call(back_kernel, out_shape=[sds((length, width), F32), sds(qkv...  11.9 us
  transfers between devices with their start and end apart: 3, of which 0 were waited for; matrix products, arithmetic and copies ran while one was open for 6% of the time, Pallas kernels for 63%

profile of v2, /device:TPU:0, one launch (start us, length us, event | category | flops | bytes accessed | tf_op | source)
XLA Modules:
  0.0 359.0 jit_solution(7267924240049204824)
XLA Ops:
  7.2 0.0 reduce-scatter.3.cloned.1.call-start
  7.2 1.2 broadcast_in_dim.21.sinb_s
  8.5 1.3 broadcast_in_dim.18.adab
  9.7 90.1 %front_and_expert.1 = (bf16[256,768]{1,0:T(8,128)(2,1)}, bf16[256,2304]{1,0:T(8,128)(2,1)}, f32[256,128]{1,0:T(8,128)}, bf16[256,768]{1,0:T(8,128)(2,1)}, f32[25...) custom-call(bf16[256,768]{1,0:T(8,128)(2,1)} %bitcast.90, ...), custom_call_target="tpu_custom_call" | custom-call | tf_op jit(solution)/shard_map/front_and_expert/pallas_call | solution.py:796
  99.8 0.0 reduce-scatter.3.cloned.1.call-update
  99.8 0.2 reduce-scatter.5.cloned.1.call-start
  100.1 15.9 %expert_back.1 = (bf16[768,3072]{1,0:T(8,128)(2,1)}, bf16[640,768]{1,0:T(8,128)(2,1)}, f32[32,128]{1,0:T(8,128)}) custom-call(s32[1]{0:T(128)} %bitcast.7.which, bf16[640,768]{1,0:T(8,128)(2,1)} %get-tuple-element.67.rows, bf16[640,768]{1,0:T(8,128)(2,1)} %get-tuple-element.68.grads, f32[640,3072]{1,0:T(8,128)} %get-tuple-element.69.slopes, ...), custom_call_target="tpu_custom_call" | custom-call | tf_op jit(solution)/shard_map/expert_back/pallas_call | solution.py:860
  116.0 0.0 reduce-scatter.5.cloned.1.call-update
  116.0 71.5 %shared_expert_combine.1 = (bf16[256,768]{1,0:T(8,128)(2,1)}, f32[256,768]{1,0:T(8,128)}, bf16[256,768]{1,0:T(8,128)(2,1)}, bf16[768,3072]{1,0:T(8,128)(2,1)}, b...) custom-call(bf16[640,768]{1,0:T(8,128)(2,1)} %get-tuple-element.66.r, ...), custom_call_target="tpu_custom_call" | custom-call | tf_op jit(solution)/shard_map/shared_expert_combine/pallas_call | solution.py:994
  187.5 11.9 %attention_back.1 = (f32[256,768]{1,0:T(8,128)}, bf16[768,2304]{1,0:T(8,128)(2,1)}, f32[16,128]{1,0:T(8,128)}, f32[48,128]{1,0:T(8,128)}) custom-call(bf16[256,768]{1,0:T(8,128)(2,1)} %bitcast.91, f32[8,768]{1,0:T(8,128)} %get-tuple-element.74.mod, bf16[256,768]{1,0:T(8,128)(2,1)} %get-tuple-element.85.normed, bf16[256,2304]{1,0:T(8,128)(2,1)} %get-tuple-element.86.proj, ...), custom_call_target="tpu_custom_call" | custom-call | tf_op jit(solution)/shard_map/attention_back/pallas_call | solution.py:1084
  199.5 125.9 %device_sums.1 = (bf16[2,48,2304]{2,1,0:T(8,128)(2,1)}, bf16[2,48,768]{2,1,0:T(8,128)(2,1)}, bf16[2,48,3072]{2,1,0:T(8,128)(2,1)}, bf16[2,192,768]{2,1,0:T(8,128...) custom-call(bf16[4,2,2,48,2304]{4,3,2,1,0:T(8,128)(2,1)} %bitcast.87, ...), custom_call_target="tpu_custom_call" | custom-call | tf_op jit(solution)/shard_map/device_sums/pallas_call | solution.py:1479
  325.3 1.2 slice_reduce_fusion
  326.5 0.0 copy-start.7
  326.5 0.7 slice_bitcast_fusion.4
  327.2 0.8 slice_bitcast_fusion.5
  328.0 0.7 slice_bitcast_fusion.3
  328.7 0.7 slice_bitcast_fusion.1
  329.4 0.7 slice_bitcast_fusion.2
  330.2 0.9 slice_bitcast_fusion
  331.1 0.0 copy-start.4
  331.1 1.2 fusion.2
  332.3 0.0 reduce-scatter.5.cloned.1.call-done
  332.3 1.1 dynamic-slice_bitcast_fusion
  333.4 1.4 collective-permute-start
  334.8 0.8 slice_reduce_fusion.1
  335.6 0.1 reshape_squeeze.3
  335.7 0.6 fusion.7
  336.3 0.6 constant_dynamic-slice_fusion.1
  336.9 0.7 dynamic_slice.42
  337.5 0.6 constant_dynamic-slice_fusion
  338.2 0.7 constant_dynamic-slice_fusion.2
  338.8 0.6 dynamic_slice.43
  339.4 0.6 dynamic_slice.41
  340.0 0.7 bitcast_convert_fusion.3
  340.8 1.0 bitcast_convert_fusion.2
  341.8 1.1 bitcast_convert_fusion
  342.9 0.6 copy-done
  343.5 1.6 convert_element_type.55
  345.0 0.1 dynamic-slice_bitcast_fusion.1
  345.1 0.6 pad_maximum_fusion
  345.7 0.7 dynamic_slice.38
  346.3 1.7 fusion.3
  348.0 1.2 bitcast_convert_fusion.1
  349.2 0.0 collective-permute-done
  349.2 0.5 copy-done.1
  349.7 0.1 fusion
  349.8 1.6 maximum_convert_fusion
  351.4 0.7 copy.52
  (16 shorter events, 0.1 us)
Async XLA Ops:
  7.2 192.3 %reduce-scatter.3.cloned.1.call-start = ((), (), s32[]{:S(2)}) async-start(), calls=%async_computation.2 | async-start | bytes 5898240 | tf_op jit(solution)/shard_map/reduce_scatter | solution.py:1525
  99.8 232.5 %reduce-scatter.5.cloned.1.call-start = ((), (), s32[]{:S(2)}) async-start(), calls=%async_computation.3 | async-start | bytes 5898240 | tf_op jit(solution)/shard_map/reduce_scatter | solution.py:1525
  326.5 9.2 %copy-start.7 = (bf16[1,768]{1,0:T(2,128)(2,1)S(1)}, bf16[1,768]{1,0:T(2,128)(2,1)}, u32[]{:S(2)}) copy-start(bf16[1,768]{1,0:T(2,128)(2,1)} %cond.1) | copy-start | bytes 4612
  327.2 12.8 %copy-start.6 = (bf16[2,48,768]{2,1,0:T(8,128)(2,1)S(1)}, bf16[2,48,768]{2,1,0:T(8,128)(2,1)}, u32[]{:S(2)}) copy-start(bf16[2,48,768]{2,1,0:T(8,128)(2,1)} %get-tuple-element.108) | copy-start | bytes 442372
  331.1 9.7 %copy-start.4 = (bf16[2,48,2304]{2,1,0:T(8,128)(2,1)S(1)}, bf16[2,48,2304]{2,1,0:T(8,128)(2,1)}, u32[]{:S(2)}) copy-start(bf16[2,48,2304]{2,1,0:T(8,128)(2,1)} %get-tuple-element.106) | copy-start | bytes 1327108
  333.4 8.3 %copy-start.3 = (bf16[2,192,768]{2,1,0:T(8,128)(2,1)S(1)}, bf16[2,192,768]{2,1,0:T(8,128)(2,1)}, u32[]{:S(2)}) copy-start(bf16[2,192,768]{2,1,0:T(8,128)(2,1)} %get-tuple-element.110) | copy-start | bytes 1769476
  333.4 15.8 %collective-permute-start = (bf16[96,3072]{1,0:T(8,128)(2,1)S(1)}, bf16[96,3072]{1,0:T(8,128)(2,1)S(1)}, u32[]{:S(2)}, u32[]{:S(2)}) collective-permute-start(bf16[96,3072]{1,0:T(8,128)(2,1)S(1)} %dynamic-slice_bitcast_fusion), channel_id=1, source_target_pairs={{0,4},{4,0},{8,12},{12,8},{16,20},{20,16},{24,28},{28,24},{1,5},{5... | collective-permute-start | bytes 1769480 | tf_op jit(solution)/shard_map/ppermute | solution.py:1530
  341.8 1.7 copy-start
  345.0 3.0 copy-start.2
  348.0 1.7 copy-start.1
  349.8 1.6 copy-start.5
Sparse Core Ops, SparseCore 0:
  100.0 83.1 reduce-scatter.2
  185.5 102.3 reduce-scatter.4

commit v3 on v2

--- a/solution.py
+++ b/solution.py
@@ -40,6 +40,10 @@
 
 def dot_tn(a, b):
     return lax.dot_general(a, b, (((0,), (0,)), ((), ())), preferred_element_type=F32)
+
+
+def gelu(v):
+    return v * (0.5 + 0.5 * jnp.tanh(v * (GELU_C + GELU_C * 0.044715 * (v * v))))
 
 
 def gelu_parts(v):
@@ -285,9 +289,15 @@
 
 
 class Column:
-    def __init__(self, shard, column, send, recv, local):
+    def __init__(self, shard, column, other, send, recv, local, xsend, xrecv):
         self.z, self.x, self.y, self.c = coords()
-        self.shard, self.column, self.send, self.recv, self.local = shard, column, send, recv, local
+        self.shard, self.column, self.other = shard, column, other
+        self.send, self.recv, self.local, self.xsend, self.xrecv = send, recv, local, xsend, xrecv
+
+    @staticmethod
+    def semaphores():
+        dma = pltpu.SemaphoreType.DMA
+        return [dma((2, NZ)), dma((NZ,)), dma((1,)), dma((NZ,)), dma((NZ,))]
 
     def block(self, zb):
         rows = self.shard.shape[0]
@@ -308,6 +318,24 @@
             dev(to, self.x, self.y, self.c),
         )
 
+    def xcopy(self, zb, mine=False):
+        rows, width = self.shard.shape[0], self.shard.shape[1] // 2
+        part = rows // 2
+        start = pl.multiple_of(self.y * part, 16)
+        if mine:
+            source = self.shard.at[
+                pl.ds(start, part), pl.ds(pl.multiple_of(self.c * width, 128), width)
+            ]
+        else:
+            source = self.column.at[pl.ds(pl.multiple_of(zb * rows + start, 16), part), :]
+        return remote(
+            source,
+            self.other.at[pl.ds(pl.multiple_of(zb * part, 16), part), :],
+            self.xsend.at[zb],
+            self.xrecv.at[zb],
+            dev(self.z, 1 - self.x, self.y, self.c),
+        )
+
     def keep(self):
         return pltpu.make_async_copy(self.own(), self.block(self.z), self.local.at[0])
 
@@ -325,6 +353,7 @@
                 self.copy(self.z, side, True).start()
 
         self.keep().start()
+        self.xcopy(self.z, True).start()
 
     def take(self, step):
         for zb, exists, side in self.blocks(step):
@@ -338,6 +367,13 @@
                     def _():
                         self.copy(zb, side).start()
 
+    def push(self, step):
+        for zb, exists, _ in self.blocks(step):
+
+            @pl.when(exists)
+            def _():
+                self.xcopy(zb).start()
+
     def finish(self):
         for side in (1, 0):
 
@@ -353,18 +389,21 @@
                     self.copy(zb, side).wait_send()
 
         self.keep().wait()
+        for zb in range(NZ):
+            self.xcopy(zb).wait_recv()
+            self.xcopy(zb).wait_send()
 
 
 class Spread:
-    def __init__(self, column, full, xs, xr, ys, yr, cs, cr, local):
+    def __init__(self, column, other, full, ys, yr, cs, cr, local):
         self.z, self.x, self.y, self.c = coords()
-        self.column, self.full, self.local = column, full, local
-        self.xs, self.xr, self.ys, self.yr, self.cs, self.cr = xs, xr, ys, yr, cs, cr
+        self.column, self.other, self.full, self.local = column, other, full, local
+        self.ys, self.yr, self.cs, self.cr = ys, yr, cs, cr
 
     @staticmethod
     def semaphores():
         dma = pltpu.SemaphoreType.DMA
-        return [dma((NZ,))] * 4 + [dma((3, NZ))] * 2 + [dma((NZ,))]
+        return [dma((NZ,))] * 2 + [dma((3, NZ))] * 2 + [dma((2, NZ))]
 
     def cols(self, c):
         width = self.full.shape[3] // 2
@@ -374,58 +413,45 @@
         rows = self.full.shape[2] // 2
         return pl.ds(pl.multiple_of(y * rows, 16), rows)
 
-    def source(self, zb):
-        rows = self.full.shape[2]
-        return self.column.at[zb * rows : (zb + 1) * rows, :]
-
-    def source_half(self, zb):
-        rows = self.full.shape[2]
-        start = zb * rows + self.y * (rows // 2)
-        return self.column.at[pl.ds(pl.multiple_of(start, 16), rows // 2), :]
-
-    def xcopy(self, zb, came=False):
-        at = self.full.at[zb, 1 - self.x if came else self.x, self.half(self.y), self.cols(self.c)]
+    def source(self, kind, zb):
+        if kind == 0:
+            rows = self.full.shape[2]
+            return self.column.at[zb * rows : (zb + 1) * rows, :]
+        rows = self.full.shape[2] // 2
+        return self.other.at[zb * rows : (zb + 1) * rows, :]
+
+    def place(self, kind, zb, c):
+        if kind == 0:
+            return self.full.at[zb, self.x, :, self.cols(c)]
+        return self.full.at[zb, 1 - self.x, self.half(self.y if kind == 1 else 1 - self.y), self.cols(c)]
+
+    def ycopy(self, zb, came=False):
         return remote(
-            self.source_half(zb), at, self.xs.at[zb], self.xr.at[zb],
-            dev(self.z, 1 - self.x, self.y, self.c),
+            self.source(1, zb), self.place(2 if came else 1, zb, self.c), self.ys.at[zb], self.yr.at[zb],
+            dev(self.z, self.x, 1 - self.y, self.c),
         )
 
-    def ycopy(self, zb, came=False):
-        at = self.full.at[zb, 1 - self.x, self.half(1 - self.y if came else self.y), self.cols(self.c)]
+    def ccopy(self, kind, zb, came=False):
+        at = self.place(kind, zb, 1 - self.c if came else self.c)
         return remote(
-            at, at, self.ys.at[zb], self.yr.at[zb], dev(self.z, self.x, 1 - self.y, self.c)
-        )
-
-    def ccopy(self, kind, zb, came=False):
-        cols = self.cols(1 - self.c if came else self.c)
-        if kind == 0:
-            at = self.full.at[zb, self.x, :, cols]
-        else:
-            at = self.full.at[zb, 1 - self.x, self.half(self.y if kind == 1 else 1 - self.y), cols]
-        return remote(
-            self.source(zb) if kind == 0 else at, at, self.cs.at[kind, zb], self.cr.at[kind, zb],
+            at if kind == 2 else self.source(kind, zb), at, self.cs.at[kind, zb], self.cr.at[kind, zb],
             dev(self.z, self.x, self.y, 1 - self.c),
         )
 
-    def keep(self, zb):
+    def keep(self, kind, zb):
         return pltpu.make_async_copy(
-            self.source(zb), self.full.at[zb, self.x, :, self.cols(self.c)], self.local.at[zb]
+            self.source(kind, zb), self.place(kind, zb, self.c), self.local.at[kind, zb]
         )
 
     def begin(self):
         for zb in range(NZ):
-            self.xcopy(zb).start()
+            self.ycopy(zb).start()
 
     def near(self):
         for zb in range(NZ):
-            self.ccopy(0, zb).start()
-            self.keep(zb).start()
-
-    def take_x(self):
-        for zb in range(NZ):
-            self.xcopy(zb, True).wait_recv()
-            self.ycopy(zb).start()
-            self.ccopy(1, zb).start()
+            for kind in range(2):
+                self.ccopy(kind, zb).start()
+                self.keep(kind, zb).start()
 
     def take_y(self):
         for zb in range(NZ):
@@ -436,11 +462,11 @@
         for zb in range(NZ):
             for kind in range(3):
                 self.ccopy(kind, zb, True).wait_recv()
-            self.keep(zb).wait()
+            for kind in range(2):
+                self.keep(kind, zb).wait()
 
     def close(self):
         for zb in range(NZ):
-            self.xcopy(zb).wait_send()
             self.ycopy(zb).wait_send()
             for kind in range(3):
                 self.ccopy(kind, zb).wait_send()
@@ -505,9 +531,10 @@
     tok, cot, routes, cond, ada, adab, qvb, outb, soutb, sinb_s, router_s, bin_r, bout_r,
     qkv_s, out_s, sin_s, sout_s, win_h, wout_h,
     normed_o, proj_o, lsum_o, mixed_o, att_o, resid_o, second_o, gates_o, place_o, mod_o, bias_o, sinb_o, rt_o,
-    condt_o, rows, grads, res_o, qkv_o, outw_o, sin_o, sout_o, slopes_o, dwout_o,
-    pack, packs, sent, got, qkv, outw, sbuf, gbuf, win, wout, dwout, lows, slopes, acc,
-    s1, r1, s2, r2, ds0, dr0, ds1, dr1, wsem, osem, *gsems,
+    condt_o, res_o, bgr_o, ebias, qkv_o, outw_o, sin_o, sout_o, sin_x, sout_x, dwin_o, dwout_o,
+    pack, packs, sent, got, qkv, outw, sbuf, gbuf, rows, grads, far_rows, far_grads, win, wout, dwin, dwout,
+    lows, pres, acc, back,
+    s1, r1, s2, r2, ds0, dr0, ds1, dr1, wsem, osem, fsem, *gsems,
 ):
     z, x, y, c = coords()
     dp, ex = lax.axis_index("dp"), lax.axis_index("expert")
@@ -516,8 +543,11 @@
     hidden = win.shape[1]
     part = width // n
     per = width // 128
-    lead = Gather((qkv_s, out_s), (qkv, outw), (True, False), gsems[:-6])
-    later = (Column(sin_s, sin_o, *gsems[-6:-3]), Column(sout_s, sout_o, *gsems[-3:]))
+    lead = Gather((qkv_s, out_s), (qkv, outw), (True, False), gsems[:-10])
+    later = (
+        Column(sin_s, sin_o, sin_x, *gsems[-10:-5]),
+        Column(sout_s, sout_o, sout_x, *gsems[-5:]),
+    )
 
     loads = [
         pltpu.make_async_copy(win_h.at[x], win, wsem.at[0]),
@@ -566,8 +596,6 @@
     peers(lambda p: first(p, dp).start())
     lead.begin(0)
     lead.begin(1)
-    for column in later:
-        column.begin()
     for load in loads:
         load.start()
     packs[dp] = pack[...]
@@ -592,6 +620,9 @@
 
     for step in range(NZ):
         step_of(lead, step)
+
+    for column in later:
+        column.begin()
 
     bias_o[...] = jnp.zeros_like(bias_o)
     for p in range(n):
@@ -626,8 +657,6 @@
         lead.take_y(m, NZ - 1)
     for m in both_mats:
         lead.finish(m)
-    for column in later:
-        column.take(1)
     keep = [
         pltpu.make_async_copy(qkv, qkv_o, wsem.at[2]),
         pltpu.make_async_copy(outw, outw_o, wsem.at[3]),
@@ -708,48 +737,100 @@
     give_grads = PlaneExchange(gbuf, grads, ds1, dr1)
     give_grads.start()
     for column in later:
-        column.take(2)
+        column.take(1)
 
     first_x = x == 0
     acc[...] = jnp.zeros_like(acc) + jnp.where(first_x, bout_r[0:1, :], bout_r[1:2, :]).astype(F32)
     for load in loads:
         load.wait()
+    for column in later:
+        column.take(2)
     give_rows.wait_in()
+
+    end = jnp.logical_or(z == 0, z == NZ - 1)
+    inner = jnp.logical_not(end)
+    partner = dev(z + 1 - 2 * lax.rem(z, 2), x, y, c)
+
+    def far_copy(i):
+        source, target = ((rows, far_rows), (grads, far_grads))[i]
+        return remote(source, target, fsem.at[0, i], fsem.at[1, i], partner)
+
+    pl.when(end)(lambda: far_copy(0).start())
+    for column in later:
+        column.push(1)
 
     def span(f):
         return pl.ds(pl.multiple_of(f * CHUNK, 128), CHUNK)
 
-    def put_slope(f):
-        return pltpu.make_async_copy(slopes.at[:, span(f)], slopes_o.at[:, span(f)], osem.at[1, f])
+    def put_in(f):
+        return pltpu.make_async_copy(dwin.at[:, span(f)], dwin_o.at[:, span(f)], osem.at[1, f])
 
     def put_out(f):
         return pltpu.make_async_copy(dwout.at[span(f), :], dwout_o.at[span(f), :], osem.at[0, f])
 
+    def bias_of(cols):
+        return jnp.where(first_x, bin_r[0:1, cols], bin_r[1:2, cols]).astype(F32)
+
     def forward(f, carry):
         cols = span(f)
-        bias = jnp.where(first_x, bin_r[0:1, cols], bin_r[1:2, cols]).astype(F32)
-        act, slope = gelu_parts(dot(rows[...], win[:, cols]) + bias)
-        low = act.astype(B16)
+        pre = dot(rows[...], win[:, cols]) + bias_of(cols)
+        pres[:, cols] = pre
+        low = gelu(pre).astype(B16)
         lows[:, cols] = low
-        slopes[:, cols] = slope
-        put_slope(f).start()
         acc[...] += dot(low, wout[cols, :])
         return carry
 
     count = hidden // CHUNK
     lax.fori_loop(0, count, forward, 0)
     res_o[...] = acc[...].astype(B16)
+    for column in later:
+        column.push(2)
+        column.take(3)
+        column.push(3)
     give_grads.wait_in()
-    for column in later:
-        column.take(3)
-
-    def outer(f, carry):
+    pl.when(end)(lambda: far_copy(1).start())
+    back[...] = jnp.zeros_like(back)
+    ebias[...] = jnp.zeros_like(ebias)
+    column_sum = jnp.sum(grads[...].astype(F32), axis=0, keepdims=True)
+    for j in range(per):
+        at = hidden // 128 + j
+        ebias[at : at + 1, :] = column_sum[:, 128 * j : 128 * (j + 1)]
+
+    def backward(f, carry):
         cols = span(f)
-        dwout[cols, :] = dot_tn(lows[:, cols], grads[...]).astype(B16)
+        pre = (dot_nt(grads[...], wout[cols, :]) * gelu_parts(pres[:, cols])[1]).astype(B16)
+        back[...] += dot_nt(pre, win[:, cols])
+        col = jnp.sum(pre.astype(F32), axis=0, keepdims=True)
+        for j in range(CHUNK // 128):
+            ebias[pl.ds(f * (CHUNK // 128) + j, 1), :] = col[:, 128 * j : 128 * (j + 1)]
+
+        @pl.when(inner)
+        def _():
+            dwout[cols, :] = dot_tn(lows[:, cols], grads[...]).astype(B16)
+            dwin[:, cols] = dot_tn(rows[...], pre).astype(B16)
+
+        return carry
+
+    lax.fori_loop(0, count, backward, 0)
+    bgr_o[...] = back[...].astype(B16)
+
+    def far(f, carry):
+        cols = span(f)
+        data, grad = far_rows[...], far_grads[...]
+        act, slope = gelu_parts(dot(data, win[:, cols]) + bias_of(cols))
+        pre = (dot_nt(grad, wout[cols, :]) * slope).astype(B16)
+        dwout[cols, :] = (dwout[cols, :].astype(F32) + dot_tn(act.astype(B16), grad)).astype(B16)
         put_out(f).start()
+        dwin[:, cols] = (dwin[:, cols].astype(F32) + dot_tn(data, pre)).astype(B16)
+        put_in(f).start()
         return carry
 
-    lax.fori_loop(0, count, outer, 0)
+    @pl.when(inner)
+    def _():
+        far_copy(0).wait_recv()
+        far_copy(1).wait_recv()
+        lax.fori_loop(0, count, far, 0)
+
     for column in later:
         column.finish()
     for exchange in (give_rows, give_grads):
@@ -758,9 +839,17 @@
     peers(lambda p: second_hop(p, p).wait_send())
     for copy in keep:
         copy.wait()
-    for f in range(count):
-        put_slope(f).wait()
-        put_out(f).wait()
+
+    @pl.when(end)
+    def _():
+        far_copy(0).wait_send()
+        far_copy(1).wait_send()
+
+    @pl.when(inner)
+    def _():
+        for f in range(count):
+            put_out(f).wait()
+            put_in(f).wait()
 
 
 def lead_part(tok, cot, route, cond, ada, adab, qvb, outb, soutb, sinb, router, bin_r, bout_r, shards, win, wout):
@@ -773,6 +862,7 @@
     tiles = (ada.shape[1] // 128 + 7) // 8 * 8
     wide = [sds((n * s.shape[0], s.shape[1]), B16) for s in shards[:2]]
     wide += [sds((NZ * s.shape[0], s.shape[1] // 2), B16) for s in shards[2:]]
+    wide += [sds((NZ * s.shape[0] // 2, s.shape[1] // 2), B16) for s in shards[2:]]
     outs = [
         sds((length, width), B16),
         sds((length, 3 * width), B16),
@@ -790,9 +880,9 @@
         sds((8, 128), F32),
         sds((slots, width), B16),
         sds((slots, width), B16),
-        sds((slots, width), B16),
+        sds((32, 128), F32),
     ]
-    far = wide + [sds((slots, hidden), F32), sds((hidden, width), B16)]
+    far = wide + [sds((width, hidden), B16), sds((hidden, width), B16)]
     return pl.pallas_call(
         lead_kernel,
         out_shape=outs + far,
@@ -807,11 +897,17 @@
             vm(wide[1].shape, B16),
             vm((slots, width), B16),
             vm((slots, width), B16),
+            vm((slots, width), B16),
+            vm((slots, width), B16),
+            vm((slots, width), B16),
+            vm((slots, width), B16),
             vm((width, hidden), B16),
             vm((hidden, width), B16),
+            vm((width, hidden), B16),
             vm((hidden, width), B16),
             vm((slots, hidden), B16),
             vm((slots, hidden), F32),
+            vm((slots, width), F32),
             vm((slots, width), F32),
             dma((n,)),
             dma((n,)),
@@ -819,86 +915,49 @@
             dma((n,)),
         ]
         + [dma((E,))] * 4
-        + [dma((4,)), dma((2, hidden // CHUNK))]
+        + [dma((4,)), dma((2, hidden // CHUNK)), dma((2, 2))]
         + Gather.semaphores(2)
-        + [dma((2, NZ)), dma((NZ,)), dma((1,))] * 2,
+        + Column.semaphores()
+        + Column.semaphores(),
         compiler_params=params(1),
         name="front_and_expert",
     )(tok, cot, route, cond, ada, adab, qvb, outb, soutb, sinb, router, bin_r, bout_r, *shards, win, wout)
 
 
-def expert_back_kernel(which, rows, grads, slopes, win, wout, dwin, bgr, ebias, back):
-    f = pl.program_id(0)
-    last = pl.num_programs(0) - 1
-    width, chunk = rows.shape[1], slopes.shape[1]
-    tiles = chunk // 128
-
-    @pl.when(f == 0)
-    def _():
-        back[...] = jnp.zeros_like(back)
-        ebias[...] = jnp.zeros_like(ebias)
-        column = jnp.sum(grads[...].astype(F32), axis=0, keepdims=True)
-        for j in range(width // 128):
-            ebias[pl.ds((last + 1) * tiles + j, 1), :] = column[:, 128 * j : 128 * (j + 1)]
-
-    pre = (dot_nt(grads[...], wout[0]) * slopes[...]).astype(B16)
-    dwin[...] = dot_tn(rows[...], pre).astype(B16)
-    back[...] += dot_nt(pre, win[0])
-    col = jnp.sum(pre.astype(F32), axis=0, keepdims=True)
-    for j in range(tiles):
-        ebias[pl.ds(f * tiles + j, 1), :] = col[:, 128 * j : 128 * (j + 1)]
-
-    @pl.when(f == last)
-    def _():
-        bgr[...] = back[...].astype(B16)
-
-
-def expert_back(which, rows, grads, slopes, win, wout):
-    slots, width = rows.shape
-    hidden = slopes.shape[1]
-    whole = lambda f, w: (0, 0)
-    return pl.pallas_call(
-        expert_back_kernel,
-        out_shape=[sds((width, hidden), B16), sds((slots, width), B16), sds((32, 128), F32)],
-        grid_spec=pltpu.PrefetchScalarGridSpec(
-            num_scalar_prefetch=1,
-            grid=(hidden // CHUNK,),
-            in_specs=[
-                pl.BlockSpec((slots, width), whole),
-                pl.BlockSpec((slots, width), whole),
-                pl.BlockSpec((slots, CHUNK), lambda f, w: (0, f)),
-                pl.BlockSpec((1, width, CHUNK), lambda f, w: (w[0], 0, f)),
-                pl.BlockSpec((1, CHUNK, width), lambda f, w: (w[0], f, 0)),
-            ],
-            out_specs=[
-                pl.BlockSpec((width, CHUNK), lambda f, w: (0, f)),
-                pl.BlockSpec((slots, width), whole),
-                pl.BlockSpec((32, 128), whole),
-            ],
-            scratch_shapes=[pltpu.VMEM((slots, width), F32)],
-        ),
-        compiler_params=params(),
-        name="expert_back",
-    )(which, rows, grads, slopes, win, wout)
-
-
 def middle_kernel(
-    res, bgr, second_r, resid_r, att_r, cot, mod, sin_c, sout_c, sinb, bias, router, gates_r, place_r,
+    res, bgr, dwout, second_r, resid_r, att_r, cot, mod, sin_c, sout_c, sin_x, sout_x, sinb, bias, router, gates_r, place_r,
     mixed, outw,
-    out_o, rgrad_o, mgrad_o, dsin, dsout, dout, drouter, vecs, mg2,
-    ret, retg, shared, sgrad, sin, sout, send, recv, send2, recv2, *ssems,
+    came_o, out_o, rgrad_o, mgrad_o, sin_half, sout_half, dout, drouter, vecs, mg2,
+    dsin, dsout, hsem, msem, lows, slopes, ret, retg, shared, sgrad, sin, sout, send, recv, send2, recv2, *ssems,
 ):
     barrier = pltpu.get_barrier_semaphore()
     for k in range(1, E):
         greet(barrier, plane_peer(k)[0])
-    pl.semaphore_wait(barrier, E - 1)
+    z, x, y, c = coords()
+    mate = NZ - 1 - z
+    greet(barrier, dev(mate, x, y, c))
+    pl.semaphore_wait(barrier, E)
+    central = jnp.logical_and(z > 0, z < NZ - 1)
+
+    def across(i):
+        block = mate + 1 - 2 * lax.rem(mate, 2) if i == 0 else mate
+        return remote(
+            dwout.at[block], came_o.at[i], msem.at[0, i], msem.at[1, i], dev(mate, x, y, c)
+        )
+
+    @pl.when(central)
+    def _():
+        across(0).start()
+        across(1).start()
+
     count = len(ssems) // 2
-    spreads = (Spread(sin_c, sin, *ssems[:count]), Spread(sout_c, sout, *ssems[count:]))
+    spreads = (
+        Spread(sin_c, sin_x, sin, *ssems[:count]),
+        Spread(sout_c, sout_x, sout, *ssems[count:]),
+    )
     for spread in spreads:
         spread.begin()
     gives = (PlaneExchange(res, ret, send, recv), PlaneExchange(bgr, retg, send2, recv2))
-    for give in gives:
-        give.start()
     for spread in spreads:
         spread.near()
     length, width = second_r.shape
@@ -911,21 +970,33 @@
     shared[...] = jnp.zeros_like(shared) + bias[3:4, :]
     sgrad[...] = jnp.zeros_like(sgrad)
     vecs[...] = jnp.zeros_like(vecs)
-    for spread in spreads:
-        spread.take_x()
-    for spread in spreads:
-        spread.take_y()
-    for spread in spreads:
-        spread.finish()
+    spreads[0].take_y()
+    for give in gives:
+        give.start()
+    spreads[0].finish()
+
+    def span(f):
+        return pl.ds(pl.multiple_of(f * chunk, 128), chunk)
+
+    def forward(f, carry):
+        cols = span(f)
+        w1 = sin[:, :, :, cols].reshape(width, chunk)
+        act, slope = gelu_parts(dot(second, w1) + sinb[:, cols])
+        lows[:, cols] = act.astype(B16)
+        slopes[:, cols] = slope
+        return carry
+
+    lax.fori_loop(0, hidden // chunk, forward, 0)
+    spreads[1].take_y()
+    spreads[1].finish()
 
     def body(f, carry):
-        cols = pl.ds(pl.multiple_of(f * chunk, 128), chunk)
+        cols = span(f)
         w1 = sin[:, :, :, cols].reshape(width, chunk)
         w2 = sout[f].reshape(chunk, width)
-        act, slope = gelu_parts(dot(second, w1) + sinb[:, cols])
-        low = act.astype(B16)
+        low = lows[:, cols]
         shared[...] += dot(low, w2)
-        pre = (dot_nt(moe_low, w2) * slope).astype(B16)
+        pre = (dot_nt(moe_low, w2) * slopes[:, cols]).astype(B16)
         dsout[cols, :] = dot_tn(low, moe_low).astype(B16)
         dsin[:, cols] = dot_tn(second, pre).astype(B16)
         sgrad[...] += dot_nt(pre, w1)
@@ -935,6 +1006,20 @@
         return carry
 
     lax.fori_loop(0, hidden // chunk, body, 0)
+    halves = ((dsin, sin_half), (dsout, sout_half))
+
+    def half_cols(i, core):
+        size = halves[i][1].shape[1]
+        return pl.ds(pl.multiple_of(core * size, 128), size)
+
+    def half_copy(i):
+        return remote(
+            halves[i][0].at[:, half_cols(i, 1 - c)], halves[i][1], hsem.at[0, i], hsem.at[1, i],
+            dev(z, x, y, 1 - c),
+        )
+
+    for i in range(2):
+        half_copy(i).start()
     lane = lax.broadcasted_iota(jnp.int32, (length, E), 1)
     gates = [gates_r[:, k : k + 1] for k in range(2)]
     maps = [
@@ -980,6 +1065,24 @@
         for j in range(width // 128):
             at = base + i * (width // 128) + j
             vecs[at : at + 1, :] = row[:, 128 * j : 128 * (j + 1)]
+    for i in range(2):
+        half_copy(i).wait_recv()
+        whole, part = halves[i]
+        step = part.shape[0] // 16
+
+        def add(j, carry):
+            at = pl.ds(pl.multiple_of(j * step, 16), step)
+            own = whole[at, half_cols(i, c)].astype(F32)
+            part[at, :] = (part[at, :].astype(F32) + own).astype(B16)
+            return carry
+
+        lax.fori_loop(0, 16, add, 0)
+        half_copy(i).wait_send()
+    @pl.when(central)
+    def _():
+        across(0).wait()
+        across(1).wait()
+
     for give in gives:
         give.wait_out()
     for spread in spreads:
@@ -987,26 +1090,33 @@
 
 
 def middle(*args):
-    res, second, sin = args[0], args[2], args[7]
+    res, dwout, second, sin = args[0], args[2], args[3], args[8]
     length, width = second.shape
     rows, hidden = res.shape[0], 2 * sin.shape[1]
     dma = pltpu.SemaphoreType.DMA
     return pl.pallas_call(
         middle_kernel,
         out_shape=[
+            sds((2,) + dwout.shape[1:], B16),
             sds((length, width), B16),
             sds((length, width), F32),
             sds((length, width), B16),
-            sds((width, hidden), B16),
-            sds((hidden, width), B16),
+            sds((width, hidden // 2), B16),
+            sds((hidden, width // 2), B16),
             sds((width, width), B16),
             sds((E, width), F32),
             sds((40, 128), F32),
             sds((8, width), F32),
         ],
-        in_specs=[VM] * 7 + [HB] * 2 + [VM] * 7,
-        out_specs=[VM] * 9,
+        in_specs=[VM] * 2 + [HB] + [VM] * 5 + [HB] * 4 + [VM] * 7,
+        out_specs=[HB] + [VM] * 9,
         scratch_shapes=[
+            pltpu.VMEM((width, hidden), B16),
+            pltpu.VMEM((hidden, width), B16),
+            dma((2, 2)),
+            dma((2, 2)),
+            pltpu.VMEM((length, hidden), B16),
+            pltpu.VMEM((length, hidden), F32),
             pltpu.VMEM((rows, width), B16),
             pltpu.VMEM((rows, width), B16),
             pltpu.VMEM((length, width), F32),
@@ -1025,81 +1135,6 @@
     )(*args)
 
 
-def back_kernel(
-    tok, mod, normed, proj, lsum, mgrad, rgrad, qkv, mg2,
-    tgrad_o, dqkv, qvec, mgt,
-    pgrad,
-):
-    length, width = tok.shape
-    low_lane = lax.broadcasted_iota(jnp.int32, (length, 128), 1) < HEAD_DIM
-    for p in range(HEADS // 2):
-        q2 = proj[:, 128 * p : 128 * (p + 1)]
-        k2 = proj[:, width + 128 * p : width + 128 * (p + 1)]
-        v2 = proj[:, 2 * width + 128 * p : 2 * width + 128 * (p + 1)]
-        m2 = mgrad[:, 128 * p : 128 * (p + 1)]
-        parts = []
-        for h in range(2):
-            mine = low_lane if h == 0 else jnp.logical_not(low_lane)
-            zero = jnp.zeros_like(q2)
-            s = dot_nt(jnp.where(mine, q2, zero), k2) * SCALE
-            prob = jnp.exp(s - lsum[:, 2 * p + h : 2 * p + h + 1])
-            pg = dot_nt(jnp.where(mine, m2, zero), v2)
-            inner = jnp.sum(prob * pg, axis=-1, keepdims=True)
-            sg = (prob * (pg - inner)).astype(B16)
-            parts.append(
-                (dot(sg, k2) * SCALE, dot_tn(sg, q2) * SCALE, dot_tn(prob.astype(B16), m2))
-            )
-        for i in range(3):
-            pgrad[:, i * width + 128 * p : i * width + 128 * (p + 1)] = jnp.where(
-                low_lane, parts[0][i], parts[1][i]
-            ).astype(B16)
-    ngrad = dot_nt(pgrad[...], qkv[...])
-    for i in range(3):
-        dqkv[:, i * width : (i + 1) * width] = dot_tn(
-            normed[...], pgrad[:, i * width : (i + 1) * width]
-        ).astype(B16)
-    per = width // 128
-    for i, k in enumerate((0, 2)):
-        row = jnp.sum(pgrad[:, k * width : (k + 1) * width].astype(F32), axis=0, keepdims=True)
-        for j in range(per):
-            qvec[i * per + j : i * per + j + 1, :] = row[:, 128 * j : 128 * (j + 1)]
-    for j in range(2 * per, qvec.shape[0]):
-        qvec[j : j + 1, :] = jnp.zeros((1, 128), F32)
-    n1, r1 = norm_parts(tok[...].astype(F32))
-    tgrad_o[...] = rgrad[...] + norm_back(ngrad * (1.0 + mod[1:2]), n1, r1)
-    rows = [
-        jnp.sum(ngrad, axis=0, keepdims=True),
-        jnp.sum(ngrad * n1, axis=0, keepdims=True),
-    ] + [mg2[i : i + 1, :] for i in range(2, 6)]
-    mgt[...] = jnp.zeros_like(mgt)
-    for i, row in enumerate(rows):
-        row = row.astype(B16).astype(F32)
-        for j in range(per):
-            mgt[i * per + j : i * per + j + 1, :] = row[:, 128 * j : 128 * (j + 1)]
-
-
-def back(*args):
-    tok, qkv = args[0], args[7]
-    length, width = tok.shape
-    return pl.pallas_call(
-        back_kernel,
-        out_shape=[
-            sds((length, width), F32),
-            sds(qkv.shape, B16),
-            sds((16, 128), F32),
-            sds((48, 128), F32),
-        ],
-        in_specs=[VM] * 9,
-        out_specs=[VM] * 4,
-        scratch_shapes=[pltpu.VMEM((length, 3 * width), B16)],
-        compiler_params=params(),
-        name="attention_back",
-    )(*args)
-
-
-PIECES = ((2, 0, 2, True), (3, 0, 1, False), (0, 0, 1, True), (2, 1, 2, False), (1, 0, 1, True))
-
-
 def add_into(target, source, lead):
     count = 1
     for n in lead:
@@ -1118,30 +1153,43 @@
     lax.fori_loop(0, count, body, 0)
 
 
-class Reduce:
-    def __init__(self, grad, out, col, width, y_first, bufs, sems):
+class Piece:
+    def __init__(self, spec, grad, out, bufs):
         self.z, self.x, self.y, self.c = coords()
-        self.grad, self.out, self.width, self.y_first = grad, out, width, y_first
-        self.half = grad.shape[-1] // 2
-        self.col = col
-        self.cbuf, self.lbuf, self.ebuf, self.fbuf, self.zin = bufs
-        self.one, self.zsem = sems
+        self.half, self.row, self.rows, self.col, self.width, self.y_first = spec
+        self.grad, self.out = grad, out
+        self.size = out.shape[-1] // 2
+        if not self.half:
+            self.cbuf, bufs = bufs[0], bufs[1:]
+        self.ebuf, self.fbuf, self.zin, self.one, self.zsem = bufs
 
     @staticmethod
-    def scratch(rows, width):
+    def scratch(spec):
+        half, _, rows, _, width, _ = spec
         vm = lambda *lead: pltpu.VMEM(lead + (rows, width), B16)
-        return [
-            vm(NZ, NX, 2),
-            vm(NZ, NX, 2),
+        dma = pltpu.SemaphoreType.DMA
+        return ([] if half else [vm(NZ, NX, 2)]) + [
             vm(NZ, 2),
             vm(NZ),
             vm(NZ),
-            pltpu.SemaphoreType.DMA((14,)),
-            pltpu.SemaphoreType.DMA((2, NZ)),
+            dma((13,)),
+            dma((2, NZ)),
         ]
 
     def cols(self, c):
-        return pl.ds(pl.multiple_of(c * self.half + self.col, 128), self.width)
+        return pl.ds(pl.multiple_of(c * self.size + self.col, 128), self.width)
+
+    def core_view(self, *lead):
+        if not self.half:
+            return self.cbuf.at[lead]
+        inner = (slice(self.row, self.row + self.rows), slice(self.col, self.col + self.width))
+        return self.grad.at[lead + inner]
+
+    def core_value(self, *lead):
+        if not self.half:
+            return self.cbuf[lead]
+        inner = (slice(self.row, self.row + self.rows), slice(self.col, self.col + self.width))
+        return self.grad[lead + inner]
 
     def core_copy(self):
         return remote(
@@ -1152,23 +1200,25 @@
             dev(self.z, self.x, self.y, 1 - self.c),
         )
 
-    def load(self):
-        return pltpu.make_async_copy(
-            self.grad.at[:, :, :, :, self.cols(self.c)], self.lbuf, self.one.at[2]
-        )
+    def to_x(self):
+        return dev(self.z, 1 - self.x, self.y, self.c)
+
+    def to_y(self):
+        return dev(self.z, self.x, 1 - self.y, self.c)
 
     def copy1(self):
+        every = slice(None)
         if self.y_first:
-            source, to = self.cbuf.at[:, :, 1 - self.y], dev(self.z, self.x, 1 - self.y, self.c)
+            source, to = self.core_view(every, every, 1 - self.y), self.to_y()
         else:
-            source, to = self.cbuf.at[:, 1 - self.x], dev(self.z, 1 - self.x, self.y, self.c)
+            source, to = self.core_view(every, 1 - self.x, every), self.to_x()
         return remote(source, self.ebuf, self.one.at[3], self.one.at[4], to)
 
     def copy2(self):
         if self.y_first:
-            source, to = self.ebuf.at[:, 1 - self.x], dev(self.z, 1 - self.x, self.y, self.c)
+            source, to = self.ebuf.at[:, 1 - self.x], self.to_x()
         else:
-            source, to = self.ebuf.at[:, 1 - self.y], dev(self.z, self.x, 1 - self.y, self.c)
+            source, to = self.ebuf.at[:, 1 - self.y], self.to_y()
         return remote(source, self.fbuf, self.one.at[5], self.one.at[6], to)
 
     def zcopy(self, zb, at):
@@ -1191,41 +1241,38 @@
         return self.fbuf.at[self.z]
 
     def place(self, y, c):
-        return self.out.at[y, :, self.cols(c)]
+        return self.out.at[y, self.row : self.row + self.rows, self.cols(c)]
 
     def keep(self):
         return pltpu.make_async_copy(self.own(), self.place(self.y, self.c), self.one.at[7])
 
-    def give_y(self):
-        return remote(
-            self.own(), self.place(self.y, self.c), self.one.at[8], self.one.at[9],
-            dev(self.z, self.x, 1 - self.y, self.c),
-        )
-
-    def give_c(self):
-        return remote(
-            self.own(), self.place(self.y, self.c), self.one.at[10], self.one.at[11],
-            dev(self.z, self.x, self.y, 1 - self.c),
-        )
-
-    def pass_c(self):
-        here = self.place(1 - self.y, self.c)
-        return remote(
-            here, here, self.one.at[12], self.one.at[13], dev(self.z, self.x, self.y, 1 - self.c)
-        )
+    def give_y(self, came=False):
+        at = self.place(1 - self.y if came else self.y, self.c)
+        return remote(self.own(), at, self.one.at[8], self.one.at[9], self.to_y())
+
+    def give_c(self, came=False):
+        at = self.place(self.y, 1 - self.c if came else self.c)
+        to = dev(self.z, self.x, self.y, 1 - self.c)
+        return remote(self.own(), at, self.one.at[10], self.one.at[11], to)
+
+    def pass_c(self, came=False):
+        at = self.place(1 - self.y, 1 - self.c if came else self.c)
+        to = dev(self.z, self.x, self.y, 1 - self.c)
+        return remote(at, at, self.one.at[12], self.one.at[2], to)
 
     def stage(self, s):
         if s == 0:
-            self.core_copy().wait_recv()
-            self.load().wait()
-            add_into(self.cbuf, lambda i: self.lbuf[i], (NZ, NX, 2))
+            if not self.half:
+                self.core_copy().wait_recv()
+                mine = self.cols(self.c)
+                add_into(self.cbuf, lambda i: self.grad[i[0], i[1], i[2], :, mine], (NZ, NX, 2))
             self.copy1().start()
         elif s == 1:
             self.copy1().wait_recv()
             if self.y_first:
-                add_into(self.ebuf, lambda i: self.cbuf[i[0], i[1], self.y], (NZ, NX))
+                add_into(self.ebuf, lambda i: self.core_value(i[0], i[1], self.y), (NZ, NX))
             else:
-                add_into(self.ebuf, lambda i: self.cbuf[i[0], self.x, i[1]], (NZ, 2))
+                add_into(self.ebuf, lambda i: self.core_value(i[0], self.x, i[1]), (NZ, 2))
             self.copy2().start()
         elif s == 2:
             self.copy2().wait_recv()
@@ -1243,13 +1290,14 @@
             self.give_c().start()
             self.keep().start()
         elif s == 4:
-            self.give_y_in().wait_recv()
+            self.give_y(True).wait_recv()
             self.pass_c().start()
         elif s == 5:
             self.keep().wait()
-            self.give_c_in().wait_recv()
-            self.pass_c_in().wait_recv()
-            self.core_copy().wait_send()
+            self.give_c(True).wait_recv()
+            self.pass_c(True).wait_recv()
+            if not self.half:
+                self.core_copy().wait_send()
             self.copy1().wait_send()
             self.copy2().wait_send()
             self.give_y().wait_send()
@@ -1257,38 +1305,161 @@
             self.pass_c().wait_send()
             self.others(lambda zb: self.zcopy(zb, zb).wait_send())
 
-    def give_y_in(self):
+
+class MidSum:
+    COUNT = 6
+
+    def __init__(self, grad, into, out, total, outer, sems):
+        self.z, self.x, self.y, self.c = coords()
+        self.grad, self.into, self.out, self.total, self.outer = grad, into, out, total, outer
+        self.sems = sems
+        self.size = grad.shape[2] // self.COUNT
+        self.inner = jnp.logical_and(self.z > 0, self.z < NZ - 1)
+        self.end = jnp.logical_not(self.inner)
+        self.mate = NZ - 1 - self.z
+
+    @staticmethod
+    def scratch(shape):
+        vm = pltpu.VMEM
+        return [vm(shape[1:], B16), vm(shape[1:], B16), pltpu.SemaphoreType.DMA((9, MidSum.COUNT))]
+
+    def cols(self, p):
+        return slice(p * self.size, (p + 1) * self.size)
+
+    @staticmethod
+    def beside(z):
+        return z + 1 - 2 * lax.rem(z, 2)
+
+    def across(self, i, p):
+        block = self.beside(self.mate) if i == 0 else self.mate
         return remote(
-            self.own(), self.place(1 - self.y, self.c), self.one.at[8], self.one.at[9],
-            dev(self.z, self.x, 1 - self.y, self.c),
+            self.grad.at[block, :, self.cols(p)],
+            self.into.at[i, :, self.cols(p)],
+            self.sems.at[i, p],
+            self.sems.at[2 + i, p],
+            dev(self.mate, self.x, self.y, self.c),
         )
 
-    def give_c_in(self):
+    def outward(self, p):
         return remote(
-            self.own(), self.place(self.y, 1 - self.c), self.one.at[10], self.one.at[11],
-            dev(self.z, self.x, self.y, 1 - self.c),
+            self.outer.at[:, self.cols(p)],
+            self.total.at[:, self.cols(p)],
+            self.sems.at[4, p],
+            self.sems.at[5, p],
+            dev(self.beside(self.z), self.x, self.y, self.c),
         )
 
-    def pass_c_in(self):
-        here = self.place(1 - self.y, 1 - self.c)
+    def begin(self, i, p):
+        pl.when(self.inner)(lambda: self.across(i, p).start())
+
+    def give(self, p, sent=True):
+        @pl.when(self.inner)
+        def _():
+            if sent:
+                self.across(0, p).wait_recv()
+            cols = self.cols(p)
+            self.outer[:, cols] = (
+                self.grad[self.beside(self.z), :, cols].astype(F32) + self.into[0, :, cols].astype(F32)
+            ).astype(B16)
+            self.outward(p).start()
+
+    def swap(self, p, came=False):
+        part = self.total.shape[0] // NX
+        start = pl.multiple_of((1 - self.x) * part, 16)
         return remote(
-            here, here, self.one.at[12], self.one.at[13], dev(self.z, self.x, self.y, 1 - self.c)
+            self.total.at[pl.ds(start, part), self.cols(p)],
+            self.out.at[1 - self.x if came else self.x, :, self.cols(p)],
+            self.sems.at[6, p],
+            self.sems.at[7, p],
+            dev(self.z, 1 - self.x, self.y, self.c),
         )
 
-    STAGES = 6
-
-
-def sums_kernel(*refs):
-    grads = refs[:4]
-    mine_out = refs[4]
-    vecs, qvec, drouter, ebias, mgt, condt, ada = refs[5:12]
-    outs = refs[12:16]
-    pair_out = refs[16]
-    small, esum, tiles, cgot = refs[17:21]
-    rest = list(refs[21:])
+    def keep(self, p):
+        part = self.total.shape[0] // NX
+        start = pl.multiple_of(self.x * part, 16)
+        return pltpu.make_async_copy(
+            self.total.at[pl.ds(start, part), self.cols(p)],
+            self.out.at[self.x, :, self.cols(p)],
+            self.sems.at[8, p],
+        )
+
+    def final(self, p, sent=True):
+        @pl.when(self.inner)
+        def _():
+            if sent:
+                self.across(1, p).wait_recv()
+            cols = self.cols(p)
+            self.total[:, cols] = (
+                self.grad[self.z, :, cols].astype(F32) + self.into[1, :, cols].astype(F32)
+            ).astype(B16)
+
+        pl.when(self.end)(lambda: self.outward(p).wait_recv())
+        self.swap(p).start()
+        self.keep(p).start()
+
+    def close(self, sent=True):
+        for p in range(self.COUNT):
+
+            @pl.when(self.inner)
+            def _():
+                self.outward(p).wait_send()
+                if sent:
+                    self.across(0, p).wait_send()
+                    self.across(1, p).wait_send()
+
+            self.swap(p, True).wait_recv()
+            self.swap(p).wait_send()
+            self.keep(p).wait()
+
+
+def piece_specs(width, hidden):
+    rows, tall = width // NZ // 4, hidden // NZ // 4
+    qkv = 3 * width // 2
+    left = (qkv // 128 + 1) // 2 * 128
+    early = (
+        (2, (True, 0, rows, 0, hidden // 4, True)),
+        (3, (True, 0, tall // 2, 0, width // 2, False)),
+        (2, (True, 0, rows, hidden // 4, hidden // 4, False)),
+        (3, (True, tall // 2, tall // 2, 0, width // 2, True)),
+    )
+    late = (
+        (0, (False, 0, rows, 0, left, True)),
+        (0, (False, 0, rows, left, qkv - left, False)),
+        (1, (False, 0, rows, 0, width // 2, False)),
+    )
+    return early, late
+
+
+def tail_kernel(*refs):
+    sin_half, sout_half, dout, dwin, dwout, dwout_came = refs[:6]
+    tok, mod, normed, proj, lsum, mgrad, rgrad, qkv, mg2, vecs, drouter, ebias, condt, ada = refs[6:20]
+    outs = refs[20:24]
+    pair_in, pair_out, tgrad_o, small, esum, tiles, cgot = refs[24:31]
+    rest = list(refs[31:])
     z, x, y, c = coords()
     dp, ex = lax.axis_index("dp"), lax.axis_index("expert")
     n = NZ * NX
+    length, width = tok.shape
+    per = width // 128
+    early_specs, late_specs = piece_specs(width, 2 * sin_half.shape[4])
+    dqkv, pgrad = rest[:2]
+    rest = rest[2:]
+    sources = (dqkv, dout, sin_half, sout_half)
+
+    def make(specs, rest):
+        made = []
+        for matrix, spec in specs:
+            count = len(Piece.scratch(spec))
+            made.append(Piece(spec, sources[matrix], outs[matrix], rest[:count]))
+            rest = rest[count:]
+        return made, rest
+
+    early, rest = make(early_specs, rest)
+    late, rest = make(late_specs, rest)
+    wide = MidSum(dwin, rest[0], pair_in, *rest[1:4])
+    tall = MidSum(dwout, dwout_came, pair_out, *rest[4:7])
+    rest = rest[7:]
+    ssum, sgot, zgot, esend, egot, mine, csend, sems, dsem, zsem, tsem = rest
 
     barrier = pltpu.get_barrier_semaphore()
 
@@ -1305,38 +1476,54 @@
         greet(barrier, mate)
     pl.semaphore_wait(barrier, n - 1 + 3)
 
-    plans = []
-    for matrix, part, share, y_first in PIECES:
-        grad = grads[matrix]
-        width = grad.shape[-1] // 2 // share
-        plans.append(
-            Reduce(grad, outs[matrix], part * width, width, y_first, rest[:5], rest[5:7])
-        )
-        rest = rest[7:]
-    ssum, sgot, zgot, esend, egot, mine, csend, sems, dsem, zsem, tsem, wsem = rest
-
-    for plan in plans:
-        plan.core_copy().start()
-        plan.load().start()
-
-    def swap():
-        return remote(
-            mine_out.at[1 - x], pair_out.at[x], wsem.at[0], wsem.at[1], dev(z, 1 - x, y, c)
-        )
-
-    def swap_in():
-        return remote(
-            mine_out.at[1 - x], pair_out.at[1 - x], wsem.at[0], wsem.at[1], dev(z, 1 - x, y, c)
-        )
-
-    swap().start()
-    swap_keep = pltpu.make_async_copy(mine_out.at[x], pair_out.at[x], wsem.at[2])
-    swap_keep.start()
+    every = range(MidSum.COUNT)
+    for i in range(2):
+        for p in every:
+            wide.begin(i, p)
+    for piece in early:
+        piece.stage(0)
+    late[2].core_copy().start()
+    for p in every:
+        tall.give(p, False)
+
+    low_lane = lax.broadcasted_iota(jnp.int32, (length, 128), 1) < HEAD_DIM
+    for p in range(HEADS // 2):
+        q2 = proj[:, 128 * p : 128 * (p + 1)]
+        k2 = proj[:, width + 128 * p : width + 128 * (p + 1)]
+        v2 = proj[:, 2 * width + 128 * p : 2 * width + 128 * (p + 1)]
+        m2 = mgrad[:, 128 * p : 128 * (p + 1)]
+        parts = []
+        for h in range(2):
+            head = low_lane if h == 0 else jnp.logical_not(low_lane)
+            zero = jnp.zeros_like(q2)
+            s = dot_nt(jnp.where(head, q2, zero), k2) * SCALE
+            prob = jnp.exp(s - lsum[:, 2 * p + h : 2 * p + h + 1])
+            pg = dot_nt(jnp.where(head, m2, zero), v2)
+            inner = jnp.sum(prob * pg, axis=-1, keepdims=True)
+            sg = (prob * (pg - inner)).astype(B16)
+            parts.append(
+                (dot(sg, k2) * SCALE, dot_tn(sg, q2) * SCALE, dot_tn(prob.astype(B16), m2))
+            )
+        for i in range(3):
+            pgrad[:, i * width + 128 * p : i * width + 128 * (p + 1)] = jnp.where(
+                low_lane, parts[0][i], parts[1][i]
+            ).astype(B16)
+    lead = dqkv.shape[:4]
+    for i in range(3):
+        cols = slice(i * width, (i + 1) * width)
+        dqkv[:, :, :, :, cols] = dot_tn(normed[...], pgrad[:, cols]).astype(B16).reshape(lead + (width,))
+    for piece in late[:2]:
+        piece.core_copy().start()
 
     rows = vecs.shape[0]
     ssum[0:rows, :] = vecs[...]
-    ssum[rows : rows + 16, :] = qvec[...]
-    per = drouter.shape[1] // 128
+    for i, k in enumerate((0, 2)):
+        row = jnp.sum(pgrad[:, k * width : (k + 1) * width].astype(F32), axis=0, keepdims=True)
+        for j in range(per):
+            at = rows + i * per + j
+            ssum[at : at + 1, :] = row[:, 128 * j : 128 * (j + 1)]
+    for at in range(rows + 2 * per, rows + 16):
+        ssum[at : at + 1, :] = jnp.zeros((1, 128), F32)
     for b in range(per):
         ssum[rows + 16 + 8 * b : rows + 24 + 8 * b, :] = drouter[:, 128 * b : 128 * (b + 1)]
     hops = (dev(z, x, y, 1 - c), dev(z, x, 1 - y, c), dev(z, 1 - x, y, c))
@@ -1344,22 +1531,18 @@
     def hop(i):
         return remote(zgot.at[4 + i], sgot.at[i], sems.at[0, i], sems.at[1, i], hops[i])
 
-    def ehop():
-        return remote(esend.at[x], egot.at[z, x], sems.at[0, 3], sems.at[1, 3], hops[2])
-
-    def ehop_in():
-        return remote(esend.at[x], egot.at[z, 1 - x], sems.at[0, 3], sems.at[1, 3], hops[2])
-
-    mine[0:40, :] = mgt[0:40, :]
-    mine[40:48, :] = condt[...]
+    def ehop(came=False):
+        return remote(
+            esend.at[x], egot.at[z, 1 - x if came else x], sems.at[0, 3], sems.at[1, 3], hops[2]
+        )
 
     def tile(p, at):
         return remote(mine, tiles.at[ex, at], dsem.at[0, p], dsem.at[1, at], (p, ex))
 
     def spread(i, theirs=False):
         e2 = 2 * (1 - y if i != 1 else y) + (1 - c if i != 0 else c)
-        rows = tiles.at[e2 if theirs else ex]
-        return remote(rows, rows, tsem.at[0, i], tsem.at[1, i], mates[i])
+        block = tiles.at[e2 if theirs else ex]
+        return remote(block, block, tsem.at[0, i], tsem.at[1, i], mates[i])
 
     def cond_copy(p, at):
         return remote(csend.at[p], cgot.at[at], dsem.at[2, p], dsem.at[3, at], (p, ex))
@@ -1387,13 +1570,26 @@
         hop(i).wait()
         ssum[...] = ssum[...] + sgot[i]
 
-    def small0():
-        start_hop(0)
-        esend[x] = ebias[...]
-        egot[z, x] = ebias[...]
-        ehop().start()
-        peers(lambda p: tile(p, dp).start())
-        tiles[ex, dp] = mine[...]
+    start_hop(0)
+    esend[x] = ebias[...]
+    egot[z, x] = ebias[...]
+    ehop().start()
+
+    ngrad = dot_nt(pgrad[...], qkv[...])
+    n1, r1 = norm_parts(tok[...].astype(F32))
+    tgrad_o[...] = rgrad[...] + norm_back(ngrad * (1.0 + mod[1:2]), n1, r1)
+    mod_rows = [
+        jnp.sum(ngrad, axis=0, keepdims=True),
+        jnp.sum(ngrad * n1, axis=0, keepdims=True),
+    ] + [mg2[i : i + 1, :] for i in range(2, 6)]
+    mine[...] = jnp.zeros_like(mine)
+    for i, row in enumerate(mod_rows):
+        row = row.astype(B16).astype(F32)
+        for j in range(per):
+            mine[i * per + j : i * per + j + 1, :] = row[:, 128 * j : 128 * (j + 1)]
+    mine[40:48, :] = condt[...]
+    peers(lambda p: tile(p, dp).start())
+    tiles[ex, dp] = mine[...]
 
     def small1():
         end_hop(0)
@@ -1413,7 +1609,7 @@
         end_hop(1)
         start_hop(2)
         ehop().wait_send()
-        ehop_in().wait_recv()
+        ehop(True).wait_recv()
         lines(lambda zb: zexp(zb, z).start())
 
     def small3():
@@ -1441,31 +1637,65 @@
         lines(lambda zb: zexp(zb, zb).wait_send())
         lines(lambda zb: zsum(zb, zb).wait_send())
 
-    steps = [small0, small1, small2, small3, small4, small5]
-    for t in range(Reduce.STAGES):
-        steps[t]()
-        for plan in plans:
-            plan.stage(t)
-    swap_in().wait_recv()
-    swap().wait_send()
-    swap_keep.wait()
-
-
-def device_sums(grads, mine_out, vecs, qvec, drouter, ebias, mgt, condt, ada):
+    def run(pieces, s):
+        for piece in pieces:
+            piece.stage(s)
+
+    run(early[:2], 1)
+    run(late, 0)
+    for p in every:
+        tall.final(p, False)
+    run(early[2:], 1)
+    for p in every[:3]:
+        wide.give(p)
+    run(early, 2)
+    small1()
+    for p in every[3:]:
+        wide.give(p)
+    run(late, 1)
+    small2()
+    for p in every[:3]:
+        wide.final(p)
+    run(early, 3)
+    small3()
+    run(late, 2)
+    for p in every[3:]:
+        wide.final(p)
+    run(early, 4)
+    small4()
+    run(late, 3)
+    run(early, 5)
+    small5()
+    run(late, 4)
+    run(late, 5)
+    tall.close(False)
+    wide.close()
+
+
+def tail_part(sin_half, sout_half, dout, dwin, dwout, dwout_came, *others):
     n = NZ * NX
     dma = pltpu.SemaphoreType.DMA
-    split = [g.reshape(NZ, NX, 2, g.shape[0] // (4 * NZ), g.shape[1]) for g in grads]
-    outs = [sds((2, g.shape[3], g.shape[4]), B16) for g in split]
-    rows = vecs.shape[0] + 16 + 8 * (drouter.shape[1] // 128)
-    scratch = []
-    for matrix, _, share, _ in PIECES:
-        g = split[matrix]
-        scratch += Reduce.scratch(g.shape[3], g.shape[4] // 2 // share)
     vm = pltpu.VMEM
+    tok, qkv, vecs = others[0], others[7], others[9]
+    width, hidden = qkv.shape[0], 2 * sin_half.shape[1]
+    split = lambda g: g.reshape(NZ, NX, 2, g.shape[0] // (4 * NZ), g.shape[1])
+    rows, tall = width // NZ // 4, hidden // NZ // 4
+    outs = [
+        sds((2, rows, 3 * width), B16),
+        sds((2, rows, width), B16),
+        sds((2, rows, hidden), B16),
+        sds((2, tall, width), B16),
+    ]
+    short = vecs.shape[0] + 16 + 8 * (width // 128)
+    scratch = [vm((NZ, NX, 2, rows, 3 * width), B16), vm((tok.shape[0], 3 * width), B16)]
+    for specs in piece_specs(width, hidden):
+        for _, spec in specs:
+            scratch += Piece.scratch(spec)
+    scratch += [vm((2,) + dwin.shape[1:], B16)] + MidSum.scratch(dwin.shape) + MidSum.scratch(dwout.shape)
     scratch += [
-        vm((rows, 128), F32),
-        vm((3, rows, 128), F32),
-        vm((NZ + 3, rows, 128), F32),
+        vm((short, 128), F32),
+        vm((3, short, 128), F32),
+        vm((NZ + 3, short, 128), F32),
         vm((2, 32, 128), F32),
         vm((NZ, 2, 32, 128), F32),
         vm((48, 128), F32),
@@ -1474,25 +1704,26 @@
         dma((4, n)),
         dma((4, NZ)),
         dma((2, 3)),
-        dma((3,)),
     ]
     out = pl.pallas_call(
-        sums_kernel,
+        tail_kernel,
         out_shape=outs
         + [
-            sds(mine_out.shape, B16),
-            sds((rows, 128), F32),
+            sds((NX, dwin.shape[1] // NX, dwin.shape[2]), B16),
+            sds((NX, dwout.shape[1] // NX, dwout.shape[2]), B16),
+            sds(tok.shape, F32),
+            sds((short, 128), F32),
             sds((2, 32, 128), F32),
             sds((4, n, 48, 128), F32),
             sds((n, 8, 128), F32),
         ],
-        in_specs=[HB] * 5 + [VM] * 7,
-        out_specs=[HB] * 5 + [VM] * 4,
+        in_specs=[VM] * 20,
+        out_specs=[HB] * 6 + [VM] * 5,
         scratch_shapes=scratch,
         compiler_params=params(4),
-        name="device_sums",
-    )(*split, mine_out, vecs, qvec, drouter, ebias, mgt, condt, ada)
-    return [o.reshape(-1, o.shape[2]).astype(F32) for o in out[:4]], out[4], out[5:]
+        name="attention_back_sums",
+    )(split(sin_half), split(sout_half), split(dout), dwin, dwout, dwout_came, *others)
+    return [o.reshape(-1, o.shape[2]).astype(F32) for o in out[:4]], out[4], out[5], out[6], out[7:]
 
 
 def on_block(
@@ -1502,7 +1733,6 @@
 ):
     n = NZ * NX
     dp = lax.axis_index("dp")
-    x = lax.rem(dp, NX)
     width = tokens.shape[2]
     hidden = shared_in.shape[1]
     part = width // n
@@ -1510,44 +1740,23 @@
     _, silu_back = jax.vjp(jax.nn.silu, conditioning.astype(F32))
     (
         normed, proj, lsum, mixed, att, resid, second, gates, place, mod, bias, sinb, router_t,
-        condt, rows, grads, res, qkv_full, out_full, sin_full, sout_full, slopes, dwout,
+        condt, res, bgr, ebias, qkv_full, out_full, sin_c, sout_c, sin_x, sout_x, dwin, dwout,
     ) = lead_part(
         tok, cot, route.T, conditioning, ada_weight, ada_bias[None], qv_bias, out_bias[None], shared_out_bias[None],
         shared_in_bias[None], router.T, expert_in_bias, expert_out_bias,
         (qkv_weight, out_weight, shared_in, shared_out), expert_in, expert_out,
     )
-    line = [[NX * z + xx for z in range(NZ)] for xx in range(NX)]
-    turn = [(i, i // NX * NX + 1 - i % NX) for i in range(n)]
-
-    first = x == 0
-
-    def over_z(grad):
-        return lax.psum_scatter(grad, "dp", scatter_dimension=0, axis_index_groups=line, tiled=True)
-
-    def swap(pair, axis):
-        keep = lax.dynamic_index_in_dim(pair, x, axis, keepdims=False)
-        give = lax.dynamic_index_in_dim(pair, 1 - x, axis, keepdims=False)
-        came = lax.ppermute(give, "dp", turn)
-        return jnp.stack(
-            [jnp.where(first, keep, came), jnp.where(first, came, keep)], axis=axis
-        )
-
-    dwout_mine = over_z(dwout)
-    dwin, bgr, ebias = expert_back(
-        jnp.reshape(x, (1,)), rows, grads, slopes, expert_in, expert_out
-    )
-    dwin_mine = over_z(dwin)
-    (output, rgrad, mgrad, dsin, dsout, dout, drouter, vecs, mg2) = middle(
-        res, bgr, second, resid, att, cot, mod, sin_full, sout_full, sinb, bias, router_t, gates, place,
+    dwout = dwout.reshape(NZ, hidden // NZ, width)
+    (dwout_came, output, rgrad, mgrad, sin_half, sout_half, dout, drouter, vecs, mg2) = middle(
+        res, bgr, dwout, second, resid, att, cot, mod, sin_c, sout_c, sin_x, sout_x, sinb, bias, router_t, gates, place,
         mixed, out_full,
     )
-    tgrad, dqkv, qvec, mgt = back(tok, mod, normed, proj, lsum, mgrad, rgrad, qkv_full, mg2)
-    dense, dwout_pair, (small, esum, tiles, cgot) = device_sums(
-        (dqkv, dout, dsin, dsout), dwout_mine.reshape(NX, hidden // n, width), vecs, qvec, drouter, ebias, mgt, condt, ada_weight
-    )
-
+    dense, dwin_pair, dwout_pair, tgrad, (small, esum, tiles, cgot) = tail_part(
+        sin_half, sout_half, dout, dwin.reshape(NZ, NX * part, hidden),
+        dwout, dwout_came, tok, mod, normed, proj, lsum, mgrad, rgrad, qkv_full, mg2, vecs, drouter, ebias, condt, ada_weight,
+    )
     dwout_sum = dwout_pair.astype(F32)
-    dwin_sum = swap(dwin_mine.reshape(NX, part, hidden), 0).astype(F32)
+    dwin_sum = dwin_pair.astype(F32)
 
     def share(v, size):
         return lax.dynamic_slice_in_dim(v.reshape(-1), dp * size, size, 0)

time: 360 us -> 336 us (0.933)
  between operations: 14.2 us -> 0.74 us
  local copies, waits for them, and re-layouts: 16.6 us -> 12.4 us
    pallas_call x4 -> x2, Pallas kernels: 225 us -> 207 us  [the longest x1 144 us: tail_part(): pl.pallas_call(tail_kernel, out_shape=outs + [sds((NX, dwin.shape[1] // N...]
    pallas_call x1, Pallas kernels: 90.1 us -> 106 us  [lead_part(): pl.pallas_call(lead_kernel, out_shape=outs + far, in_specs=[VM] * 13 + [H...]
  transfers between devices with their start and end apart: 3 -> 0, of which waited for: 0 -> 0; matrix products, arithmetic and copies ran while one was open for 6% -> 0% of each run, Pallas kernels for 63% -> 0%
where the time goes in v3:
time: 336 us
  Pallas kernels  313 us (93%)
  local copies, waits for them, and re-layouts  12.4 us (4%)
  other arithmetic  8.49 us (3%)
    pallas_call x1, Pallas kernels, tail_part(): pl.pallas_call(tail_kernel, out_shape=outs + [sds((NX, dwin.shape[1] // N...  144 us
    pallas_call x1, Pallas kernels, lead_part(): pl.pallas_call(lead_kernel, out_shape=outs + far, in_specs=[VM] * 13 + [H...  106 us
    pallas_call x1, Pallas kernels, middle(): pl.pallas_call(middle_kernel, out_shape=[sds((2,) + dwout.shape[1:], B16)...  63.3 us

profile of v3, /device:TPU:0, one launch (start us, length us, event | category | flops | bytes accessed | tf_op | source)
XLA Modules:
  0.0 336.1 jit_solution(6212168465395526035)
XLA Ops:
  0.7 1.3 broadcast_in_dim.18.adab
  1.9 1.2 broadcast_in_dim.21.sinb_s
  3.2 105.6 %front_and_expert.1 = (bf16[256,768]{1,0:T(8,128)(2,1)}, bf16[256,2304]{1,0:T(8,128)(2,1)}, f32[256,128]{1,0:T(8,128)}, bf16[256,768]{1,0:T(8,128)(2,1)}, f32[25...) custom-call(bf16[256,768]{1,0:T(8,128)(2,1)} %bitcast.77, ...), custom_call_target="tpu_custom_call" | custom-call | tf_op jit(solution)/shard_map/front_and_expert/pallas_call | solution.py:886
  108.8 63.3 %shared_expert_combine.1 = (bf16[2,768,768]{2,1,0:T(8,128)(2,1)}, bf16[256,768]{1,0:T(8,128)(2,1)}, f32[256,768]{1,0:T(8,128)}, bf16[256,768]{1,0:T(8,128)(2,1)}...) custom-call(bf16[640,768]{1,0:T(8,128)(2,1)} %get-tuple-element.64.r, ...), custom_call_target="tpu_custom_call" | custom-call | tf_op jit(solution)/shard_map/shared_expert_combine/pallas_call | solution.py:1097
  172.1 143.9 %attention_back_sums.1 = (bf16[2,48,2304]{2,1,0:T(8,128)(2,1)}, bf16[2,48,768]{2,1,0:T(8,128)(2,1)}, bf16[2,48,3072]{2,1,0:T(8,128)(2,1)}, bf16[2,192,768]{2,1,0...) custom-call(bf16[4,2,2,48,1536]{4,3,2,1,0:T(8,128)(2,1)} %bitcast.73, ...), custom_call_target="tpu_custom_call" | custom-call | tf_op jit(solution)/shard_map/attention_back_sums/pallas_call | solution.py:1708
  316.0 0.0 copy-start.2
  316.0 0.8 slice_bitcast_fusion.5
  316.8 0.1 dynamic-slice_bitcast_fusion
  316.9 0.6 pad_maximum_fusion
  317.4 1.1 fusion
  318.6 0.9 slice_bitcast_fusion
  319.5 1.7 fusion.1
  321.2 0.0 copy-done.2
  321.2 0.0 copy-start.1
  321.2 1.7 convert_element_type.54
  322.9 0.0 copy-done.1
  322.9 0.0 copy-start.5
  322.9 1.6 convert_element_type.55
  324.5 0.0 copy-start.4
  324.5 0.0 copy-done.5
  324.5 0.0 copy-start.6
  324.5 1.1 bitcast_convert_fusion
  325.6 0.0 copy-start.8
  325.6 0.0 copy-done.4
  325.6 1.2 bitcast_convert_fusion.1
  326.8 0.0 copy-done.6
  326.8 1.0 bitcast_convert_fusion.2
  327.8 0.0 copy-done.8
  327.8 0.7 bitcast_convert_fusion.3
  328.6 0.0 copy-done.10
  328.6 0.6 constant_dynamic-slice_fusion.1
  329.2 0.0 copy-done.9
  329.2 0.7 constant_dynamic-slice_fusion.2
  329.8 0.0 copy-done
  329.8 0.1 slice_reduce_fusion
  329.9 0.7 dynamic_slice.31
  330.6 0.6 dynamic_slice.34
  331.2 0.6 dynamic_slice.36
  331.7 0.6 constant_dynamic-slice_fusion
  332.4 0.7 dynamic_slice.35
  333.0 0.8 slice_reduce_fusion.1
  333.8 0.1 reshape_squeeze.3
  333.9 0.0 copy-done.11
  333.9 0.6 fusion.5
  334.5 0.0 copy-done.7
  334.5 0.7 copy.53
  335.2 0.0 copy-done.3
  335.2 0.9 copy.54
  (13 shorter events, 0.1 us)
Async XLA Ops:
  316.0 5.3 %copy-start.2 = (bf16[2,96,3072]{2,1,0:T(8,128)(2,1)S(1)}, bf16[2,96,3072]{2,1,0:T(8,128)(2,1)}, u32[]{:S(2)}) copy-start(bf16[2,96,3072]{2,1,0:T(8,128)(2,1)} %get-tuple-element.107) | copy-start | bytes 3538948
  321.2 1.7 copy-start.1
  322.9 1.6 copy-start.5
  324.5 1.2 copy-start.4
  324.5 2.3 copy-start.6
  325.6 2.2 copy-start.8
  325.6 2.9 copy-start.10
  325.6 3.5 %copy-start.9 = (f32[104,128]{1,0:T(8,128)S(1)}, f32[104,128]{1,0:T(8,128)}, u32[]{:S(2)}) copy-start(f32[104,128]{1,0:T(8,128)} %get-tuple-element.103) | copy-start | bytes 159748
  325.6 4.2 %copy-start = (f32[4,8,48,128]{3,2,1,0:T(8,128)S(1)}, f32[4,8,48,128]{3,2,1,0:T(8,128)}, u32[]{:S(2)}) copy-start(f32[4,8,48,128]{3,2,1,0:T(8,128)} %get-tuple-element.101) | copy-start | bytes 2359300
  326.8 7.1 %copy-start.11 = (bf16[1,768]{1,0:T(2,128)(2,1)S(1)}, bf16[1,768]{1,0:T(2,128)(2,1)}, u32[]{:S(2)}) copy-start(bf16[1,768]{1,0:T(2,128)(2,1)} %cond.1) | copy-start | bytes 4612
  326.8 7.7 %copy-start.7 = (bf16[256,768]{1,0:T(8,128)(2,1)S(1)}, bf16[256,768]{1,0:T(8,128)(2,1)}, u32[]{:S(2)}) copy-start(bf16[256,768]{1,0:T(8,128)(2,1)} %get-tuple-element.82) | copy-start | bytes 1179652
  326.8 8.4 %copy-start.3 = (f32[256,768]{1,0:T(8,128)S(1)}, f32[256,768]{1,0:T(8,128)}, u32[]{:S(2)}) copy-start(f32[256,768]{1,0:T(8,128)} %get-tuple-element.99) | copy-start | bytes 2359300
